TPU v7x, 32 devices: a whole 2x2x4 slice. The times are simulated.
32 devices in a mesh: dp: 8 (over z, x), seq: 4 (over y, core).
Axes of the slice: x: 2, y: 2, z: 4, core: 2. Of those that a mesh axis runs over, the one named last changes fastest.
Arguments:
- tokens: bfloat16 [16, 2048, 1088], P('dp', 'seq'), may hold values from -6 to 6
- qkv_weight: bfloat16 [1088, 3264], P('dp'), may hold values from -0.1875 to 0.1875
- out_weight: bfloat16 [1088, 1088], P('dp'), may hold values from -0.75 to 0.75
- up_weight: bfloat16 [1088, 4352], P('dp'), may hold values from -0.1875 to 0.1875
- down_weight: bfloat16 [4352, 1088], P('dp'), may hold values from -0.09375 to 0.09375
- norm_gain: bfloat16 [2, 1088], P(None, 'dp'), may hold values from 0.5 to 1.5
- norm_shift: bfloat16 [2, 1088], P(None, 'dp'), may hold values from -4 to 4
- bias_rows: bfloat16 [4, 1088], P(None, 'dp'), may hold values from -6 to 6
- bias_hidden: bfloat16 [4352], P('dp'), may hold values from -6 to 6
- doc_lengths: int32 [16, 6], P('dp'), may hold values from 32 to 1888, as said below
- cotangent: bfloat16 [16, 2048, 1088], P('dp', 'seq'), may hold values from -6 to 6
Outputs:
- layer_out: bfloat16 [16, 2048, 1088], P('dp', 'seq')
- grad_tokens: float32 [16, 2048, 1088], P('dp', 'seq')
- grad_qkv: float32 [1088, 3264], P('dp')
- grad_out_weight: float32 [1088, 1088], P('dp')
- grad_up: float32 [1088, 4352], P('dp')
- grad_down: float32 [4352, 1088], P('dp')
- grad_gain: float32 [2, 1088], P(None, 'dp')
- grad_shift: float32 [2, 1088], P(None, 'dp')
- grad_bias_rows: float32 [4, 1088], P(None, 'dp')
- grad_bias_hidden: float32 [4352], P('dp')
Inputs may be any that keep to these rules, and one draw needn't show every extreme that they name: `doc_lengths`: each row lists the lengths of the 6 documents packed into one sequence, in order; they sum to 2048.
All inputs are finite; a program needn't handle non-finite values.
Results may differ from a plain program's by a relative error of at most 0.015.
Values may be sent and summed in bfloat16 or wider, within the bound.
No kernel may reach another device: no remote copies, remote signals or barrier semaphores. Data moves between devices by JAX's collectives and lax.ppermute only.
A program may use at most 384 MiB of HBM per device.

v0:
```python
import jax
import jax.numpy as jnp
from jax import lax
from jax.sharding import PartitionSpec as P

D = 1088
H = 17
HD = 64
FF = 4352


norm_eps = 1e-05
masked_score = -1e30


def layer_norm(values_in, gain_row, shift_row):
    centre = values_in - jnp.mean(values_in, axis=-1, keepdims=True)
    spread = jnp.mean(centre * centre, axis=-1, keepdims=True)
    return centre * lax.rsqrt(spread + norm_eps) * gain_row + shift_row


def segment_ids(doc_lengths, positions):
    bounds = jnp.cumsum(doc_lengths)[:-1]
    return jnp.sum((positions[:, None] >= bounds[None, :]).astype(jnp.int32), axis=1)


def attention_set(qkv_weight, out_weight, norm_gain, norm_shift, bias_rows):
    return (
        lax.all_gather(qkv_weight, "dp", axis=0, tiled=True),
        lax.all_gather(out_weight, "dp", axis=0, tiled=True),
        lax.all_gather(norm_gain, "dp", axis=1, tiled=True),
        lax.all_gather(norm_shift, "dp", axis=1, tiled=True),
        lax.all_gather(bias_rows, "dp", axis=1, tiled=True),
    )


def hidden_set(up_weight, down_weight, bias_hidden):
    return (
        lax.all_gather(up_weight, "dp", axis=0, tiled=True),
        lax.all_gather(down_weight, "dp", axis=0, tiled=True),
        lax.all_gather(bias_hidden, "dp", axis=0, tiled=True),
    )


def key_loop(step_fn, state_init, block_count):
    return lax.fori_loop(0, block_count, step_fn, state_init)


def block_scores(query_heads, key_all, block_idx, query_pos, query_seg, seg_all):
    rows_blk = query_heads.shape[0]
    key_blk = lax.dynamic_slice_in_dim(key_all, block_idx * rows_blk, rows_blk, 0)
    scores = jnp.einsum(
        "qhd,khd->hqk", query_heads, key_blk, preferred_element_type=jnp.float32
    ) * HD ** (-0.5)
    key_pos = block_idx * rows_blk + jnp.arange(rows_blk, dtype=jnp.int32)
    key_seg = lax.dynamic_slice_in_dim(seg_all, block_idx * rows_blk, rows_blk, 0)
    allowed = (query_pos[:, None] >= key_pos[None, :]) & (query_seg[:, None] == key_seg[None, :])
    return (scores, allowed[None])


def attend(query_heads, key_all, value_all, query_pos, query_seg, seg_all, block_count):
    rows_blk, head_count, head_size = query_heads.shape

    def peak_pass(block_idx, state_in):
        run_peak, run_sum = state_in
        scores, allowed = block_scores(
            query_heads, key_all, block_idx, query_pos, query_seg, seg_all
        )
        masked = jnp.where(allowed, scores, masked_score)
        new_peak = jnp.maximum(run_peak, jnp.max(masked, axis=-1))
        shifted = jnp.where(allowed, jnp.exp(masked - new_peak[..., None]), 0.0)
        return (new_peak, run_sum * jnp.exp(run_peak - new_peak) + jnp.sum(shifted, axis=-1))

    start_state = (
        jnp.full((head_count, rows_blk), masked_score, jnp.float32),
        jnp.zeros((head_count, rows_blk), jnp.float32),
    )
    run_peak, run_sum = key_loop(peak_pass, start_state, block_count)
    log_total = run_peak + jnp.log(run_sum)

    def value_pass(block_idx, mixed_acc):
        scores, allowed = block_scores(
            query_heads, key_all, block_idx, query_pos, query_seg, seg_all
        )
        prob_rows = jnp.where(allowed, jnp.exp(scores - log_total[..., None]), 0.0).astype(
            jnp.bfloat16
        )
        value_blk = lax.dynamic_slice_in_dim(value_all, block_idx * rows_blk, rows_blk, 0)
        return mixed_acc + jnp.einsum(
            "hqk,khd->qhd", prob_rows, value_blk, preferred_element_type=jnp.float32
        )

    mixed_heads = key_loop(
        value_pass, jnp.zeros((rows_blk, head_count, head_size), jnp.float32), block_count
    )
    return (mixed_heads, log_total)


def attend_back(
    query_heads,
    key_all,
    value_all,
    grad_mixed,
    mixed_heads,
    log_total,
    query_pos,
    query_seg,
    seg_all,
    block_count,
):
    rows_blk, head_count, head_size = query_heads.shape
    length_all = key_all.shape[0]
    row_delta = jnp.sum(grad_mixed.astype(jnp.float32) * mixed_heads, axis=-1).T

    def grad_pass(block_idx, state_in):
        grad_query, grad_keys, grad_values = state_in
        scores, allowed = block_scores(
            query_heads, key_all, block_idx, query_pos, query_seg, seg_all
        )
        prob_rows = jnp.where(allowed, jnp.exp(scores - log_total[..., None]), 0.0)
        key_blk = lax.dynamic_slice_in_dim(key_all, block_idx * rows_blk, rows_blk, 0)
        value_blk = lax.dynamic_slice_in_dim(value_all, block_idx * rows_blk, rows_blk, 0)
        grad_prob = jnp.einsum(
            "qhd,khd->hqk", grad_mixed, value_blk, preferred_element_type=jnp.float32
        )
        grad_score = (prob_rows * (grad_prob - row_delta[..., None])).astype(jnp.bfloat16)
        grad_query = grad_query + jnp.einsum(
            "hqk,khd->qhd", grad_score, key_blk, preferred_element_type=jnp.float32
        )
        key_part = jnp.einsum(
            "hqk,qhd->khd", grad_score, query_heads, preferred_element_type=jnp.float32
        )
        value_part = jnp.einsum(
            "hqk,qhd->khd",
            prob_rows.astype(jnp.bfloat16),
            grad_mixed,
            preferred_element_type=jnp.float32,
        )
        grad_keys = lax.dynamic_update_slice_in_dim(grad_keys, key_part, block_idx * rows_blk, 0)
        grad_values = lax.dynamic_update_slice_in_dim(
            grad_values, value_part, block_idx * rows_blk, 0
        )
        return (grad_query, grad_keys, grad_values)

    start_state = (
        jnp.zeros((rows_blk, head_count, head_size), jnp.float32),
        jnp.zeros((length_all, head_count, head_size), jnp.float32),
        jnp.zeros((length_all, head_count, head_size), jnp.float32),
    )
    grad_query, grad_keys, grad_values = key_loop(grad_pass, start_state, block_count)
    score_scale = HD ** (-0.5)
    return (grad_query * score_scale, grad_keys * score_scale, grad_values)


def body(
    tokens,
    qkv_weight,
    out_weight,
    up_weight,
    down_weight,
    norm_gain,
    norm_shift,
    bias_rows,
    bias_hidden,
    doc_lengths,
    cotangent,
):
    rows_blk = tokens.shape[1]
    block_count = lax.axis_size("seq")
    own_index = lax.axis_index("seq")
    length_all = rows_blk * block_count
    all_pos = jnp.arange(length_all, dtype=jnp.int32)
    query_pos = own_index * rows_blk + jnp.arange(rows_blk, dtype=jnp.int32)

    def fetch_sets():
        return (
            attention_set(qkv_weight, out_weight, norm_gain, norm_shift, bias_rows),
            hidden_set(up_weight, down_weight, bias_hidden),
        )

    def micro_step(grad_acc, micro_in):
        seq_tokens, seq_cot, seq_lengths = micro_in
        (qkv_full, out_full, gain_full, shift_full, bias_full), (
            up_full,
            down_full,
            hidden_bias_full,
        ) = fetch_sets()
        gains = gain_full.astype(jnp.float32)
        shifts = shift_full.astype(jnp.float32)
        biases = bias_full.astype(jnp.float32)
        hidden_bias = hidden_bias_full.astype(jnp.float32)
        seg_all = segment_ids(seq_lengths, all_pos)
        query_seg = lax.dynamic_slice_in_dim(seg_all, own_index * rows_blk, rows_blk, 0)
        x_float = seq_tokens.astype(jnp.float32)
        normed = layer_norm(x_float, gains[0], shifts[0]).astype(jnp.bfloat16)
        joined = jnp.dot(normed, qkv_full, preferred_element_type=jnp.float32)
        query_rows = (joined[:, :D] + biases[0]).astype(jnp.bfloat16)
        key_rows = joined[:, D : 2 * D].astype(jnp.bfloat16)
        value_rows = (joined[:, 2 * D :] + biases[1]).astype(jnp.bfloat16)
        key_all, value_all = (
            lax.all_gather(key_rows, "seq", axis=0, tiled=True),
            lax.all_gather(value_rows, "seq", axis=0, tiled=True),
        )
        query_heads = query_rows.reshape(rows_blk, H, HD)
        key_heads = key_all.reshape(length_all, H, HD)
        value_heads = value_all.reshape(length_all, H, HD)
        mixed_heads, log_total = attend(
            query_heads, key_heads, value_heads, query_pos, query_seg, seg_all, block_count
        )
        mixed_low = mixed_heads.reshape(rows_blk, D).astype(jnp.bfloat16)
        residual = (
            x_float + jnp.dot(mixed_low, out_full, preferred_element_type=jnp.float32) + biases[2]
        )
        normed_two = layer_norm(residual, gains[1], shifts[1]).astype(jnp.bfloat16)
        up_proj = jnp.dot(normed_two, up_full, preferred_element_type=jnp.float32) + hidden_bias
        active_low = jax.nn.gelu(up_proj, approximate=True).astype(jnp.bfloat16)
        branch = jnp.dot(active_low, down_full, preferred_element_type=jnp.float32) + biases[3]
        layer_rows = (residual + branch).astype(jnp.bfloat16)
        (qkv_back, out_back, gain_back, shift_back, bias_back), (
            up_back,
            down_back,
            hidden_back,
        ) = fetch_sets()
        cot_float = seq_cot.astype(jnp.float32)
        grad_down = jnp.dot(active_low.T, seq_cot, preferred_element_type=jnp.float32)
        grad_active = jnp.dot(seq_cot, down_back.T, preferred_element_type=jnp.float32)
        unused_gelu, gelu_back = jax.vjp(
            lambda pre_act: jax.nn.gelu(pre_act, approximate=True), up_proj
        )
        grad_up_proj = gelu_back(grad_active)[0].astype(jnp.bfloat16)
        grad_up = jnp.dot(normed_two.T, grad_up_proj, preferred_element_type=jnp.float32)
        grad_hidden_bias = jnp.sum(grad_up_proj.astype(jnp.float32), axis=0)
        grad_a2 = jnp.dot(grad_up_proj, up_back.T, preferred_element_type=jnp.float32)
        unused_norm, norm_back_two = jax.vjp(layer_norm, residual, gains[1], shifts[1])
        grad_resid_part, grad_gain_two, grad_shift_two = norm_back_two(grad_a2)
        grad_residual = cot_float + grad_resid_part
        grad_branch = grad_residual.astype(jnp.bfloat16)
        grad_out_weight = jnp.dot(mixed_low.T, grad_branch, preferred_element_type=jnp.float32)
        grad_mixed = jnp.dot(grad_branch, out_back.T, preferred_element_type=jnp.float32).astype(
            jnp.bfloat16
        )
        grad_query, grad_keys, grad_values = attend_back(
            query_heads,
            key_heads,
            value_heads,
            grad_mixed.reshape(rows_blk, H, HD),
            mixed_heads,
            log_total,
            query_pos,
            query_seg,
            seg_all,
            block_count,
        )
        own_keys, own_values = (
            lax.psum_scatter(
                grad_keys.reshape(length_all, D).astype(jnp.bfloat16),
                "seq",
                scatter_dimension=0,
                tiled=True,
            ).astype(jnp.float32),
            lax.psum_scatter(
                grad_values.reshape(length_all, D).astype(jnp.bfloat16),
                "seq",
                scatter_dimension=0,
                tiled=True,
            ).astype(jnp.float32),
        )
        grad_joined = jnp.concatenate(
            [grad_query.reshape(rows_blk, D), own_keys, own_values], axis=1
        ).astype(jnp.bfloat16)
        grad_qkv = jnp.dot(normed.T, grad_joined, preferred_element_type=jnp.float32)
        joined_float = grad_joined.astype(jnp.float32)
        grad_bias_rows = jnp.stack(
            [
                jnp.sum(joined_float[:, :D], axis=0),
                jnp.sum(joined_float[:, 2 * D :], axis=0),
                jnp.sum(grad_branch.astype(jnp.float32), axis=0),
                jnp.sum(cot_float, axis=0),
            ]
        )
        grad_a1 = jnp.dot(grad_joined, qkv_back.T, preferred_element_type=jnp.float32)
        unused_first, norm_back_one = jax.vjp(layer_norm, x_float, gains[0], shifts[0])
        grad_x_part, grad_gain_one, grad_shift_one = norm_back_one(grad_a1)
        grad_rows = grad_residual + grad_x_part
        grad_gain = jnp.stack([grad_gain_one, grad_gain_two])
        grad_shift = jnp.stack([grad_shift_one, grad_shift_two])
        new_acc = (
            grad_acc[0] + grad_qkv,
            grad_acc[1] + grad_out_weight,
            grad_acc[2] + grad_up,
            grad_acc[3] + grad_down,
            grad_acc[4] + grad_gain,
            grad_acc[5] + grad_shift,
            grad_acc[6] + grad_bias_rows,
            grad_acc[7] + grad_hidden_bias,
        )
        return (new_acc, (layer_rows, grad_rows))

    start_acc = (
        jnp.zeros((D, 3 * D), jnp.float32),
        jnp.zeros((D, D), jnp.float32),
        jnp.zeros((D, FF), jnp.float32),
        jnp.zeros((FF, D), jnp.float32),
        jnp.zeros((2, D), jnp.float32),
        jnp.zeros((2, D), jnp.float32),
        jnp.zeros((4, D), jnp.float32),
        jnp.zeros((FF,), jnp.float32),
    )
    grad_acc, (layer_out, grad_tokens) = lax.scan(
        micro_step, start_acc, (tokens, cotangent, doc_lengths)
    )
    column_parts = (
        lax.psum_scatter(
            grad_acc[0].astype(jnp.bfloat16), "seq", scatter_dimension=1, tiled=True
        ).astype(jnp.float32),
        lax.psum_scatter(
            grad_acc[1].astype(jnp.bfloat16), "seq", scatter_dimension=1, tiled=True
        ).astype(jnp.float32),
        lax.psum_scatter(
            grad_acc[2].astype(jnp.bfloat16), "seq", scatter_dimension=1, tiled=True
        ).astype(jnp.float32),
        lax.psum_scatter(
            grad_acc[3].astype(jnp.bfloat16), "seq", scatter_dimension=1, tiled=True
        ).astype(jnp.float32),
    )
    grad_shards = (
        lax.psum_scatter(column_parts[0], "dp", scatter_dimension=0, tiled=True),
        lax.psum_scatter(column_parts[1], "dp", scatter_dimension=0, tiled=True),
        lax.psum_scatter(column_parts[2], "dp", scatter_dimension=0, tiled=True),
        lax.psum_scatter(column_parts[3], "dp", scatter_dimension=0, tiled=True),
        lax.psum_scatter(grad_acc[4], "dp", scatter_dimension=1, tiled=True),
        lax.psum_scatter(grad_acc[5], "dp", scatter_dimension=1, tiled=True),
        lax.psum_scatter(grad_acc[6], "dp", scatter_dimension=1, tiled=True),
        lax.psum_scatter(grad_acc[7], "dp", scatter_dimension=0, tiled=True),
    )
    grad_large = (
        lax.all_gather(grad_shards[0].astype(jnp.bfloat16), "seq", axis=1, tiled=True).astype(
            jnp.float32
        ),
        lax.all_gather(grad_shards[1].astype(jnp.bfloat16), "seq", axis=1, tiled=True).astype(
            jnp.float32
        ),
        lax.all_gather(grad_shards[2].astype(jnp.bfloat16), "seq", axis=1, tiled=True).astype(
            jnp.float32
        ),
        lax.all_gather(grad_shards[3].astype(jnp.bfloat16), "seq", axis=1, tiled=True).astype(
            jnp.float32
        ),
    )
    grad_small = lax.psum((grad_shards[4], grad_shards[5], grad_shards[6], grad_shards[7]), "seq")
    return (
        layer_out,
        grad_tokens,
        grad_large[0],
        grad_large[1],
        grad_large[2],
        grad_large[3],
        grad_small[0],
        grad_small[1],
        grad_small[2],
        grad_small[3],
    )


def solution(mesh):
    placed = (
        P("dp", "seq", None),
        P("dp", None),
        P("dp", None),
        P("dp", None),
        P("dp", None),
        P(None, "dp"),
        P(None, "dp"),
        P(None, "dp"),
        P("dp"),
        P("dp", None),
        P("dp", "seq", None),
    )
    return jax.shard_map(
        body,
        mesh=mesh,
        in_specs=placed,
        out_specs=(
            P("dp", "seq", None),
            P("dp", "seq", None),
            P("dp", None),
            P("dp", None),
            P("dp", None),
            P("dp", None),
            P(None, "dp"),
            P(None, "dp"),
            P(None, "dp"),
            P("dp"),
        ),
        check_vma=False,
    )
```

profile of v0, /device:TPU:0, one launch (start us, length us, event | category | flops | bytes accessed | tf_op | source)
XLA Modules:
  0.0 2451.8 jit_solution(9915789523374429286)
XLA Ops:
  8.1 1715.1 %while.115 = (s32[]{:T(128)}, f32[1088,3264]{1,0:T(8,128)}, f32[1088,1088]{1,0:T(8,128)}, f32[1088,4352]{1,0:T(8,128)}, f32[4352,1088]{0,1:T(8,128)}, /*index=5*...) while((s32[]{:T(128)}, f32[1088,3264]{1,0:T(8,128)}, ...), condition=%wide.region_31.32_spmd.clone, body=%wide.region_0.31_spmd.clone.sunk | while | flops 48521506816 | bytes 878560512 | solution.py:309
  52.4 72.8 %all-gather.28.cloned.1.call-done = bf16[1088,3264]{1,0:T(8,128)(2,1)} async-done(((bf16[136,3264]{1,0:T(8,128)(2,1)}), bf16[1088,3264]{1,0:T(8,128)(2,1)}) %all-gather.28.cloned.1.call-update) | async-done | bytes 7102480 | tf_op jit(solution)/shard_map/while/body/eval_jaxpr/all_gather | solution.py:29
  173.2 33.4 %all-reduce.12 = bf16[4352]{0:T(1024)(128)(2,1)S(1)} all-reduce(bf16[4352]{0:T(1024)(128)(2,1)S(1)} %dynamic-update-slice.3), channel_id=1, replica_groups=mesh['dp'=8,'seq'=4] {'dp'}, use_global_device_ids=true, to_apply=%add | all-reduce | flops 4352 | bytes 17408 | tf_op jit(solution)/shard_map/while
  206.7 80.0 %while.116 = (s32[]{:T(128)}, f32[17,512]{1,0:T(8,128)S(1)}, f32[17,512]{1,0:T(8,128)S(1)}, s32[512]{0:T(512)S(1)}, s32[512]{0:T(512)S(1)}, /*index=5*/s32[2048]...) while((s32[]{:T(128)}, f32[17,512]{1,0:T(8,128)S(1)}, ...), condition=%wide.region_8.8_spmd.clone, body=%wide.region_5.7_spmd.clone.sunk | while | flops 606907392 | bytes 39133376 | solution.py:46
  286.8 35.9 %while.117 = (s32[]{:T(128)}, f32[512,17,64]{0,2,1:T(8,128)}, bf16[2048,17,64]{0,2,1:T(8,128)(2,1)}, s32[512]{0:T(512)S(1)}, s32[512]{0:T(512)S(1)}, /*index=5*/...) while((s32[]{:T(128)}, f32[512,17,64]{0,2,1:T(8,128)}, ...), condition=%wide.region_10.10_spmd.clone, body=%wide.region_9.9_spmd.clone.sunk | while | flops 1160577536 | bytes 8373956 | solution.py:46
  330.1 73.5 %all-gather.36.cloned.1.call-done = bf16[1088,4352]{1,0:T(8,128)(2,1)} async-done(((bf16[136,4352]{1,0:T(8,128)(2,1)}), bf16[1088,4352]{1,0:T(8,128)(2,1)}) %all-gather.36.cloned.1.call-update) | async-done | bytes 9469968 | tf_op jit(solution)/shard_map/while/body/eval_jaxpr/all_gather | solution.py:39
  416.0 133.1 %all-gather.38.cloned.1.call-done = bf16[4352,1088]{1,0:T(8,128)(2,1)} async-done(((bf16[544,1088]{1,0:T(8,128)(2,1)}), bf16[4352,1088]{1,0:T(8,128)(2,1)}) %all-gather.38.cloned.1.call-update) | async-done | bytes 9469968 | tf_op jit(solution)/shard_map/while/body/eval_jaxpr/all_gather | solution.py:40
  584.9 156.0 %while.118 = (s32[]{:T(128)}, f32[512,17,64]{0,2,1:T(8,128)S(1)}, f32[2048,17,64]{0,2,1:T(8,128)}, bf16[2048,17,64]{0,2,1:T(8,128)(2,1)}, bf16[2048,17,64]{0,2,1...) while((s32[]{:T(128)}, f32[512,17,64]{0,2,1:T(8,128)S(1)}, ...), condition=%wide.region_17.17_spmd.clone, body=%wide.region_16.16_spmd.clone.sunk | while | flops 2898592256 | bytes 97833200 | solution.py:46
  795.2 39.1 %reduce-scatter.48.cloned.1.call-done = bf16[512,1088]{0,1:T(8,128)(2,1)} async-done(((bf16[2048,1088]{0,1:T(8,128)(2,1)}), bf16[512,1088]{0,1:T(8,128)(2,1)}) %reduce-scatter.48.cloned.1.call-update) | async-done | bytes 1114128 | tf_op jit(solution)/shard_map/while/body/eval_jaxpr/reduce_scatter | solution.py:255
  903.5 71.9 %all-gather.28.cloned.1.call-done = bf16[1088,3264]{1,0:T(8,128)(2,1)} async-done(((bf16[136,3264]{1,0:T(8,128)(2,1)}), bf16[1088,3264]{1,0:T(8,128)(2,1)}) %all-gather.28.cloned.1.call-update) | async-done | bytes 7102480 | tf_op jit(solution)/shard_map/while/body/eval_jaxpr/all_gather | solution.py:29
  1023.6 33.4 %all-reduce.12 = bf16[4352]{0:T(1024)(128)(2,1)S(1)} all-reduce(bf16[4352]{0:T(1024)(128)(2,1)S(1)} %dynamic-update-slice.3), channel_id=1, replica_groups=mesh['dp'=8,'seq'=4] {'dp'}, use_global_device_ids=true, to_apply=%add | all-reduce | flops 4352 | bytes 17408 | tf_op jit(solution)/shard_map/while
  1057.2 80.0 %while.116 = (s32[]{:T(128)}, f32[17,512]{1,0:T(8,128)S(1)}, f32[17,512]{1,0:T(8,128)S(1)}, s32[512]{0:T(512)S(1)}, s32[512]{0:T(512)S(1)}, /*index=5*/s32[2048]...) while((s32[]{:T(128)}, f32[17,512]{1,0:T(8,128)S(1)}, ...), condition=%wide.region_8.8_spmd.clone, body=%wide.region_5.7_spmd.clone.sunk | while | flops 606907392 | bytes 39133376 | solution.py:46
  1137.3 35.9 %while.117 = (s32[]{:T(128)}, f32[512,17,64]{0,2,1:T(8,128)}, bf16[2048,17,64]{0,2,1:T(8,128)(2,1)}, s32[512]{0:T(512)S(1)}, s32[512]{0:T(512)S(1)}, /*index=5*/...) while((s32[]{:T(128)}, f32[512,17,64]{0,2,1:T(8,128)}, ...), condition=%wide.region_10.10_spmd.clone, body=%wide.region_9.9_spmd.clone.sunk | while | flops 1160577536 | bytes 8373956 | solution.py:46
  1180.5 73.4 %all-gather.36.cloned.1.call-done = bf16[1088,4352]{1,0:T(8,128)(2,1)} async-done(((bf16[136,4352]{1,0:T(8,128)(2,1)}), bf16[1088,4352]{1,0:T(8,128)(2,1)}) %all-gather.36.cloned.1.call-update) | async-done | bytes 9469968 | tf_op jit(solution)/shard_map/while/body/eval_jaxpr/all_gather | solution.py:39
  1266.4 133.1 %all-gather.38.cloned.1.call-done = bf16[4352,1088]{1,0:T(8,128)(2,1)} async-done(((bf16[544,1088]{1,0:T(8,128)(2,1)}), bf16[4352,1088]{1,0:T(8,128)(2,1)}) %all-gather.38.cloned.1.call-update) | async-done | bytes 9469968 | tf_op jit(solution)/shard_map/while/body/eval_jaxpr/all_gather | solution.py:40
  1435.3 156.0 %while.118 = (s32[]{:T(128)}, f32[512,17,64]{0,2,1:T(8,128)S(1)}, f32[2048,17,64]{0,2,1:T(8,128)}, bf16[2048,17,64]{0,2,1:T(8,128)(2,1)}, bf16[2048,17,64]{0,2,1...) while((s32[]{:T(128)}, f32[512,17,64]{0,2,1:T(8,128)S(1)}, ...), condition=%wide.region_17.17_spmd.clone, body=%wide.region_16.16_spmd.clone.sunk | while | flops 2898592256 | bytes 97833200 | solution.py:46
  1788.5 42.2 %reduce-scatter.34.cloned.1.call-done = bf16[1088,1088]{1,0:T(8,128)(2,1)} async-done(((bf16[4352,1088]{1,0:T(8,128)(2,1)}), bf16[1088,1088]{1,0:T(8,128)(2,1)}) %reduce-scatter.34.cloned.1.call-update) | async-done | bytes 2367504
  1837.4 74.4 %reduce-scatter.36.cloned.1.call-done = bf16[272,4352]{1,0:T(8,128)(2,1)} async-done(((bf16[1088,4352]{1,0:T(8,128)(2,1)}), bf16[272,4352]{1,0:T(8,128)(2,1)}) %reduce-scatter.36.cloned.1.call-update) | async-done | bytes 2367504
  1919.2 29.5 %reduce-scatter.32.cloned.1.call-done = bf16[272,1088]{1,0:T(8,128)(2,1)} async-done(((bf16[1088,1088]{1,0:T(8,128)(2,1)}), bf16[272,1088]{1,0:T(8,128)(2,1)}) %reduce-scatter.32.cloned.1.call-update) | async-done | bytes 591888
  1951.5 66.5 %reduce-scatter.30.cloned.1.call-done = bf16[816,1088]{1,0:T(8,128)(2,1)} async-done(((bf16[3264,1088]{1,0:T(8,128)(2,1)}), bf16[816,1088]{1,0:T(8,128)(2,1)}) %reduce-scatter.30.cloned.1.call-update) | async-done | bytes 1775632
  2023.6 97.9 %reduce-scatter.44.cloned.1.call-done = f32[136,1088]{1,0:T(8,128)} async-done(((f32[1088,1088]{1,0:T(8,128)}), f32[136,1088]{1,0:T(8,128)}) %reduce-scatter.44.cloned.1.call-update) | async-done | bytes 591888
  2123.4 124.5 %reduce-scatter.38.cloned.1.call-done = f32[544,272]{1,0:T(8,128)} async-done(((f32[4352,272]{1,0:T(8,128)}), f32[544,272]{1,0:T(8,128)}) %reduce-scatter.38.cloned.1.call-update) | async-done | bytes 591888
  2251.9 36.4 %all-reduce.9 = (f32[2,1088]{1,0:T(2,128)S(1)}, f32[2,1088]{1,0:T(2,128)S(1)}, f32[4,1088]{1,0:T(4,128)S(1)}, f32[4352]{0:T(1024)S(1)}) all-reduce(f32[2,1088]{1,0:T(2,128)S(1)} %copy-done.53, f32[2,1088]{1,0:T(2,128)S(1)} %copy-done.50, f32[4,1088]{1,0:T(4,128)S(1)} %copy-done.42, ...), channel_id=12, replica_groups=mesh['dp'=8,'seq'=4] {'dp'}, use_global_device_ids=true, to_apply=%region_40.41.clone | all-reduce | flops 13056 | bytes 104448
  2325.5 76.0 %reduce-scatter.40.cloned.1.call-done = f32[136,816]{1,0:T(8,128)} async-done(((f32[1088,816]{1,0:T(8,128)}), f32[136,816]{1,0:T(8,128)}) %reduce-scatter.40.cloned.1.call-update) | async-done | bytes 443920
  (673 shorter events, 1209.6 us)
Async XLA Ops:
  8.6 116.6 %all-gather.28.cloned.1.call-start = ((), (), s32[]{:S(2)}) async-start(), calls=%async_computation.20 | async-start | bytes 8146944 | tf_op jit(solution)/shard_map/while/body/eval_jaxpr/all_gather | solution.py:29
  9.3 197.4 %all-gather.30.cloned.1.call-start = ((), (), s32[]{:S(2)}) async-start(), calls=%async_computation.21 | async-start | bytes 5570560 | tf_op jit(solution)/shard_map/while/body/eval_jaxpr/all_gather | solution.py:201
  136.4 150.4 %all-gather.32.cloned.1.call-start = ((), (), s32[]{:S(2)}) async-start(), calls=%async_computation.22 | async-start | bytes 5570560 | tf_op jit(solution)/shard_map/while/body/eval_jaxpr/all_gather | solution.py:202
  166.9 158.8 %all-gather.34.cloned.1.call-start = ((), (), s32[]{:S(2)}) async-start(), calls=%async_computation.23 | async-start | bytes 2820096 | tf_op jit(solution)/shard_map/while/body/eval_jaxpr/all_gather | solution.py:30
  167.5 236.1 %all-gather.36.cloned.1.call-start = ((), (), s32[]{:S(2)}) async-start(), calls=%async_computation.24 | async-start | bytes 10653696 | tf_op jit(solution)/shard_map/while/body/eval_jaxpr/all_gather | solution.py:39
  168.1 381.0 %all-gather.38.cloned.1.call-start = ((), (), s32[]{:S(2)}) async-start(), calls=%async_computation.25 | async-start | bytes 11280384 | tf_op jit(solution)/shard_map/while/body/eval_jaxpr/all_gather | solution.py:40
  168.7 626.5 %reduce-scatter.46.cloned.1.call-start = ((), (), s32[]{:S(2)}) async-start(), calls=%async_computation.26 | async-start | bytes 5570560 | tf_op jit(solution)/shard_map/while/body/eval_jaxpr/reduce_scatter | solution.py:261
  861.5 113.9 %all-gather.28.cloned.1.call-start = ((), (), s32[]{:S(2)}) async-start(), calls=%async_computation.20 | async-start | bytes 8146944 | tf_op jit(solution)/shard_map/while/body/eval_jaxpr/all_gather | solution.py:29
  862.3 194.9 %all-gather.30.cloned.1.call-start = ((), (), s32[]{:S(2)}) async-start(), calls=%async_computation.21 | async-start | bytes 5570560 | tf_op jit(solution)/shard_map/while/body/eval_jaxpr/all_gather | solution.py:201
  986.7 150.6 %all-gather.32.cloned.1.call-start = ((), (), s32[]{:S(2)}) async-start(), calls=%async_computation.22 | async-start | bytes 5570560 | tf_op jit(solution)/shard_map/while/body/eval_jaxpr/all_gather | solution.py:202
  1017.2 159.0 %all-gather.34.cloned.1.call-start = ((), (), s32[]{:S(2)}) async-start(), calls=%async_computation.23 | async-start | bytes 2820096 | tf_op jit(solution)/shard_map/while/body/eval_jaxpr/all_gather | solution.py:30
  1017.7 236.3 %all-gather.36.cloned.1.call-start = ((), (), s32[]{:S(2)}) async-start(), calls=%async_computation.24 | async-start | bytes 10653696 | tf_op jit(solution)/shard_map/while/body/eval_jaxpr/all_gather | solution.py:39
  1018.5 381.0 %all-gather.38.cloned.1.call-start = ((), (), s32[]{:S(2)}) async-start(), calls=%async_computation.25 | async-start | bytes 11280384 | tf_op jit(solution)/shard_map/while/body/eval_jaxpr/all_gather | solution.py:40
  1019.1 636.7 %reduce-scatter.46.cloned.1.call-start = ((), (), s32[]{:S(2)}) async-start(), calls=%async_computation.26 | async-start | bytes 5570560 | tf_op jit(solution)/shard_map/while/body/eval_jaxpr/reduce_scatter | solution.py:261
  1723.2 107.4 %reduce-scatter.34.cloned.1.call-start = ((), (), s32[]{:S(2)}) async-start(), calls=%async_computation.14 | async-start | bytes 12533760
  1748.5 163.2 %reduce-scatter.36.cloned.1.call-start = ((), (), s32[]{:S(2)}) async-start(), calls=%async_computation.15 | async-start | bytes 11837440
  1761.1 187.6 %reduce-scatter.32.cloned.1.call-start = ((), (), s32[]{:S(2)}) async-start(), calls=%async_computation.13 | async-start | bytes 3133440
  1768.3 249.8 %reduce-scatter.30.cloned.1.call-start = ((), (), s32[]{:S(2)}) async-start(), calls=%async_computation.12 | async-start | bytes 9400320
  1788.4 333.1 %reduce-scatter.44.cloned.1.call-start = ((), (), s32[]{:S(2)}) async-start(), calls=%async_computation.19 | async-start | bytes 5640192
  1837.3 410.6 %reduce-scatter.38.cloned.1.call-start = ((), (), s32[]{:S(2)}) async-start(), calls=%async_computation.16 | async-start | bytes 7520256
  1919.2 397.4 %reduce-scatter.42.cloned.1.call-start = ((), (), s32[]{:S(2)}) async-start(), calls=%async_computation.18 | async-start | bytes 1880064
  1951.5 450.0 %reduce-scatter.40.cloned.1.call-start = ((), (), s32[]{:S(2)}) async-start(), calls=%async_computation.17 | async-start | bytes 4386816
  2023.5 397.3 %all-gather.26.cloned.1.call-start = ((), (), s32[]{:S(2)}) async-start(), calls=%async_computation.11 | async-start | bytes 1566720 | tf_op jit(solution)/shard_map/all_gather | solution.py:343
  2123.3 318.2 %all-gather.24.cloned.1.call-start = ((), (), s32[]{:S(2)}) async-start(), calls=%async_computation.10 | async-start | bytes 1740800 | tf_op jit(solution)/shard_map/all_gather | solution.py:346
  (129 other events, 7097.7 us)
Sparse Core Ops, SparseCore 0:
  11.6 113.5 all-gather.27
  136.5 34.1 all-gather.29
  172.9 35.9 all-gather.31
  210.9 53.5 all-gather.33
  266.5 137.0 all-gather.35
  405.6 143.4 all-gather.37
  741.0 44.3 reduce-scatter.45
  788.0 46.1 reduce-scatter.47
  864.5 110.8 all-gather.27
  986.8 34.1 all-gather.29
  1023.1 35.9 all-gather.31
  1061.2 53.5 all-gather.33
  1116.9 137.0 all-gather.35
  1256.0 143.4 all-gather.37
  1591.4 44.3 reduce-scatter.45
  1638.3 46.2 reduce-scatter.47
Sparse Core Ops, SparseCore 1:
  1748.6 82.0 reduce-scatter.33
  1833.1 78.6 reduce-scatter.35
  1914.8 33.9 reduce-scatter.31
  1951.5 66.5 reduce-scatter.29
  2021.8 99.7 reduce-scatter.43
  2125.6 122.3 reduce-scatter.37
  2252.3 64.3 reduce-scatter.41
  2320.0 81.4 reduce-scatter.39
  2403.5 17.3 all-gather.25
  2423.0 18.5 all-gather.23
where the time goes:
time: 2460 us; the launch traced here: 2450 us
  waiting for transfers between devices  1180 us (48%)
  matrix products  684 us (28%)
  blocking collectives  260 us (11%)
  other arithmetic  201 us (8%)
  local copies, waits for them, and re-layouts  92.5 us (4%)
    unnamed x18, waiting for transfers between devices  528 us
    all_gather x2, waiting for transfers between devices, hidden_set(): lax.all_gather(down_weight, 'dp', axis=0, tiled=True)  266 us
    dot_general x16, matrix products, block_scores(): jnp.einsum('qhd,khd->hqk', query_heads, key_blk, preferred_element_type=j...  152 us
    all_gather x2, waiting for transfers between devices, hidden_set(): lax.all_gather(up_weight, 'dp', axis=0, tiled=True)  147 us
    all_gather x2, waiting for transfers between devices, attention_set(): lax.all_gather(qkv_weight, 'dp', axis=0, tiled=True)  145 us
    dot_general x8, matrix products, grad_pass(): jnp.einsum('hqk,qhd->khd', prob_rows.astype(jnp.bfloat16), grad_mixed, pr...  87.6 us
    reduce_sum x8, other arithmetic, peak_pass(): jnp.sum(shifted, axis=-1)  83.5 us
    dot_general x8, matrix products, grad_pass(): jnp.einsum('qhd,khd->hqk', grad_mixed, value_blk, preferred_element_type=...  79.6 us
  transfers between devices with their start and end apart: 26, of which 18 were waited for; matrix products, arithmetic and copies ran while one was open for 20% of the time, Pallas kernels for 0%

commit v1 on v0

v1 whole, which is shorter than its diff:
```python
import functools

import jax
import jax.numpy as jnp
from jax import lax
from jax.experimental import pallas as pl
from jax.experimental.pallas import tpu as pltpu
from jax.sharding import PartitionSpec as P

D = 1088
H = 17
HD = 64
FF = 4352

norm_eps = 1e-05
masked_score = -1e30
score_scale = HD ** (-0.5)

TQ = 512
TK = 512
VMEM_BYTES = 56 * 1024 * 1024

f32 = jnp.float32
bf16 = jnp.bfloat16


def dot_tn(left, right):
    return lax.dot_general(left, right, (((0,), (0,)), ((), ())), preferred_element_type=f32)


def dot_nn(left, right):
    return lax.dot_general(left, right, (((1,), (0,)), ((), ())), preferred_element_type=f32)


def dot_nt(left, right):
    return lax.dot_general(left, right, (((1,), (1,)), ((), ())), preferred_element_type=f32)


def norm_stats(rows):
    centre = rows - jnp.mean(rows, axis=0, keepdims=True)
    spread = jnp.mean(centre * centre, axis=0, keepdims=True)
    inverse = lax.rsqrt(spread + norm_eps)
    return centre * inverse, inverse


def norm_back(grad, unit, inverse, gain):
    scaled = grad * gain
    mean_one = jnp.mean(scaled, axis=0, keepdims=True)
    mean_two = jnp.mean(scaled * unit, axis=0, keepdims=True)
    return inverse * (scaled - mean_one - unit * mean_two)


def place_blocks(info_ref, store):
    for which in range(4):
        store(which // 2, which % 2, info_ref[which])


def allowed_mask(key_first, query_first, start_row):
    shape = (TK, TQ)
    key_pos = key_first + lax.broadcasted_iota(jnp.int32, shape, 0)
    query_pos = query_first + lax.broadcasted_iota(jnp.int32, shape, 1)
    return (key_pos <= query_pos) & (key_pos >= start_row)


def attend_kernel(
    info_ref, query_ref, key_ref, value_ref, key_sib_ref, value_sib_ref, start_ref,
    mixed_ref, log_ref, key_s, value_s,
):
    half = query_ref.shape[1] // 2
    ones_rows = jnp.ones((16, half), bf16)

    def store(sibling, part, block):
        key_from, value_from = (key_sib_ref, value_sib_ref) if sibling else (key_ref, value_ref)
        lanes = slice(part * half, (part + 1) * half)
        key_s[block] = key_from[:, lanes].astype(f32).T.astype(bf16)
        value_s[block] = jnp.concatenate([value_from[:, lanes], ones_rows], axis=0)

    place_blocks(info_ref, store)
    for part in range(2):
        lanes = slice(part * half, (part + 1) * half)
        query = query_ref[:, lanes] * jnp.asarray(score_scale, bf16)
        start_row = start_ref[:, lanes]
        own_block = info_ref[part]
        first = info_ref[4 + part]
        clear = info_ref[6 + part]

        def step(block, state, masked, query=query, start_row=start_row, own_block=own_block):
            peak, total = state
            scores = dot_nn(key_s[block], query)
            if masked:
                scores = jnp.where(
                    allowed_mask(block * TK, own_block * TQ, start_row), scores, masked_score
                )
            new_peak = jnp.maximum(peak, jnp.max(scores, axis=0, keepdims=True))
            weights = jnp.exp(scores - new_peak).astype(bf16)
            total = total * jnp.exp(peak - new_peak) + dot_nn(value_s[block], weights)
            return new_peak, total

        state = (
            jnp.full((1, half), masked_score, f32),
            jnp.zeros((HD + 16, half), f32),
        )
        state = lax.fori_loop(first, clear, functools.partial(step, masked=True), state)
        state = lax.fori_loop(clear, own_block, functools.partial(step, masked=False), state)
        peak, total = step(own_block, state, masked=True)
        row_sum = total[HD : HD + 1]
        mixed_ref[:, lanes] = (total[:HD] / row_sum).astype(bf16)
        log_ref[0, :, lanes] = peak + jnp.log(row_sum)


def split_three(row):
    high = row.astype(bf16)
    rest = row - high.astype(f32)
    mid = rest.astype(bf16)
    low = (rest - mid.astype(f32)).astype(bf16)
    return high, mid, low


def with_rows(rows, row):
    high, mid, low = (part.astype(f32) for part in split_three(row))
    index = lax.broadcasted_iota(jnp.int32, (HD, row.shape[1]), 0)
    tail = jnp.where(index == 0, high, jnp.where(index == 1, mid, jnp.where(index == 2, low, 0.0)))
    return jnp.concatenate([rows, tail.astype(bf16)], axis=0)


def attend_back_kernel(
    info_ref, query_ref, key_ref, value_ref, key_sib_ref, value_sib_ref, start_ref,
    mixed_ref, grad_ref, log_ref,
    own_ref, sib_ref, key_s, value_s, key_t, grad_key_s, grad_value_s,
):
    half = query_ref.shape[1] // 2
    ones_cols = jnp.where(
        lax.broadcasted_iota(jnp.int32, (half, HD), 1) < 3, 1.0, 0.0
    ).astype(bf16)

    def store(sibling, part, block):
        key_from, value_from = (key_sib_ref, value_sib_ref) if sibling else (key_ref, value_ref)
        lanes = slice(part * half, (part + 1) * half)
        key_rows = key_from[:, lanes]
        key_t[block] = key_rows
        key_s[block] = jnp.concatenate([key_rows.astype(f32).T.astype(bf16), ones_cols], axis=1)
        value_s[block] = jnp.concatenate(
            [value_from[:, lanes].astype(f32).T.astype(bf16), ones_cols], axis=1
        )

    place_blocks(info_ref, store)
    grad_key_s[...] = jnp.zeros_like(grad_key_s)
    grad_value_s[...] = jnp.zeros_like(grad_value_s)
    for part in range(2):
        lanes = slice(part * half, (part + 1) * half)
        query = query_ref[:, lanes] * jnp.asarray(score_scale, bf16)
        grad = grad_ref[:, lanes]
        start_row = start_ref[:, lanes]
        delta = jnp.sum(
            grad.astype(f32) * mixed_ref[:, lanes].astype(f32), axis=0, keepdims=True
        )
        query_rows = with_rows(query, -log_ref[0, :, lanes])
        grad_rows = with_rows(grad, -delta)
        query_n = query.astype(f32).T.astype(bf16)
        grad_n = grad.astype(f32).T.astype(bf16)
        own_block = info_ref[part]
        first = info_ref[4 + part]
        clear = info_ref[6 + part]

        def step(
            block, grad_query, masked, query_rows=query_rows, grad_rows=grad_rows,
            query_n=query_n, grad_n=grad_n, start_row=start_row, own_block=own_block,
        ):
            weights = jnp.exp(dot_nn(key_s[block], query_rows))
            if masked:
                weights = jnp.where(
                    allowed_mask(block * TK, own_block * TQ, start_row), weights, 0.0
                )
            grad_score = (weights * dot_nn(value_s[block], grad_rows)).astype(bf16)
            grad_value_s[block] += dot_nn(weights.astype(bf16), grad_n)
            grad_key_s[block] += dot_nn(grad_score, query_n)
            return grad_query + dot_nn(key_t[block], grad_score)

        grad_query = jnp.zeros((HD, half), f32)
        grad_query = lax.fori_loop(first, clear, functools.partial(step, masked=True), grad_query)
        grad_query = lax.fori_loop(
            clear, own_block, functools.partial(step, masked=False), grad_query
        )
        grad_query = step(own_block, grad_query, masked=True)
        own_ref[0, 0, :, lanes] = (grad_query * score_scale).astype(bf16)

    def give(sibling, part, block):
        lanes = slice(part * half, (part + 1) * half)
        key_rows = grad_key_s[block].T.astype(bf16)
        value_rows = grad_value_s[block].T.astype(bf16)
        if sibling:
            sib_ref[0, 0, :, lanes] = key_rows
            sib_ref[1, 0, :, lanes] = value_rows
        else:
            own_ref[1, 0, :, lanes] = key_rows
            own_ref[2, 0, :, lanes] = value_rows

    place_blocks(info_ref, give)


def head_spec(offset, tokens):
    return pl.BlockSpec((HD, tokens), lambda head, info: (head + offset, 0))


head_parts = ((0, 9), (9, 17))
head_parts_back = ((0, 6), (6, 12), (12, 17))


def attend(info, joined, sibling, start_row):
    tokens = joined.shape[1]
    blocks = 2 * tokens // TK
    held = ()
    for first, last in head_parts:
        heads = last - first

        def kernel(info_ref, *refs, skip=len(held)):
            attend_kernel(info_ref, *refs[:6], *refs[6 + skip :])

        held = pl.pallas_call(
            kernel,
            out_shape=(
                jax.ShapeDtypeStruct((D, tokens), bf16),
                jax.ShapeDtypeStruct((H, 1, tokens), f32),
            ),
            grid_spec=pltpu.PrefetchScalarGridSpec(
                num_scalar_prefetch=1,
                grid=(heads,),
                in_specs=[
                    head_spec(first, tokens),
                    head_spec(H + first, tokens),
                    head_spec(2 * H + first, tokens),
                    head_spec(first, tokens),
                    head_spec(H + first, tokens),
                    pl.BlockSpec((1, tokens), lambda head, info: (0, 0)),
                ]
                + [pl.BlockSpec(memory_space=pl.ANY)] * len(held),
                out_specs=(
                    head_spec(first, tokens),
                    pl.BlockSpec((1, 1, tokens), lambda head, info, f=first: (head + f, 0, 0)),
                ),
                scratch_shapes=[
                    pltpu.VMEM((blocks, TK, HD), bf16),
                    pltpu.VMEM((blocks, HD + 16, TK), bf16),
                ],
            ),
            input_output_aliases={7 + i: i for i in range(len(held))},
            compiler_params=pltpu.CompilerParams(vmem_limit_bytes=VMEM_BYTES),
            cost_estimate=pl.CostEstimate(
                flops=heads * 10 * 4 * TK * TQ * 384,
                bytes_accessed=14 * HD * heads * tokens,
                transcendentals=heads * 5 * TK * TQ,
            ),
            name="attend",
        )(info, joined, joined, joined, sibling, sibling, start_row, *held)
    return held


def attend_back(info, joined, sibling, start_row, mixed, grad_mixed, log_total):
    tokens = joined.shape[1]
    blocks = 2 * tokens // TK
    held = ()
    for first, last in head_parts_back:
        heads = last - first

        def kernel(info_ref, *refs, skip=len(held)):
            attend_back_kernel(info_ref, *refs[:9], *refs[9 + skip :])

        held = pl.pallas_call(
            kernel,
            out_shape=(
                jax.ShapeDtypeStruct((3, H, HD, tokens), bf16),
                jax.ShapeDtypeStruct((2, H, HD, tokens), bf16),
            ),
            grid_spec=pltpu.PrefetchScalarGridSpec(
                num_scalar_prefetch=1,
                grid=(heads,),
                in_specs=[
                    head_spec(first, tokens),
                    head_spec(H + first, tokens),
                    head_spec(2 * H + first, tokens),
                    head_spec(first, tokens),
                    head_spec(H + first, tokens),
                    pl.BlockSpec((1, tokens), lambda head, info: (0, 0)),
                    head_spec(first, tokens),
                    head_spec(first, tokens),
                    pl.BlockSpec((1, 1, tokens), lambda head, info, f=first: (head + f, 0, 0)),
                ]
                + [pl.BlockSpec(memory_space=pl.ANY)] * len(held),
                out_specs=(
                    pl.BlockSpec((3, 1, HD, tokens), lambda head, info, f=first: (0, head + f, 0, 0)),
                    pl.BlockSpec((2, 1, HD, tokens), lambda head, info, f=first: (0, head + f, 0, 0)),
                ),
                scratch_shapes=[
                    pltpu.VMEM((blocks, TK, 2 * HD), bf16),
                    pltpu.VMEM((blocks, TK, 2 * HD), bf16),
                    pltpu.VMEM((blocks, HD, TK), bf16),
                    pltpu.VMEM((blocks, TK, HD), f32),
                    pltpu.VMEM((blocks, TK, HD), f32),
                ],
            ),
            input_output_aliases={10 + i: i for i in range(len(held))},
            compiler_params=pltpu.CompilerParams(vmem_limit_bytes=VMEM_BYTES),
            cost_estimate=pl.CostEstimate(
                flops=heads * 10 * 10 * TK * TQ * 256,
                bytes_accessed=30 * HD * heads * tokens,
                transcendentals=heads * 5 * TK * TQ,
            ),
            name="attend_back",
        )(info, joined, joined, joined, sibling, sibling, start_row, mixed, grad_mixed, log_total, *held)
    return held


lines = [(i, (i + 2) % 8) for i in range(8)]
line_hops = [[(i, (i + 2 * hop) % 8) for i in range(8)] for hop in range(4)]
across = [(i, i ^ 1) for i in range(8)]
sibling_pairs = [(i, i ^ 1) for i in range(4)]
far_pairs = [(i, i ^ 2) for i in range(4)]
mirror_pairs = [(i, 3 - i) for i in range(4)]


def half_groups(groups):
    return (groups + 1) // 2


def assemble_kernel(info_ref, *refs, groups, pieces):
    half = half_groups(groups)
    full_ref, extra_ref, stage, in_sems, out_sems = refs[-5:]
    z, x, core = info_ref[0], info_ref[1], info_ref[2]
    slots, come, leave = [], [], []
    for which in range(2 * pieces):
        part = pl.ds((core if which < pieces else 1 - core) * half, half)
        if pieces == 1:
            target = stage.at[:, part]
        else:
            hop, side = which % 4, (which // 4) % 2
            slot = lax.rem(z - hop + 4, 4) * 2 + (1 - x if side else x)
            slots.append(slot)
            target = stage.at[slot, part]
        come.append(pltpu.make_async_copy(refs[which], target, in_sems.at[which]))
    for copy in come:
        copy.start()
    for index in range(8):
        slot = index if pieces == 1 else slots[index]
        if pieces == 1:
            if index == 0:
                come[0].wait()
                come[1].wait()
        else:
            come[index].wait()
            come[index + 8].wait()
        leave.append(
            pltpu.make_async_copy(
                stage.at[slot, pl.ds(0, groups)],
                full_ref.at[pl.ds(slot * groups, groups)],
                out_sems.at[index],
            )
        )
        if 2 * half > groups:
            leave.append(
                pltpu.make_async_copy(
                    stage.at[slot, pl.ds(groups, 1)],
                    extra_ref.at[pl.ds(slot, 1)],
                    out_sems.at[8 + index],
                )
            )
        for copy in leave[-1 if 2 * half == groups else -2 :]:
            copy.start()
    for copy in leave:
        copy.wait()


def assemble(info, pieces, groups, columns):
    any_spec = pl.BlockSpec(memory_space=pl.ANY)
    half = half_groups(groups)
    return pl.pallas_call(
        functools.partial(assemble_kernel, groups=groups, pieces=len(pieces) // 2),
        out_shape=(
            jax.ShapeDtypeStruct((8 * groups, 8, columns), bf16),
            jax.ShapeDtypeStruct((8, 8, columns), bf16),
        ),
        grid_spec=pltpu.PrefetchScalarGridSpec(
            num_scalar_prefetch=1,
            grid=(1,),
            in_specs=[any_spec] * len(pieces),
            out_specs=(any_spec, any_spec),
            scratch_shapes=[
                pltpu.VMEM((8, 2 * half, 8, columns), bf16),
                pltpu.SemaphoreType.DMA((len(pieces),)),
                pltpu.SemaphoreType.DMA((16,)),
            ],
        ),
        compiler_params=pltpu.CompilerParams(vmem_limit_bytes=VMEM_BYTES),
        cost_estimate=pl.CostEstimate(
            flops=0, bytes_accessed=2 * 8 * groups * 8 * columns * 2, transcendentals=0
        ),
        name="assemble",
    )(info, *pieces)


def core_piece(weight, core, extra=None):
    rows, columns = weight.shape
    groups = rows // 8
    half = half_groups(groups)
    grouped = weight.reshape(groups, 8, columns)
    if 2 * half > groups:
        spare = jnp.zeros((1, 8, columns), weight.dtype)
        if extra is not None:
            spare = lax.dynamic_update_slice(spare, extra.reshape(1, 1, -1), (0, 0, 0))
        grouped = jnp.concatenate([grouped, spare], axis=0)
    return lax.dynamic_slice_in_dim(grouped, core * half, half, 0)


def gather_by_lines(weight, info, core, extra=None):
    rows, columns = weight.shape
    piece = core_piece(weight, core, extra)
    line = [piece]
    for _ in range(3):
        line.append(lax.ppermute(line[-1], "dp", lines))
    other = [lax.ppermute(part, "dp", across) for part in line]
    own = line + other
    sib = [lax.ppermute(part, "seq", sibling_pairs) for part in own]
    full, spare = assemble(info, own + sib, rows // 8, columns)
    return full.reshape(8 * rows, columns), spare


def gather_whole(weight, info, core):
    rows, columns = weight.shape
    own = lax.all_gather(core_piece(weight, core), "dp", axis=0)
    sib = lax.ppermute(own, "seq", sibling_pairs)
    full, _ = assemble(info, [own, sib], rows // 8, columns)
    return full.reshape(8 * rows, columns)


def reduce_weight(grad, core, x, z):
    shards = lax.axis_size("dp")
    total_rows, columns = grad.shape
    rows = total_rows // shards
    if shards != 8:
        part = lax.psum_scatter(grad.astype(bf16), "dp", scatter_dimension=0, tiled=True)
        return lax.psum(part, "seq").astype(f32)
    groups = rows // 8
    half = half_groups(groups)
    even = groups - half
    parts = grad.astype(bf16).reshape(4, 2, groups, 8, columns)

    def core_part(which):
        return lax.dynamic_slice_in_dim(parts, which * even, half, 2)

    from_core = lax.ppermute(core_part(1 - core), "seq", sibling_pairs)
    chip = core_part(core).astype(f32) + from_core.astype(f32)
    to_x = lax.dynamic_index_in_dim(chip, 1 - x, 1, keepdims=False).astype(bf16)
    keep_x = lax.dynamic_index_in_dim(chip, x, 1, keepdims=False).astype(bf16)
    from_x = lax.ppermute(to_x, "dp", across)

    def chunk(which):
        mine = lax.dynamic_index_in_dim(keep_x, which, 0, keepdims=False)
        theirs = lax.dynamic_index_in_dim(from_x, which, 0, keepdims=False)
        return mine.astype(f32) + theirs.astype(f32)

    total = chunk(z)
    for hop in range(1, 4):
        sent = chunk(lax.rem(z + hop, 4)).astype(bf16)
        total = total + lax.ppermute(sent, "dp", line_hops[hop]).astype(f32)
    near = total.astype(bf16)
    far = lax.ppermute(near, "seq", far_pairs)
    own = near.astype(f32) + far.astype(f32)
    sib = lax.ppermute(own, "seq", sibling_pairs)
    own = own.reshape(half * 8, columns)
    sib = sib.reshape(half * 8, columns)
    cut = (half - even) * 8
    first = jnp.where(core == 0, own, sib)
    second = jnp.where(core == 0, sib, own)
    return jnp.concatenate([first, second[cut:]], axis=0)


def reduce_small(rows, x, z):
    shards = rows.shape[0]
    if shards != 8:
        part = lax.psum_scatter(rows, "dp", scatter_dimension=0)
        return lax.psum(part, "seq")
    total = rows + lax.ppermute(rows, "seq", sibling_pairs)
    total = total + lax.ppermute(total, "seq", far_pairs)
    parts = total.reshape((4, 2) + total.shape[1:])
    keep = lax.dynamic_index_in_dim(parts, x, 1, keepdims=False)
    give = lax.dynamic_index_in_dim(parts, 1 - x, 1, keepdims=False)
    keep = keep + lax.ppermute(give, "dp", across)

    def chunk(which):
        return lax.dynamic_index_in_dim(keep, which, 0, keepdims=False)

    out = chunk(z)
    for hop in range(1, 4):
        out = out + lax.ppermute(chunk(lax.rem(z + hop, 4)), "dp", line_hops[hop])
    return out


def body(
    tokens,
    qkv_weight,
    out_weight,
    up_weight,
    down_weight,
    norm_gain,
    norm_shift,
    bias_rows,
    bias_hidden,
    doc_lengths,
    cotangent,
):
    block_rows = tokens.shape[1]
    length = block_rows * lax.axis_size("seq")
    shard = tokens.shape[2] // lax.axis_size("dp")
    own = lax.axis_index("seq")
    dp_index = lax.axis_index("dp")
    core = own % 2
    kept = own // 2
    z, x = dp_index // 2, dp_index % 2
    place = jnp.stack([z, x, core]).astype(jnp.int32)

    small = jnp.concatenate(
        [norm_gain, norm_shift, bias_rows, bias_hidden.reshape(4, shard)], axis=0
    )
    if lax.axis_size("dp") == 8:
        qkv_full, spare = gather_by_lines(qkv_weight, place, core, small)
        small_all = spare[:, 0, : small.size].reshape(8, 12, shard).astype(f32)
        out_full, _ = gather_by_lines(out_weight, place, core)
        up_full = gather_whole(up_weight, place, core)
        down_full = gather_whole(down_weight, place, core)
    else:
        small_all = lax.all_gather(small, "dp", axis=0).astype(f32)
        qkv_full, out_full, up_full, down_full = (
            lax.all_gather(weight, "dp", axis=0, tiled=True)
            for weight in (qkv_weight, out_weight, up_weight, down_weight)
        )
    small_rows = jnp.transpose(small_all[:, :8], (1, 0, 2)).reshape(8, D)
    small_cols = small_rows.T
    gain_one, gain_two = small_cols[:, 0:1], small_cols[:, 1:2]
    shift_one, shift_two = small_cols[:, 2:3], small_cols[:, 3:4]
    bias_query, bias_value = small_cols[:, 4:5], small_cols[:, 5:6]
    bias_out, bias_down = small_cols[:, 6:7], small_cols[:, 7:8]
    bias_up = small_all[:, 8:].reshape(FF, 1)

    def take(rows):
        cols = jnp.transpose(rows, (0, 2, 1))
        keep = lax.dynamic_index_in_dim(cols, kept, 0, keepdims=False)
        give = lax.dynamic_index_in_dim(cols, 1 - kept, 0, keepdims=False)
        return jnp.concatenate([keep, lax.ppermute(give, "seq", mirror_pairs)], axis=1)

    def give_back(cols, dtype):
        keep = cols[:, :block_rows]
        got = lax.ppermute(cols[:, block_rows:].astype(bf16), "seq", mirror_pairs)
        keep, got = keep.astype(dtype), got.astype(dtype)
        first = jnp.where(kept == 0, keep, got)
        second = jnp.where(kept == 0, got, keep)
        return jnp.transpose(jnp.stack([first, second]), (0, 2, 1))

    x_in = take(tokens)
    cot = take(cotangent)

    lengths = lax.dynamic_index_in_dim(doc_lengths, kept, 0, keepdims=False)
    bounds = jnp.cumsum(lengths)[:-1].astype(jnp.int32)
    mirror = 3 - own
    inside = jnp.arange(block_rows, dtype=jnp.int32)
    positions = jnp.concatenate([own * block_rows + inside, mirror * block_rows + inside])
    starts = jnp.max(jnp.where(bounds[:, None] <= positions[None, :], bounds[:, None], 0), axis=0)
    firsts = jnp.stack([starts[0], starts[block_rows]]) // TK
    lasts = jnp.stack([starts[block_rows - 1], starts[2 * block_rows - 1]])
    own_blocks = jnp.stack([own, mirror])
    clears = jnp.minimum((lasts + TK - 1) // TK, own_blocks)
    near = own ^ 1
    info = jnp.concatenate(
        [own_blocks, jnp.stack([near, 3 - near]), jnp.minimum(firsts, clears), clears]
    ).astype(jnp.int32)
    start_row = starts[None, :]

    x_float = x_in.astype(f32)
    unit_one, inverse_one = norm_stats(x_float)
    normed = (unit_one * gain_one + shift_one).astype(bf16)
    joined_bias = jnp.concatenate([bias_query, jnp.zeros_like(bias_query), bias_value], axis=0)
    joined = (dot_tn(qkv_full, normed) + joined_bias).astype(bf16)
    sibling = lax.ppermute(joined[D:], "seq", sibling_pairs)
    mixed, log_total = attend(info, joined, sibling, start_row)
    residual = x_float + dot_tn(out_full, mixed) + bias_out
    unit_two, inverse_two = norm_stats(residual)
    normed_two = (unit_two * gain_two + shift_two).astype(bf16)
    up_proj = dot_tn(up_full, normed_two) + bias_up
    active, slope_of = jax.vjp(lambda pre: jax.nn.gelu(pre, approximate=True), up_proj)
    slope = slope_of(jnp.ones_like(up_proj))[0].astype(bf16)
    active = active.astype(bf16)
    layer_cols = residual + dot_tn(down_full, active) + bias_down
    layer_out = give_back(layer_cols, bf16)

    cot_float = cot.astype(f32)
    grad_down = reduce_weight(dot_nt(active, cot).astype(bf16), core, x, z)
    grad_up_proj = (dot_nn(down_full, cot) * slope.astype(f32)).astype(bf16)
    grad_up = reduce_weight(dot_nt(normed_two, grad_up_proj).astype(bf16), core, x, z)
    grad_hidden = jnp.sum(grad_up_proj.astype(f32), axis=1)
    grad_a2 = dot_nn(up_full, grad_up_proj)
    grad_gain_two = jnp.sum(grad_a2 * unit_two, axis=1)
    grad_shift_two = jnp.sum(grad_a2, axis=1)
    grad_residual = cot_float + norm_back(grad_a2, unit_two, inverse_two, gain_two)
    grad_branch = grad_residual.astype(bf16)

    grad_out = reduce_weight(dot_nt(mixed, grad_branch).astype(bf16), core, x, z)
    grad_mixed = dot_nn(out_full, grad_branch).astype(bf16)
    own_grads, sib_grads = attend_back(
        info, joined, sibling, start_row, mixed, grad_mixed, log_total
    )
    tokens_here = x_in.shape[1]
    own_grads = own_grads.reshape(3 * D, tokens_here)
    from_sib = lax.ppermute(sib_grads.reshape(2 * D, tokens_here), "seq", sibling_pairs)
    grad_joined = jnp.concatenate(
        [own_grads[:D], (own_grads[D:].astype(f32) + from_sib.astype(f32)).astype(bf16)], axis=0
    )
    grad_qkv = reduce_weight(dot_nt(normed, grad_joined).astype(bf16), core, x, z)
    joined_sums = jnp.sum(grad_joined.astype(f32), axis=1)
    grad_a1 = dot_nn(qkv_full, grad_joined)
    grad_gain_one = jnp.sum(grad_a1 * unit_one, axis=1)
    grad_shift_one = jnp.sum(grad_a1, axis=1)
    grad_x = grad_residual + norm_back(grad_a1, unit_one, inverse_one, gain_one)
    grad_tokens = give_back(grad_x, f32)

    small_grads = jnp.stack(
        [
            grad_gain_one,
            grad_gain_two,
            grad_shift_one,
            grad_shift_two,
            joined_sums[:D],
            joined_sums[2 * D :],
            jnp.sum(grad_branch.astype(f32), axis=1),
            jnp.sum(cot_float, axis=1),
        ]
    )
    shards = lax.axis_size("dp")
    small_parts = jnp.concatenate(
        [
            jnp.transpose(small_grads.reshape(8, shards, shard), (1, 0, 2)),
            grad_hidden.reshape(shards, 4, shard),
        ],
        axis=1,
    )
    small_own = reduce_small(small_parts, x, z)
    hidden_own = small_own[8:].reshape(4 * shard)

    return (
        layer_out,
        grad_tokens,
        grad_qkv,
        grad_out,
        grad_up,
        grad_down,
        small_own[0:2],
        small_own[2:4],
        small_own[4:8],
        hidden_own,
    )


def solution(mesh):
    placed = (
        P("dp", "seq", None),
        P("dp", None),
        P("dp", None),
        P("dp", None),
        P("dp", None),
        P(None, "dp"),
        P(None, "dp"),
        P(None, "dp"),
        P("dp"),
        P("dp", None),
        P("dp", "seq", None),
    )
    return jax.shard_map(
        body,
        mesh=mesh,
        in_specs=placed,
        out_specs=(
            P("dp", "seq", None),
            P("dp", "seq", None),
            P("dp", None),
            P("dp", None),
            P("dp", None),
            P("dp", None),
            P(None, "dp"),
            P(None, "dp"),
            P(None, "dp"),
            P("dp"),
        ),
        check_vma=False,
    )
```

time: 2460 us -> 986 us (0.40)
  waiting for transfers between devices: 1180 us -> 412 us
  matrix products: 684 us -> 178 us
  blocking collectives: 260 us -> 0 us
  Pallas kernels: 0 us -> 188 us
  other arithmetic: 201 us -> 63.7 us
  starting transfers between devices: 1.93 us -> 64 us
  local copies, waits for them, and re-layouts: 92.5 us -> 56 us
    all_gather x14 -> x2, waiting for transfers between devices: 580 us -> 27 us  [gather_whole(): own = lax.all_gather(core_piece(weight, core), 'dp', axis=0)]
    unnamed x18 -> x2, waiting for transfers between devices: 528 us -> 0.03 us
    dot_general x80 -> x12, matrix products: 684 us -> 178 us  [the longest x4 70.1 us: dot_nn(): lax.dot_general(left, right, (((1,), (0,)), ((), ())), preferred_element_...]
    ppermute x0 -> x72, waiting for transfers between devices: none -> 385 us  [the longest x4 120 us: reduce_weight(): from_x = lax.ppermute(to_x, 'dp', across)]
    pallas_call x0 -> x9, Pallas kernels: none -> 188 us  [the longest x3 95.1 us: attend_back(): pl.pallas_call(kernel, out_shape=(jax.ShapeDtypeStruct((3, H, HD, tokens)...]
    all_gather x8 -> x0, blocking collectives: 146 us -> none  [the longest x2 52 us: attention_set(): lax.all_gather(bias_rows, 'dp', axis=1, tiled=True)]
    reduce_sum x26 -> x5, other arithmetic: 98.1 us -> 8.91 us  [the longest x1 3.93 us: body(): joined_sums = jnp.sum(grad_joined.astype(f32), axis=1)]
    reduce_scatter x4 -> x0, waiting for transfers between devices: 67.8 us -> none  [the longest x2 67.8 us: micro_step(): lax.psum_scatter(grad_keys.reshape(length_all, D).astype(jnp.bfloat16), '...]
  transfers between devices with their start and end apart: 26 -> 74, of which waited for: 18 -> 28; matrix products, arithmetic and copies ran while one was open for 20% -> 18% of each run, Pallas kernels for 0% -> 19%
where the time goes in v1:
time: 986 us; the launch traced here: 978 us
  waiting for transfers between devices  412 us (42%)
  Pallas kernels  188 us (19%)
  matrix products  178 us (18%)
  starting transfers between devices  64 us (6%)
  other arithmetic  63.7 us (6%)
  local copies, waits for them, and re-layouts  56 us (6%)
  between operations  16 us (2%)
    ppermute x4, waiting for transfers between devices, reduce_weight(): from_x = lax.ppermute(to_x, 'dp', across)  120 us
    ppermute x12, waiting for transfers between devices, reduce_weight(): total = total + lax.ppermute(sent, 'dp', line_hops[hop]).astype(f32)  111 us
    pallas_call x3, Pallas kernels, attend_back(): pl.pallas_call(kernel, out_shape=(jax.ShapeDtypeStruct((3, H, HD, tokens)...  95.1 us
    ppermute x6, waiting for transfers between devices, gather_by_lines(): line.append(lax.ppermute(line[-1], 'dp', lines))  79.2 us
    dot_general x4, matrix products, dot_nn(): lax.dot_general(left, right, (((1,), (0,)), ((), ())), preferred_element_...  70.1 us
    pallas_call x2, Pallas kernels, attend(): pl.pallas_call(kernel, out_shape=(jax.ShapeDtypeStruct((D, tokens), bf16)...  65 us
    dot_general x4, matrix products, dot_tn(): lax.dot_general(left, right, (((0,), (0,)), ((), ())), preferred_element_...  55.9 us
    dot_general x4, matrix products, dot_nt(): lax.dot_general(left, right, (((1,), (1,)), ((), ())), preferred_element_...  52.2 us
  transfers between devices with their start and end apart: 74, of which 28 were waited for; matrix products, arithmetic and copies ran while one was open for 18% of the time, Pallas kernels for 19%

profile of v1, /device:TPU:0, one launch (start us, length us, event | category | flops | bytes accessed | tf_op | source)
XLA Modules:
  0.0 977.7 jit_solution(9878282273727644501)
XLA Ops:
  17.8 15.0 %collective-permute-done.16.refs_1_ = bf16[9,8,3264]{2,1,0:T(8,128)(2,1)} collective-permute-done((bf16[9,8,3264]{2,1,0:T(8,128)(2,1)}, bf16[9,8,3264]{2,1,0:T(8,128)(2,1)}, u32[]{:S(2)}, u32[]{:S(2)}) %collective-permute-start.16) | collective-permute-done | bytes 470048 | tf_op jit(solution)/shard_map/ppermute | solution.py:418
  39.4 20.3 %collective-permute-done.17.refs_2_ = bf16[9,8,3264]{2,1,0:T(8,128)(2,1)S(1)} collective-permute-done((bf16[9,8,3264]{2,1,0:T(8,128)(2,1)}, bf16[9,8,3264]{2,1,0:T(8,128)(2,1)S(1)}, u32[]{:S(2)}, u32[]{:S(2)}) %collective-permute-start.17) | collective-permute-done | bytes 470048 | tf_op jit(solution)/shard_map/ppermute | solution.py:418
  62.1 17.9 %collective-permute-done.18.refs_3_ = bf16[9,8,3264]{2,1,0:T(8,128)(2,1)} collective-permute-done((bf16[9,8,3264]{2,1,0:T(8,128)(2,1)S(1)}, bf16[9,8,3264]{2,1,0:T(8,128)(2,1)}, u32[]{:S(2)}, u32[]{:S(2)}) %collective-permute-start.18) | collective-permute-done | bytes 470048 | tf_op jit(solution)/shard_map/ppermute | solution.py:418
  83.7 19.9 %collective-permute-done.21.refs_6_ = bf16[9,8,3264]{2,1,0:T(8,128)(2,1)} collective-permute-done((bf16[9,8,3264]{2,1,0:T(8,128)(2,1)S(1)}, bf16[9,8,3264]{2,1,0:T(8,128)(2,1)}, u32[]{:S(2)}, u32[]{:S(2)}) %collective-permute-start.21) | collective-permute-done | bytes 470048 | tf_op jit(solution)/shard_map/ppermute | solution.py:419
  103.7 17.3 %collective-permute-done.22.refs_7_ = bf16[9,8,3264]{2,1,0:T(8,128)(2,1)} collective-permute-done((bf16[9,8,3264]{2,1,0:T(8,128)(2,1)}, bf16[9,8,3264]{2,1,0:T(8,128)(2,1)}, u32[]{:S(2)}, u32[]{:S(2)}) %collective-permute-start.22) | collective-permute-done | bytes 470048 | tf_op jit(solution)/shard_map/ppermute | solution.py:419
  203.5 27.0 %all-gather.7.cloned.1.call-done = bf16[72,8,4352]{2,1,0:T(8,128)(2,1)} async-done(((bf16[9,8,4352]{2,1,0:T(8,128)(2,1)}), bf16[72,8,4352]{2,1,0:T(8,128)(2,1)}) %all-gather.7.cloned.1.call-update) | async-done | bytes 5013520 | tf_op jit(solution)/shard_map/all_gather | solution.py:428
  230.5 34.3 %attend.2 = (bf16[1088,1024]{1,0:T(8,128)(2,1)}, f32[17,1,1024]{2,1,0:T(1,128)}) custom-call(s32[8]{0:T(128)} %concatenate.50.info_ref, bf16[3264,1024]{1,0:T(8,128)(2,1)} %copy-done.11, bf16[3264,1024]{1,0:T(8,128)(2,1)} %copy-done.11, bf16[3264,1024]{1,0:T(8,128)(2,1)} %copy-done.11, bf16[2176,1024]{1,0:T(8,128)(2,1)} %collective-permute-done.31.refs_3_.refs_4_, ...), custom_call_target="tpu_custom_call" | custom-call | flops 36238786560 | bytes 8257536 | tf_op jit(solution)/shard_map/attend/pallas_call | solution.py:219
  264.8 30.7 %attend.3 = (bf16[1088,1024]{1,0:T(8,128)(2,1)}, f32[17,1,1024]{2,1,0:T(1,128)}) custom-call(s32[8]{0:T(128)} %concatenate.50.info_ref, bf16[3264,1024]{1,0:T(8,128)(2,1)} %copy-done.11, bf16[3264,1024]{1,0:T(8,128)(2,1)} %copy-done.11, bf16[3264,1024]{1,0:T(8,128)(2,1)} %copy-done.11, ...), custom_call_target="tpu_custom_call", output_to_operand_aliasing={{0}: (7, {}), {1}: (8, {})} | custom-call | flops 32212254720 | bytes 7340032 | tf_op jit(solution)/shard_map/attend/pallas_call | solution.py:219
  319.2 19.0 %fusion.12 = f32[4352,1024]{0,1:T(8,128)} fusion(bf16[136,8,4352]{2,1,0:T(8,128)(2,1)} %get-tuple-element.32, f32[1088,1024]{1,0:T(8,128)S(1)} %get-tuple-element.108, f32[1088]{0:T(1024)S(1)} %get-tuple-element.50, f32[1088]{0:T(1024)S(1)} %get-tuple-element.48, f32[1024]{0:T(1024)S(1)} %add_rsqrt_fusion, f32[1024]{0:T(1024)S(1)} %broadcast_multiply_fusion.4), kind=kOutput, calls=%fused_computation.24 | convolution fusion | flops 9702801408 | bytes 31769088 | tf_op jit(solution)/shard_map/dot_general | solution.py:28
  338.2 31.8 %convert_reduce_fusion = (f32[4352]{0:T(1024)}, bf16[4352,1024]{0,1:T(8,128)(2,1)}) fusion(f32[4352,1024]{0,1:T(8,128)} %fusion.12, f32[4352]{0:T(1024)S(1)} %add.430, bf16[1088,512]{1,0:T(8,128)(2,1)} %collective-permute-done.35, bf16[1088,512]{1,0:T(8,128)(2,1)S(1)} %get-tuple-element.80, bf16[544,8,1088]{2,1,0:T(8,128)(2,1)} %get-tuple-element.31), kind=kOutput, calls=%fused_computation.11 | convolution fusion | flops 9808637952 | bytes 38471680 | tf_op jit(solution)/shard_map/dot_general | solution.py:32
  370.0 18.3 %multiply_reduce_fusion = (f32[1088]{0:T(1024)}, f32[1024]{0:T(1024)S(1)}, f32[1024]{0:T(1024)S(1)}, f32[1088]{0:T(1024)}, f32[1088,1024]{1,0:T(8,128)S(1)}) fusion(f32[1088,1024]{1,0:T(8,128)S(1)} %get-tuple-element.108, f32[1024]{0:T(1024)S(1)} %add_rsqrt_fusion, f32[1024]{0:T(1024)S(1)} %broadcast_multiply_fusion.4, f32[1088]{0:T(1024)S(1)} %get-tuple-element.48, ...), kind=kOutput, calls=%fused_computation.62 | convolution fusion | flops 9707253760 | bytes 27325184 | tf_op jit(solution)/shard_map/dot_general | solution.py:32
  400.7 18.9 %fusion.39 = bf16[1088,1024]{1,0:T(8,128)(2,1)} fusion(f32[1088,1024]{1,0:T(8,128)S(1)} %get-tuple-element.108, bf16[544,8,1088]{2,1,0:T(8,128)(2,1)} %get-tuple-element.31, f32[1088]{0:T(1024)S(1)} %copy-done.48, f32[4352,1024]{0,1:T(8,128)} %fusion.12, f32[4352]{0:T(1024)S(1)} %add.430), kind=kOutput, calls=%fused_computation.71 | convolution fusion | flops 9745137664 | bytes 34002176 | tf_op jit(solution)/shard_map/dot_general | solution.py:28
  419.6 17.3 %convolution_convert_fusion = bf16[4352,1088]{0,1:T(8,128)(2,1)} fusion(bf16[1088,512]{1,0:T(8,128)(2,1)} %collective-permute-done.35, bf16[1088,512]{1,0:T(8,128)(2,1)S(1)} %get-tuple-element.80, f32[4352,1024]{0,1:T(8,128)} %fusion.12, f32[4352]{0:T(1024)S(1)} %add.430), kind=kOutput, calls=%fused_computation.2 | convolution fusion | flops 9750986752 | bytes 29541376 | tf_op jit(solution)/shard_map/dot_general | solution.py:36
  456.6 33.1 %attend_back.3 = (bf16[3,17,64,1024]{3,2,1,0:T(8,128)(2,1)}, bf16[2,17,64,1024]{3,2,1,0:T(8,128)(2,1)}) custom-call(s32[8]{0:T(128)} %concatenate.50.info_ref, bf16[3264,1024]{1,0:T(8,128)(2,1)} %copy-done.11, bf16[3264,1024]{1,0:T(8,128)(2,1)} %copy-done.11, bf16[3264,1024]{1,0:T(8,128)(2,1)} %copy-done.11, ...), custom_call_target="tpu_custom_call" | custom-call | flops 40265318400 | bytes 11796480 | tf_op jit(solution)/shard_map/attend_back/pallas_call | solution.py:268
  489.7 33.5 %attend_back.4 = (bf16[3,17,64,1024]{3,2,1,0:T(8,128)(2,1)}, bf16[2,17,64,1024]{3,2,1,0:T(8,128)(2,1)}) custom-call(s32[8]{0:T(128)} %concatenate.50.info_ref, bf16[3264,1024]{1,0:T(8,128)(2,1)} %copy-done.11, bf16[3264,1024]{1,0:T(8,128)(2,1)} %copy-done.11, bf16[3264,1024]{1,0:T(8,128)(2,1)} %copy-done.11, ...), custom_call_target="tpu_custom_call", output_to_operand_aliasing={{0}: (10, {}), {1}: (11, {})} | custom-call | flops 40265318400 | bytes 11796480 | tf_op jit(solution)/shard_map/attend_back/pallas_call | solution.py:268
  523.3 28.6 %attend_back.5 = (bf16[3,17,64,1024]{3,2,1,0:T(8,128)(2,1)}, bf16[2,17,64,1024]{3,2,1,0:T(8,128)(2,1)}) custom-call(s32[8]{0:T(128)} %concatenate.50.info_ref, bf16[3264,1024]{1,0:T(8,128)(2,1)} %copy-done.11, bf16[3264,1024]{1,0:T(8,128)(2,1)} %copy-done.11, bf16[3264,1024]{1,0:T(8,128)(2,1)} %copy-done.11, ...), custom_call_target="tpu_custom_call", output_to_operand_aliasing={{0}: (10, {}), {1}: (11, {})} | custom-call | flops 33554432000 | bytes 9830400 | tf_op jit(solution)/shard_map/attend_back/pallas_call | solution.py:268
  552.0 17.2 %convolution_convert_fusion.1 = bf16[1088,4352]{1,0:T(8,128)(2,1)} fusion(bf16[4352,1024]{0,1:T(8,128)(2,1)} %get-tuple-element.112, f32[1088,1024]{1,0:T(8,128)} %copy-done.5, f32[1088]{0:T(1024)S(1)} %copy-done.47, f32[1088]{0:T(1024)S(1)} %copy-done.33, f32[1024]{0:T(1024)S(1)} %copy-done.40, f32[1024]{0:T(1024)S(1)} %copy-done.29), kind=kOutput, calls=%fused_computation.3 | convolution fusion | flops 9707536384 | bytes 22856192 | tf_op jit(solution)/shard_map/dot_general | solution.py:36
  622.5 15.6 %fusion.37 = (f32[1088]{0:T(1024)S(1)}, f32[1024]{0:T(1024)S(1)}, f32[1024]{0:T(1024)S(1)}, f32[1088]{0:T(1024)S(1)}, f32[1088,1024]{1,0:T(8,128)}) fusion(f32[1024]{0:T(1024)S(1)} %copy-done.42, f32[1024]{0:T(1024)S(1)} %copy-done.31, bf16[1088,512]{1,0:T(8,128)(2,1)S(1)} %copy-done.9, bf16[1088,512]{1,0:T(8,128)(2,1)S(1)} %copy-done.3, ...), kind=kOutput, calls=%fused_computation.58 | convolution fusion | flops 7300771840 | bytes 20501248 | tf_op jit(solution)/shard_map/dot_general | solution.py:32
  697.1 30.5 %collective-permute-done.60 = bf16[4,34,8,1088]{3,2,1,0:T(8,128)(2,1)} collective-permute-done((bf16[4,34,8,1088]{3,2,1,0:T(8,128)(2,1)}, bf16[4,34,8,1088]{3,2,1,0:T(8,128)(2,1)}, u32[]{:S(2)}, u32[]{:S(2)}) %collective-permute-start.60) | collective-permute-done | bytes 2367520 | tf_op jit(solution)/shard_map/ppermute | solution.py:453
  734.0 45.5 %collective-permute-done.53 = bf16[4,9,8,4352]{3,2,1,0:T(8,128)(2,1)} collective-permute-done((bf16[4,9,8,4352]{3,2,1,0:T(8,128)(2,1)}, bf16[4,9,8,4352]{3,2,1,0:T(8,128)(2,1)}, u32[]{:S(2)}, u32[]{:S(2)}) %collective-permute-start.53) | collective-permute-done | bytes 2506784 | tf_op jit(solution)/shard_map/ppermute | solution.py:453
  791.1 46.4 %collective-permute-done.62 = bf16[34,8,1088]{2,1,0:T(8,128)(2,1)S(1)} collective-permute-done((bf16[34,8,1088]{2,1,0:T(8,128)(2,1)S(1)}, bf16[34,8,1088]{2,1,0:T(8,128)(2,1)S(1)}, u32[]{:S(2)}, u32[]{:S(2)}) %collective-permute-start.62) | collective-permute-done | bytes 591904 | tf_op jit(solution)/shard_map/ppermute | solution.py:463
  840.7 23.2 %collective-permute-done.55 = bf16[9,8,4352]{2,1,0:T(8,128)(2,1)S(1)} collective-permute-done((bf16[9,8,4352]{2,1,0:T(8,128)(2,1)S(1)}, bf16[9,8,4352]{2,1,0:T(8,128)(2,1)S(1)}, u32[]{:S(2)}, u32[]{:S(2)}) %collective-permute-start.55) | collective-permute-done | bytes 626720 | tf_op jit(solution)/shard_map/ppermute | solution.py:463
  881.5 32.0 %collective-permute-done.39 = bf16[4,9,8,3264]{3,2,1,0:T(8,128)(2,1)S(1)} collective-permute-done((bf16[4,9,8,3264]{3,2,1,0:T(8,128)(2,1)S(1)}, bf16[4,9,8,3264]{3,2,1,0:T(8,128)(2,1)S(1)}, u32[]{:S(2)}, u32[]{:S(2)}) %collective-permute-start.39) | collective-permute-done | bytes 1880096 | tf_op jit(solution)/shard_map/ppermute | solution.py:453
  937.7 17.7 %collective-permute-done.41 = bf16[9,8,3264]{2,1,0:T(8,128)(2,1)S(1)} collective-permute-done((bf16[9,8,3264]{2,1,0:T(8,128)(2,1)S(1)}, bf16[9,8,3264]{2,1,0:T(8,128)(2,1)S(1)}, u32[]{:S(2)}, u32[]{:S(2)}) %collective-permute-start.41) | collective-permute-done | bytes 470048 | tf_op jit(solution)/shard_map/ppermute | solution.py:463
  (416 shorter events, 350.8 us)
Async XLA Ops:
  7.2 196.2 %all-gather.5.cloned.1.call-start = ((), (), s32[]{:S(2)}) async-start(), calls=%async_computation | async-start | bytes 5640192 | tf_op jit(solution)/shard_map/all_gather | solution.py:428
  9.4 221.1 %all-gather.7.cloned.1.call-start = ((), (), s32[]{:S(2)}) async-start(), calls=%async_computation.1 | async-start | bytes 5640192 | tf_op jit(solution)/shard_map/all_gather | solution.py:428
  17.2 44.4 %collective-permute-start = (bf16[1088,512]{1,0:T(8,128)(2,1)}, bf16[1088,512]{1,0:T(8,128)(2,1)S(1)}, u32[]{:S(2)}, u32[]{:S(2)}) collective-permute-start(bf16[1088,512]{1,0:T(8,128)(2,1)} %get-tuple-element.83), channel_id=1, source_target_pairs={{0,3},{1,2},{2,1},{3,0},{4,7},{5,6},{6,5},{7,4},{8,11},{9,10},{10,... | collective-permute-start | bytes 3342344 | tf_op jit(solution)/shard_map/ppermute | solution.py:547
  149.1 81.4 %collective-permute-start.31 = (bf16[2176,1024]{1,0:T(8,128)(2,1)}, bf16[2176,1024]{1,0:T(8,128)(2,1)}, u32[]{:S(2)}, u32[]{:S(2)}) collective-permute-start(bf16[2176,1024]{1,0:T(8,128)(2,1)} %slice.166), channel_id=1, source_target_pairs={{0,1},{1,0},{2,3},{3,2},{4,5},{5,4},{6,7},{7,6},{8,9},{9,8},{10,11... | collective-permute-start | bytes 13369352 | tf_op jit(solution)/shard_map/ppermute | solution.py:581
  198.1 140.1 %collective-permute-start.35 = (bf16[1088,512]{1,0:T(8,128)(2,1)}, bf16[1088,512]{1,0:T(8,128)(2,1)}, u32[]{:S(2)}, u32[]{:S(2)}) collective-permute-start(bf16[1088,512]{1,0:T(8,128)(2,1)} %get-tuple-element.81), channel_id=1, source_target_pairs={{0,3},{1,2},{2,1},{3,0},{4,7},{5,6},{6,5},{7,4},{8,11},{9,10},{10,... | collective-permute-start | bytes 3342344 | tf_op jit(solution)/shard_map/ppermute | solution.py:547
  203.5 98.4 %collective-permute-start.32 = (bf16[8,34,8,1088]{3,2,1,0:T(8,128)(2,1)}, bf16[8,34,8,1088]{3,2,1,0:T(8,128)(2,1)}, u32[]{:S(2)}, u32[]{:S(2)}) collective-permute-start(bf16[8,34,8,1088]{3,2,1,0:T(8,128)(2,1)} %bitcast.279), channel_id=1, source_target_pairs={{0,1},{1,0},{2,3},{3,2},{4,5},{5,4},{6,7},{7,6},{8,9},{9,8},{10,11... | collective-permute-start | bytes 14204936 | tf_op jit(solution)/shard_map/ppermute | solution.py:429
  230.5 80.1 %collective-permute-start.33 = (bf16[8,9,8,4352]{3,2,1,0:T(8,128)(2,1)}, bf16[8,9,8,4352]{3,2,1,0:T(8,128)(2,1)}, u32[]{:S(2)}, u32[]{:S(2)}) collective-permute-start(bf16[8,9,8,4352]{3,2,1,0:T(8,128)(2,1)} %bitcast.281), channel_id=1, source_target_pairs={{0,1},{1,0},{2,3},{3,2},{4,5},{5,4},{6,7},{7,6},{8,9},{9,8},{10,11... | collective-permute-start | bytes 15040520 | tf_op jit(solution)/shard_map/ppermute | solution.py:429
  452.2 156.1 %collective-permute-start.34 = (bf16[1088,512]{1,0:T(8,128)(2,1)}, bf16[1088,512]{1,0:T(8,128)(2,1)}, u32[]{:S(2)}, u32[]{:S(2)}) collective-permute-start(bf16[1088,512]{1,0:T(8,128)(2,1)} %slice.173), channel_id=1, source_target_pairs={{0,3},{1,2},{2,1},{3,0},{4,7},{5,6},{6,5},{7,4},{8,11},{9,10},{10,... | collective-permute-start | bytes 3342344 | tf_op jit(solution)/shard_map/ppermute | solution.py:551
  454.6 114.6 %collective-permute-start.45 = (bf16[4,2,9,8,1088]{4,3,2,1,0:T(8,128)(2,1)}, bf16[4,2,9,8,1088]{4,3,2,1,0:T(8,128)(2,1)}, u32[]{:S(2)}, u32[]{:S(2)}) collective-permute-start(bf16[4,2,9,8,1088]{4,3,2,1,0:T(8,128)(2,1)} %constant_dynamic-slice_fusion.7), channel_id=1, source_target_pairs={{0,1},{1,0},{2,3},{3,2},{4,5},{5,4},{6,7},{7,6},{8,9},{9,8},{10,11... | collective-permute-start | bytes 3760136 | tf_op jit(solution)/shard_map/ppermute | solution.py:449
  551.9 65.9 %collective-permute-start.36 = (bf16[2176,1024]{1,0:T(8,128)(2,1)}, bf16[2176,1024]{1,0:T(8,128)(2,1)}, u32[]{:S(2)}, u32[]{:S(2)}) collective-permute-start(bf16[2176,1024]{1,0:T(8,128)(2,1)} %bitcast.300), channel_id=1, source_target_pairs={{0,1},{1,0},{2,3},{3,2},{4,5},{5,4},{6,7},{7,6},{8,9},{9,8},{10,11... | collective-permute-start | bytes 13369352 | tf_op jit(solution)/shard_map/ppermute | solution.py:611
  600.7 71.0 %collective-permute-start.52 = (bf16[4,2,9,8,4352]{4,3,2,1,0:T(8,128)(2,1)}, bf16[4,2,9,8,4352]{4,3,2,1,0:T(8,128)(2,1)}, u32[]{:S(2)}, u32[]{:S(2)}) collective-permute-start(bf16[4,2,9,8,4352]{4,3,2,1,0:T(8,128)(2,1)} %constant_dynamic-slice_fusion.2), channel_id=1, source_target_pairs={{0,1},{1,0},{2,3},{3,2},{4,5},{5,4},{6,7},{7,6},{8,9},{9,8},{10,11... | collective-permute-start | bytes 15040520 | tf_op jit(solution)/shard_map/ppermute | solution.py:449
  600.8 61.0 %collective-permute-start.59 = (bf16[4,2,34,8,1088]{4,3,2,1,0:T(8,128)(2,1)}, bf16[4,2,34,8,1088]{4,3,2,1,0:T(8,128)(2,1)}, u32[]{:S(2)}, u32[]{:S(2)}) collective-permute-start(bf16[4,2,34,8,1088]{4,3,2,1,0:T(8,128)(2,1)} %constant_dynamic-slice_fusion.1), channel_id=1, source_target_pairs={{0,1},{1,0},{2,3},{3,2},{4,5},{5,4},{6,7},{7,6},{8,9},{9,8},{10,11... | collective-permute-start | bytes 14204936 | tf_op jit(solution)/shard_map/ppermute | solution.py:449
  669.9 57.7 %collective-permute-start.60 = (bf16[4,34,8,1088]{3,2,1,0:T(8,128)(2,1)}, bf16[4,34,8,1088]{3,2,1,0:T(8,128)(2,1)}, u32[]{:S(2)}, u32[]{:S(2)}) collective-permute-start(bf16[4,34,8,1088]{3,2,1,0:T(8,128)(2,1)} %get-tuple-element.64), channel_id=1, source_target_pairs={{0,4},{4,0},{8,12},{12,8},{16,20},{20,16},{24,28},{28,24},{1,5},{5... | collective-permute-start | bytes 7102472 | tf_op jit(solution)/shard_map/ppermute | solution.py:453
  679.5 100.1 %collective-permute-start.53 = (bf16[4,9,8,4352]{3,2,1,0:T(8,128)(2,1)}, bf16[4,9,8,4352]{3,2,1,0:T(8,128)(2,1)}, u32[]{:S(2)}, u32[]{:S(2)}) collective-permute-start(bf16[4,9,8,4352]{3,2,1,0:T(8,128)(2,1)} %get-tuple-element.69), channel_id=1, source_target_pairs={{0,4},{4,0},{8,12},{12,8},{16,20},{20,16},{24,28},{28,24},{1,5},{5... | collective-permute-start | bytes 7520264 | tf_op jit(solution)/shard_map/ppermute | solution.py:453
  693.3 93.1 %collective-permute-start.37 = (bf16[1088,512]{1,0:T(8,128)(2,1)S(1)}, bf16[1088,512]{1,0:T(8,128)(2,1)S(1)}, u32[]{:S(2)}, u32[]{:S(2)}) collective-permute-start(bf16[1088,512]{1,0:T(8,128)(2,1)S(1)} %slice.214), channel_id=1, source_target_pairs={{0,3},{1,2},{2,1},{3,0},{4,7},{5,6},{6,5},{7,4},{8,11},{9,10},{10,... | collective-permute-start | bytes 3342344 | tf_op jit(solution)/shard_map/ppermute | solution.py:551
  693.4 173.7 %collective-permute-start.38 = (bf16[4,2,9,8,3264]{4,3,2,1,0:T(8,128)(2,1)}, bf16[4,2,9,8,3264]{4,3,2,1,0:T(8,128)(2,1)}, u32[]{:S(2)}, u32[]{:S(2)}) collective-permute-start(bf16[4,2,9,8,3264]{4,3,2,1,0:T(8,128)(2,1)} %constant_dynamic-slice_fusion.9), channel_id=1, source_target_pairs={{0,1},{1,0},{2,3},{3,2},{4,5},{5,4},{6,7},{7,6},{8,9},{9,8},{10,11... | collective-permute-start | bytes 11280392 | tf_op jit(solution)/shard_map/ppermute | solution.py:449
  730.2 56.3 %collective-permute-start.61 = (bf16[34,8,1088]{2,1,0:T(8,128)(2,1)S(1)}, bf16[34,8,1088]{2,1,0:T(8,128)(2,1)S(1)}, u32[]{:S(2)}, u32[]{:S(2)}) collective-permute-start(bf16[34,8,1088]{2,1,0:T(8,128)(2,1)S(1)} %get-tuple-element.60), channel_id=1, source_target_pairs={{0,8},{4,12},{8,16},{12,20},{16,24},{20,28},{24,0},{28,4},{1,9},{5... | collective-permute-start | bytes 1775624 | tf_op jit(solution)/shard_map/ppermute | solution.py:463
  732.7 57.6 %collective-permute-start.63 = (bf16[34,8,1088]{2,1,0:T(8,128)(2,1)S(1)}, bf16[34,8,1088]{2,1,0:T(8,128)(2,1)S(1)}, u32[]{:S(2)}, u32[]{:S(2)}) collective-permute-start(bf16[34,8,1088]{2,1,0:T(8,128)(2,1)S(1)} %get-tuple-element.61), channel_id=1, source_target_pairs={{0,24},{4,28},{8,0},{12,4},{16,8},{20,12},{24,16},{28,20},{1,25},{... | collective-permute-start | bytes 1775624 | tf_op jit(solution)/shard_map/ppermute | solution.py:463
  779.6 57.9 %collective-permute-start.62 = (bf16[34,8,1088]{2,1,0:T(8,128)(2,1)S(1)}, bf16[34,8,1088]{2,1,0:T(8,128)(2,1)S(1)}, u32[]{:S(2)}, u32[]{:S(2)}) collective-permute-start(bf16[34,8,1088]{2,1,0:T(8,128)(2,1)S(1)} %get-tuple-element.62), channel_id=1, source_target_pairs={{0,16},{4,20},{8,24},{12,28},{16,0},{20,4},{24,8},{28,12},{1,17},{... | collective-permute-start | bytes 1775624 | tf_op jit(solution)/shard_map/ppermute | solution.py:463
  786.4 54.3 %collective-permute-start.54 = (bf16[9,8,4352]{2,1,0:T(8,128)(2,1)S(1)}, bf16[9,8,4352]{2,1,0:T(8,128)(2,1)S(1)}, u32[]{:S(2)}, u32[]{:S(2)}) collective-permute-start(bf16[9,8,4352]{2,1,0:T(8,128)(2,1)S(1)} %get-tuple-element.65), channel_id=1, source_target_pairs={{0,8},{4,12},{8,16},{12,20},{16,24},{20,28},{24,0},{28,4},{1,9},{5... | collective-permute-start | bytes 1880072 | tf_op jit(solution)/shard_map/ppermute | solution.py:463
  786.5 54.2 %collective-permute-start.56 = (bf16[9,8,4352]{2,1,0:T(8,128)(2,1)S(1)}, bf16[9,8,4352]{2,1,0:T(8,128)(2,1)S(1)}, u32[]{:S(2)}, u32[]{:S(2)}) collective-permute-start(bf16[9,8,4352]{2,1,0:T(8,128)(2,1)S(1)} %get-tuple-element.66), channel_id=1, source_target_pairs={{0,24},{4,28},{8,0},{12,4},{16,8},{20,12},{24,16},{28,20},{1,25},{... | collective-permute-start | bytes 1880072 | tf_op jit(solution)/shard_map/ppermute | solution.py:463
  790.3 73.6 %collective-permute-start.55 = (bf16[9,8,4352]{2,1,0:T(8,128)(2,1)S(1)}, bf16[9,8,4352]{2,1,0:T(8,128)(2,1)S(1)}, u32[]{:S(2)}, u32[]{:S(2)}) collective-permute-start(bf16[9,8,4352]{2,1,0:T(8,128)(2,1)S(1)} %get-tuple-element.67), channel_id=1, source_target_pairs={{0,16},{4,20},{8,24},{12,28},{16,0},{20,4},{24,8},{28,12},{1,17},{... | collective-permute-start | bytes 1880072 | tf_op jit(solution)/shard_map/ppermute | solution.py:463
  873.8 43.9 %collective-permute-start.65 = (f32[34,8,1088]{2,1,0:T(8,128)S(1)}, f32[34,8,1088]{2,1,0:T(8,128)S(1)}, u32[]{:S(2)}, u32[]{:S(2)}) collective-permute-start(f32[34,8,1088]{2,1,0:T(8,128)S(1)} %convert_add_fusion.15), channel_id=1, source_target_pairs={{0,1},{1,0},{2,3},{3,2},{4,5},{5,4},{6,7},{7,6},{8,9},{9,8},{10,11... | collective-permute-start | bytes 3551240 | tf_op jit(solution)/shard_map/ppermute | solution.py:467
  881.5 74.8 %collective-permute-start.58 = (f32[9,8,4352]{2,1,0:T(8,128)S(1)}, f32[9,8,4352]{2,1,0:T(8,128)S(1)}, u32[]{:S(2)}, u32[]{:S(2)}) collective-permute-start(f32[9,8,4352]{2,1,0:T(8,128)S(1)} %convert_add_fusion.16), channel_id=1, source_target_pairs={{0,1},{1,0},{2,3},{3,2},{4,5},{5,4},{6,7},{7,6},{8,9},{9,8},{10,11... | collective-permute-start | bytes 3760136 | tf_op jit(solution)/shard_map/ppermute | solution.py:467
  (119 other events, 3328.2 us)
Sparse Core Ops, SparseCore 0:
  10.8 125.7 all-gather.4
  139.3 91.2 all-gather.6

commit v2 on v1

--- a/solution.py
+++ b/solution.py
@@ -4,6 +4,7 @@
 import jax.numpy as jnp
 from jax import lax
 from jax.experimental import pallas as pl
+from jax.experimental.layout import Layout, with_layout_constraint
 from jax.experimental.pallas import tpu as pltpu
 from jax.sharding import PartitionSpec as P
 
@@ -34,6 +35,14 @@
 
 def dot_nt(left, right):
     return lax.dot_general(left, right, (((1,), (1,)), ((), ())), preferred_element_type=f32)
+
+
+def after(value, *others):
+    return lax.optimization_barrier((value,) + others)[0]
+
+
+def by_rows(value):
+    return with_layout_constraint(value, Layout(major_to_minor=(0, 1)))
 
 
 def norm_stats(rows):
@@ -202,112 +211,100 @@
     return pl.BlockSpec((HD, tokens), lambda head, info: (head + offset, 0))
 
 
-head_parts = ((0, 9), (9, 17))
-head_parts_back = ((0, 6), (6, 12), (12, 17))
-
-
-def attend(info, joined, sibling, start_row):
+def attend(info, joined, sibling, start_row, first, last, held=()):
     tokens = joined.shape[1]
     blocks = 2 * tokens // TK
-    held = ()
-    for first, last in head_parts:
-        heads = last - first
-
-        def kernel(info_ref, *refs, skip=len(held)):
-            attend_kernel(info_ref, *refs[:6], *refs[6 + skip :])
-
-        held = pl.pallas_call(
-            kernel,
-            out_shape=(
-                jax.ShapeDtypeStruct((D, tokens), bf16),
-                jax.ShapeDtypeStruct((H, 1, tokens), f32),
+    heads = last - first
+
+    def kernel(info_ref, *refs):
+        attend_kernel(info_ref, *refs[:6], *refs[6 + len(held) :])
+
+    return pl.pallas_call(
+        kernel,
+        out_shape=(
+            jax.ShapeDtypeStruct((D, tokens), bf16),
+            jax.ShapeDtypeStruct((H, 1, tokens), f32),
+        ),
+        grid_spec=pltpu.PrefetchScalarGridSpec(
+            num_scalar_prefetch=1,
+            grid=(heads,),
+            in_specs=[
+                head_spec(first, tokens),
+                head_spec(H + first, tokens),
+                head_spec(2 * H + first, tokens),
+                head_spec(first, tokens),
+                head_spec(H + first, tokens),
+                pl.BlockSpec((1, tokens), lambda head, info: (0, 0)),
+            ]
+            + [pl.BlockSpec(memory_space=pl.ANY)] * len(held),
+            out_specs=(
+                head_spec(first, tokens),
+                pl.BlockSpec((1, 1, tokens), lambda head, info: (head + first, 0, 0)),
             ),
-            grid_spec=pltpu.PrefetchScalarGridSpec(
-                num_scalar_prefetch=1,
-                grid=(heads,),
-                in_specs=[
-                    head_spec(first, tokens),
-                    head_spec(H + first, tokens),
-                    head_spec(2 * H + first, tokens),
-                    head_spec(first, tokens),
-                    head_spec(H + first, tokens),
-                    pl.BlockSpec((1, tokens), lambda head, info: (0, 0)),
-                ]
-                + [pl.BlockSpec(memory_space=pl.ANY)] * len(held),
-                out_specs=(
-                    head_spec(first, tokens),
-                    pl.BlockSpec((1, 1, tokens), lambda head, info, f=first: (head + f, 0, 0)),
-                ),
-                scratch_shapes=[
-                    pltpu.VMEM((blocks, TK, HD), bf16),
-                    pltpu.VMEM((blocks, HD + 16, TK), bf16),
-                ],
-            ),
-            input_output_aliases={7 + i: i for i in range(len(held))},
-            compiler_params=pltpu.CompilerParams(vmem_limit_bytes=VMEM_BYTES),
-            cost_estimate=pl.CostEstimate(
-                flops=heads * 10 * 4 * TK * TQ * 384,
-                bytes_accessed=14 * HD * heads * tokens,
-                transcendentals=heads * 5 * TK * TQ,
-            ),
-            name="attend",
-        )(info, joined, joined, joined, sibling, sibling, start_row, *held)
-    return held
-
-
-def attend_back(info, joined, sibling, start_row, mixed, grad_mixed, log_total):
+            scratch_shapes=[
+                pltpu.VMEM((blocks, TK, HD), bf16),
+                pltpu.VMEM((blocks, HD + 16, TK), bf16),
+            ],
+        ),
+        input_output_aliases={7 + i: i for i in range(len(held))},
+        compiler_params=pltpu.CompilerParams(vmem_limit_bytes=VMEM_BYTES),
+        cost_estimate=pl.CostEstimate(
+            flops=10**6, bytes_accessed=10**5, transcendentals=0
+        ),
+        name="attend",
+    )(info, joined, joined, joined, sibling, sibling, start_row, *held)
+
+
+def attend_back(
+    info, joined, sibling, start_row, mixed, grad_mixed, log_total, first, last, held=()
+):
     tokens = joined.shape[1]
     blocks = 2 * tokens // TK
-    held = ()
-    for first, last in head_parts_back:
-        heads = last - first
-
-        def kernel(info_ref, *refs, skip=len(held)):
-            attend_back_kernel(info_ref, *refs[:9], *refs[9 + skip :])
-
-        held = pl.pallas_call(
-            kernel,
-            out_shape=(
-                jax.ShapeDtypeStruct((3, H, HD, tokens), bf16),
-                jax.ShapeDtypeStruct((2, H, HD, tokens), bf16),
+    heads = last - first
+
+    def kernel(info_ref, *refs):
+        attend_back_kernel(info_ref, *refs[:9], *refs[9 + len(held) :])
+
+    return pl.pallas_call(
+        kernel,
+        out_shape=(
+            jax.ShapeDtypeStruct((3, H, HD, tokens), bf16),
+            jax.ShapeDtypeStruct((2, heads, HD, tokens), bf16),
+        ),
+        grid_spec=pltpu.PrefetchScalarGridSpec(
+            num_scalar_prefetch=1,
+            grid=(heads,),
+            in_specs=[
+                head_spec(first, tokens),
+                head_spec(H + first, tokens),
+                head_spec(2 * H + first, tokens),
+                head_spec(first, tokens),
+                head_spec(H + first, tokens),
+                pl.BlockSpec((1, tokens), lambda head, info: (0, 0)),
+                head_spec(first, tokens),
+                head_spec(first, tokens),
+                pl.BlockSpec((1, 1, tokens), lambda head, info: (head + first, 0, 0)),
+            ]
+            + [pl.BlockSpec(memory_space=pl.ANY)] * len(held),
+            out_specs=(
+                pl.BlockSpec((3, 1, HD, tokens), lambda head, info: (0, head + first, 0, 0)),
+                pl.BlockSpec((2, 1, HD, tokens), lambda head, info: (0, head, 0, 0)),
             ),
-            grid_spec=pltpu.PrefetchScalarGridSpec(
-                num_scalar_prefetch=1,
-                grid=(heads,),
-                in_specs=[
-                    head_spec(first, tokens),
-                    head_spec(H + first, tokens),
-                    head_spec(2 * H + first, tokens),
-                    head_spec(first, tokens),
-                    head_spec(H + first, tokens),
-                    pl.BlockSpec((1, tokens), lambda head, info: (0, 0)),
-                    head_spec(first, tokens),
-                    head_spec(first, tokens),
-                    pl.BlockSpec((1, 1, tokens), lambda head, info, f=first: (head + f, 0, 0)),
-                ]
-                + [pl.BlockSpec(memory_space=pl.ANY)] * len(held),
-                out_specs=(
-                    pl.BlockSpec((3, 1, HD, tokens), lambda head, info, f=first: (0, head + f, 0, 0)),
-                    pl.BlockSpec((2, 1, HD, tokens), lambda head, info, f=first: (0, head + f, 0, 0)),
-                ),
-                scratch_shapes=[
-                    pltpu.VMEM((blocks, TK, 2 * HD), bf16),
-                    pltpu.VMEM((blocks, TK, 2 * HD), bf16),
-                    pltpu.VMEM((blocks, HD, TK), bf16),
-                    pltpu.VMEM((blocks, TK, HD), f32),
-                    pltpu.VMEM((blocks, TK, HD), f32),
-                ],
-            ),
-            input_output_aliases={10 + i: i for i in range(len(held))},
-            compiler_params=pltpu.CompilerParams(vmem_limit_bytes=VMEM_BYTES),
-            cost_estimate=pl.CostEstimate(
-                flops=heads * 10 * 10 * TK * TQ * 256,
-                bytes_accessed=30 * HD * heads * tokens,
-                transcendentals=heads * 5 * TK * TQ,
-            ),
-            name="attend_back",
-        )(info, joined, joined, joined, sibling, sibling, start_row, mixed, grad_mixed, log_total, *held)
-    return held
+            scratch_shapes=[
+                pltpu.VMEM((blocks, TK, 2 * HD), bf16),
+                pltpu.VMEM((blocks, TK, 2 * HD), bf16),
+                pltpu.VMEM((blocks, HD, TK), bf16),
+                pltpu.VMEM((blocks, TK, HD), f32),
+                pltpu.VMEM((blocks, TK, HD), f32),
+            ],
+        ),
+        input_output_aliases={10 + i: i for i in range(len(held))},
+        compiler_params=pltpu.CompilerParams(vmem_limit_bytes=VMEM_BYTES),
+        cost_estimate=pl.CostEstimate(
+            flops=10**6, bytes_accessed=10**5, transcendentals=0
+        ),
+        name="attend_back",
+    )(info, joined, joined, joined, sibling, sibling, start_row, mixed, grad_mixed, log_total, *held)
 
 
 lines = [(i, (i + 2) % 8) for i in range(8)]
@@ -322,58 +319,70 @@
     return (groups + 1) // 2
 
 
-def assemble_kernel(info_ref, *refs, groups, pieces):
-    half = half_groups(groups)
+def assemble_kernel(info_ref, *refs, groups, half, pieces, by_columns):
     full_ref, extra_ref, stage, in_sems, out_sems = refs[-5:]
-    z, x, core = info_ref[0], info_ref[1], info_ref[2]
-    slots, come, leave = [], [], []
-    for which in range(2 * pieces):
-        part = pl.ds((core if which < pieces else 1 - core) * half, half)
-        if pieces == 1:
-            target = stage.at[:, part]
-        else:
+    z, x, core, far = info_ref[0], info_ref[1], info_ref[2], info_ref[3]
+    slots, come, leave = list(range(8)), [], []
+    for which in range(pieces):
+        if pieces == 16:
+            part = pl.ds((core if which < 8 else 1 - core) * half, half)
             hop, side = which % 4, (which // 4) % 2
             slot = lax.rem(z - hop + 4, 4) * 2 + (1 - x if side else x)
-            slots.append(slot)
+            if which < 8:
+                slots[which] = slot
             target = stage.at[slot, part]
+        else:
+            side = core if which % 2 == 0 else 1 - core
+            plane = far if which < 2 else 1 - far
+            if pieces == 2:
+                target = stage.at[:, pl.ds(side * half, half)]
+            elif by_columns:
+                width = stage.shape[3] // 2
+                lanes = pl.ds(pl.multiple_of(plane * width, 128), width)
+                target = stage.at[:, pl.ds(side * half, half), :, lanes]
+            else:
+                target = stage.at[:, pl.ds((plane * 2 + side) * half, half)]
         come.append(pltpu.make_async_copy(refs[which], target, in_sems.at[which]))
     for copy in come:
         copy.start()
+    if pieces < 16:
+        for copy in come:
+            copy.wait()
     for index in range(8):
-        slot = index if pieces == 1 else slots[index]
-        if pieces == 1:
-            if index == 0:
-                come[0].wait()
-                come[1].wait()
-        else:
+        slot = slots[index]
+        if pieces == 16:
             come[index].wait()
             come[index + 8].wait()
-        leave.append(
+        out = [
             pltpu.make_async_copy(
                 stage.at[slot, pl.ds(0, groups)],
                 full_ref.at[pl.ds(slot * groups, groups)],
                 out_sems.at[index],
             )
-        )
-        if 2 * half > groups:
-            leave.append(
+        ]
+        if pieces == 16:
+            out.append(
                 pltpu.make_async_copy(
                     stage.at[slot, pl.ds(groups, 1)],
                     extra_ref.at[pl.ds(slot, 1)],
                     out_sems.at[8 + index],
                 )
             )
-        for copy in leave[-1 if 2 * half == groups else -2 :]:
+        for copy in out:
             copy.start()
+        leave += out
     for copy in leave:
         copy.wait()
 
 
-def assemble(info, pieces, groups, columns):
+def assemble(info, pieces, groups, columns, by_columns=False):
     any_spec = pl.BlockSpec(memory_space=pl.ANY)
-    half = half_groups(groups)
+    half = pieces[0].shape[-3]
+    staged = groups + groups % 2
     return pl.pallas_call(
-        functools.partial(assemble_kernel, groups=groups, pieces=len(pieces) // 2),
+        functools.partial(
+            assemble_kernel, groups=groups, half=half, pieces=len(pieces), by_columns=by_columns
+        ),
         out_shape=(
             jax.ShapeDtypeStruct((8 * groups, 8, columns), bf16),
             jax.ShapeDtypeStruct((8, 8, columns), bf16),
@@ -384,14 +393,14 @@
             in_specs=[any_spec] * len(pieces),
             out_specs=(any_spec, any_spec),
             scratch_shapes=[
-                pltpu.VMEM((8, 2 * half, 8, columns), bf16),
+                pltpu.VMEM((8, staged, 8, columns), bf16),
                 pltpu.SemaphoreType.DMA((len(pieces),)),
                 pltpu.SemaphoreType.DMA((16,)),
             ],
         ),
         compiler_params=pltpu.CompilerParams(vmem_limit_bytes=VMEM_BYTES),
         cost_estimate=pl.CostEstimate(
-            flops=0, bytes_accessed=2 * 8 * groups * 8 * columns * 2, transcendentals=0
+            flops=0, bytes_accessed=10**5, transcendentals=0
         ),
         name="assemble",
     )(info, *pieces)
@@ -410,88 +419,163 @@
     return lax.dynamic_slice_in_dim(grouped, core * half, half, 0)
 
 
-def gather_by_lines(weight, info, core, extra=None):
-    rows, columns = weight.shape
-    piece = core_piece(weight, core, extra)
+def along_line(piece):
     line = [piece]
     for _ in range(3):
         line.append(lax.ppermute(line[-1], "dp", lines))
-    other = [lax.ppermute(part, "dp", across) for part in line]
-    own = line + other
-    sib = [lax.ppermute(part, "seq", sibling_pairs) for part in own]
-    full, spare = assemble(info, own + sib, rows // 8, columns)
+    return line
+
+
+def from_all(piece):
+    groups, _, columns = piece.shape
+    flat = lax.all_gather(piece.reshape(groups * 8, columns), "dp", axis=0, tiled=True)
+    return flat.reshape(8, groups, 8, columns)
+
+
+def from_across(parts):
+    return [lax.ppermute(part, "dp", across) for part in parts]
+
+
+def from_sibling(parts):
+    return [lax.ppermute(part, "seq", sibling_pairs) for part in parts]
+
+
+def whole(info, weight, pieces, by_columns=False):
+    rows, columns = weight.shape
+    full, spare = assemble(info, pieces, rows // 8, columns, by_columns)
     return full.reshape(8 * rows, columns), spare
 
 
-def gather_whole(weight, info, core):
-    rows, columns = weight.shape
-    own = lax.all_gather(core_piece(weight, core), "dp", axis=0)
-    sib = lax.ppermute(own, "seq", sibling_pairs)
-    full, _ = assemble(info, [own, sib], rows // 8, columns)
-    return full.reshape(8 * rows, columns)
-
-
-def reduce_weight(grad, core, x, z):
-    shards = lax.axis_size("dp")
-    total_rows, columns = grad.shape
-    rows = total_rows // shards
-    if shards != 8:
-        part = lax.psum_scatter(grad.astype(bf16), "dp", scatter_dimension=0, tiled=True)
-        return lax.psum(part, "seq").astype(f32)
-    groups = rows // 8
-    half = half_groups(groups)
-    even = groups - half
-    parts = grad.astype(bf16).reshape(4, 2, groups, 8, columns)
-
-    def core_part(which):
-        return lax.dynamic_slice_in_dim(parts, which * even, half, 2)
-
-    from_core = lax.ppermute(core_part(1 - core), "seq", sibling_pairs)
-    chip = core_part(core).astype(f32) + from_core.astype(f32)
-    to_x = lax.dynamic_index_in_dim(chip, 1 - x, 1, keepdims=False).astype(bf16)
-    keep_x = lax.dynamic_index_in_dim(chip, x, 1, keepdims=False).astype(bf16)
-    from_x = lax.ppermute(to_x, "dp", across)
-
-    def chunk(which):
-        mine = lax.dynamic_index_in_dim(keep_x, which, 0, keepdims=False)
-        theirs = lax.dynamic_index_in_dim(from_x, which, 0, keepdims=False)
+def whole_of_quarters(info, weight, near, far, by_columns=False):
+    near_sib, far_sib = from_sibling([near, far])
+    return whole(info, weight, [near, near_sib, far, far_sib], by_columns)[0]
+
+
+class GradSum:
+    def __init__(self, grad, place, kind, extra=None):
+        self.z, self.x, self.core, self.plane = place
+        self.shards = lax.axis_size("dp")
+        self.rows = grad.shape[0] // self.shards
+        self.columns = grad.shape[1]
+        self.kind = kind
+        grad = grad.astype(bf16)
+        self.stage = 0
+        self.extra = extra
+        self.operand = grad
+        if self.shards == 8:
+            groups = self.rows // 8
+            parts = grad.reshape(8, groups, 8, self.columns)
+            if kind == "rows":
+                self.half = self.even = groups // 4
+                parts = parts.reshape(8, 2, groups // 2, 8, self.columns)
+            else:
+                self.half = half_groups(groups)
+                self.even = groups - self.half
+            if kind == "hops":
+                if extra is not None:
+                    below = jnp.pad(extra.astype(bf16)[:, None, None, :], ((0, 0), (0, 0), (0, 7), (0, 0)))
+                    parts = jnp.concatenate([parts, below], axis=1)
+                    self.even = self.half
+                parts = parts.reshape((4, 2) + parts.shape[1:])
+            self.parts = parts
+            self.operand = self.core_part(1 - self.core)
+
+    def core_part(self, which):
+        axis = self.parts.ndim - 3
+        return lax.dynamic_slice_in_dim(self.parts, which * self.even, self.half, axis)
+
+    def chunk(self, which):
+        mine = lax.dynamic_index_in_dim(self.keep, which, 0, keepdims=False)
+        theirs = lax.dynamic_index_in_dim(self.came, which, 0, keepdims=False)
         return mine.astype(f32) + theirs.astype(f32)
 
-    total = chunk(z)
-    for hop in range(1, 4):
-        sent = chunk(lax.rem(z + hop, 4)).astype(bf16)
-        total = total + lax.ppermute(sent, "dp", line_hops[hop]).astype(f32)
-    near = total.astype(bf16)
-    far = lax.ppermute(near, "seq", far_pairs)
-    own = near.astype(f32) + far.astype(f32)
-    sib = lax.ppermute(own, "seq", sibling_pairs)
-    own = own.reshape(half * 8, columns)
-    sib = sib.reshape(half * 8, columns)
-    cut = (half - even) * 8
-    first = jnp.where(core == 0, own, sib)
-    second = jnp.where(core == 0, sib, own)
-    return jnp.concatenate([first, second[cut:]], axis=0)
-
-
-def reduce_small(rows, x, z):
-    shards = rows.shape[0]
-    if shards != 8:
-        part = lax.psum_scatter(rows, "dp", scatter_dimension=0)
-        return lax.psum(part, "seq")
-    total = rows + lax.ppermute(rows, "seq", sibling_pairs)
-    total = total + lax.ppermute(total, "seq", far_pairs)
-    parts = total.reshape((4, 2) + total.shape[1:])
-    keep = lax.dynamic_index_in_dim(parts, x, 1, keepdims=False)
-    give = lax.dynamic_index_in_dim(parts, 1 - x, 1, keepdims=False)
-    keep = keep + lax.ppermute(give, "dp", across)
-
-    def chunk(which):
-        return lax.dynamic_index_in_dim(keep, which, 0, keepdims=False)
-
-    out = chunk(z)
-    for hop in range(1, 4):
-        out = out + lax.ppermute(chunk(lax.rem(z + hop, 4)), "dp", line_hops[hop])
-    return out
+    def plane_part(self, value, which):
+        if self.kind == "rows":
+            return lax.dynamic_index_in_dim(value, which, 1, keepdims=False)
+        width = self.columns // 2
+        return lax.dynamic_slice_in_dim(value, which * width, width, 3)
+
+    def move(self, *beside):
+        self.stage += 1
+        if self.shards != 8:
+            if self.stage == 5:
+                part = lax.psum_scatter(self.operand, "dp", scatter_dimension=0, tiled=True)
+                self.operand = lax.psum(part, "seq").astype(f32)
+                if self.extra is not None:
+                    self.extra = lax.psum_scatter(self.extra, "dp", scatter_dimension=0)
+                    self.extra = lax.psum(self.extra, "seq")
+            return
+        core, x, z, plane = self.core, self.x, self.z, self.plane
+        hops = self.kind == "hops"
+
+        def arrived(value):
+            return after(value, *beside) if beside else value
+
+        if self.stage == 1:
+            from_core = arrived(lax.ppermute(self.operand, "seq", sibling_pairs))
+            chip = self.core_part(core).astype(f32) + from_core.astype(f32)
+            if hops:
+                self.operand = lax.dynamic_index_in_dim(chip, 1 - x, 1, keepdims=False).astype(bf16)
+                self.keep = lax.dynamic_index_in_dim(chip, x, 1, keepdims=False).astype(bf16)
+            elif self.kind == "plain":
+                self.operand = chip.astype(bf16)
+            else:
+                self.operand = self.plane_part(chip, 1 - plane).astype(bf16)
+                self.keep = self.plane_part(chip, plane).astype(bf16)
+        elif self.stage == 2:
+            if hops:
+                self.came = arrived(lax.ppermute(self.operand, "dp", across))
+                self.operand = [
+                    self.chunk(lax.rem(z + hop, 4)).astype(bf16) for hop in range(1, 4)
+                ]
+            elif self.kind != "plain":
+                came = arrived(lax.ppermute(self.operand, "seq", far_pairs))
+                self.operand = (self.keep.astype(f32) + came.astype(f32)).astype(bf16)
+        elif self.stage == 3:
+            if hops:
+                moved = arrived(
+                    [
+                        lax.ppermute(self.operand[hop - 1], "dp", line_hops[hop])
+                        for hop in range(1, 4)
+                    ]
+                )
+                total = self.chunk(z)
+                for part in moved:
+                    total = total + part.astype(f32)
+                self.operand = total.astype(bf16)
+            else:
+                columns = self.operand.shape[-1]
+                flat = self.operand.reshape(-1, columns)
+                self.operand = arrived(
+                    lax.psum_scatter(flat, "dp", scatter_dimension=0, tiled=True)
+                )
+        elif self.stage == 4:
+            far = arrived(lax.ppermute(self.operand, "seq", far_pairs))
+            if hops or self.kind == "plain":
+                self.operand = (self.operand.astype(f32) + far.astype(f32)).astype(bf16)
+            else:
+                first = jnp.where(plane == 0, self.operand, far)
+                second = jnp.where(plane == 0, far, self.operand)
+                axis = 1 if self.kind == "columns" else 0
+                self.operand = jnp.stack([first, second]) if axis == 0 else jnp.concatenate([first, second], axis=1)
+        else:
+            own = self.operand
+            sib = arrived(lax.ppermute(own, "seq", sibling_pairs))
+            if self.kind == "rows":
+                first = jnp.where(core == 0, own, sib)
+                second = jnp.where(core == 0, sib, own)
+                both = jnp.stack([first, second], axis=1)
+                self.operand = both.reshape(self.rows, self.columns).astype(f32)
+            else:
+                own = own.reshape(self.half * 8, self.columns)
+                sib = sib.reshape(self.half * 8, self.columns)
+                first = jnp.where(core == 0, own, sib)
+                second = jnp.where(core == 0, sib, own)
+                cut = (self.half - self.even) * 8
+                both = jnp.concatenate([first, second[cut:]], axis=0).astype(f32)
+                self.operand = both[: self.rows]
+                if self.extra is not None:
+                    self.extra = both[self.rows]
 
 
 def body(
@@ -515,17 +599,24 @@
     core = own % 2
     kept = own // 2
     z, x = dp_index // 2, dp_index % 2
-    place = jnp.stack([z, x, core]).astype(jnp.int32)
+    place = jnp.stack([z, x, core, kept]).astype(jnp.int32)
+    where = (z, x, core, kept)
 
     small = jnp.concatenate(
         [norm_gain, norm_shift, bias_rows, bias_hidden.reshape(4, shard)], axis=0
     )
-    if lax.axis_size("dp") == 8:
-        qkv_full, spare = gather_by_lines(qkv_weight, place, core, small)
+    eight = lax.axis_size("dp") == 8
+    if eight:
+        qkv_line = along_line(core_piece(qkv_weight, core, small))
+        qkv_own = qkv_line + from_across(qkv_line)
+        qkv_full, spare = whole(place, qkv_weight, qkv_own + from_sibling(qkv_own))
         small_all = spare[:, 0, : small.size].reshape(8, 12, shard).astype(f32)
-        out_full, _ = gather_by_lines(out_weight, place, core)
-        up_full = gather_whole(up_weight, place, core)
-        down_full = gather_whole(down_weight, place, core)
+        up_part = lax.dynamic_slice_in_dim(core_piece(up_weight, core), kept * (FF // 2), FF // 2, 2)
+        both_part = jnp.concatenate([up_part, core_piece(out_weight, core)], axis=2)
+        both_near = from_all(after(both_part, qkv_line[2]))
+        quarter = down_weight.shape[0] // 4
+        down_part = lax.dynamic_slice_in_dim(down_weight, own * quarter, quarter, 0)
+        down_near = from_all(after(down_part.reshape(-1, 8, D), qkv_own[5]))
     else:
         small_all = lax.all_gather(small, "dp", axis=0).astype(f32)
         qkv_full, out_full, up_full, down_full = (
@@ -546,9 +637,10 @@
         give = lax.dynamic_index_in_dim(cols, 1 - kept, 0, keepdims=False)
         return jnp.concatenate([keep, lax.ppermute(give, "seq", mirror_pairs)], axis=1)
 
-    def give_back(cols, dtype):
+    def give_back(cols, dtype, beside=()):
         keep = cols[:, :block_rows]
         got = lax.ppermute(cols[:, block_rows:].astype(bf16), "seq", mirror_pairs)
+        got = after(got, beside)
         keep, got = keep.astype(dtype), got.astype(dtype)
         first = jnp.where(kept == 0, keep, got)
         second = jnp.where(kept == 0, got, keep)
@@ -579,47 +671,88 @@
     joined_bias = jnp.concatenate([bias_query, jnp.zeros_like(bias_query), bias_value], axis=0)
     joined = (dot_tn(qkv_full, normed) + joined_bias).astype(bf16)
     sibling = lax.ppermute(joined[D:], "seq", sibling_pairs)
-    mixed, log_total = attend(info, joined, sibling, start_row)
+    held = attend(info, joined, sibling, start_row, 0, 5)
+    if eight:
+        both_near = after(both_near, held)
+        up_near, out_own = both_near[..., : FF // 2], both_near[..., FF // 2 :]
+        up_far = lax.ppermute(up_near, "seq", far_pairs)
+    mixed, log_total = attend(info, joined, sibling, start_row, 5, 17, held)
+    if eight:
+        up_far = after(up_far, mixed)
+        mixed = after(mixed, up_far, down_near)
+        down_near = after(down_near, mixed)
+        down_far = lax.ppermute(down_near, "seq", far_pairs)
+        out_own = after(out_own, mixed)
+        out_full, _ = whole(place, out_weight, [out_own] + from_sibling([out_own]))
     residual = x_float + dot_tn(out_full, mixed) + bias_out
     unit_two, inverse_two = norm_stats(residual)
     normed_two = (unit_two * gain_two + shift_two).astype(bf16)
+    if eight:
+        up_full = whole_of_quarters(place, up_weight, up_near, up_far, True)
     up_proj = dot_tn(up_full, normed_two) + bias_up
     active, slope_of = jax.vjp(lambda pre: jax.nn.gelu(pre, approximate=True), up_proj)
     slope = slope_of(jnp.ones_like(up_proj))[0].astype(bf16)
     active = active.astype(bf16)
-    layer_cols = residual + dot_tn(down_full, active) + bias_down
-    layer_out = give_back(layer_cols, bf16)
-
-    cot_float = cot.astype(f32)
-    grad_down = reduce_weight(dot_nt(active, cot).astype(bf16), core, x, z)
-    grad_up_proj = (dot_nn(down_full, cot) * slope.astype(f32)).astype(bf16)
-    grad_up = reduce_weight(dot_nt(normed_two, grad_up_proj).astype(bf16), core, x, z)
+    active, slope = lax.optimization_barrier((by_rows(active), by_rows(slope)))
+    down_sum = GradSum(by_rows(dot_nt(active, cot).astype(bf16)), where, "rows")
+    active = after(active, down_sum.operand)
+    if eight:
+        down_far = after(down_far, active)
+        down_full = whole_of_quarters(place, down_weight, down_near, down_far)
+    layer_cols = (residual + dot_tn(down_full, active) + bias_down).astype(bf16)
+
+    down_sum.move(layer_cols)
+    cot_two = after(cot, down_sum.operand)
+    grad_up_proj = (dot_nn(down_full, cot_two) * slope.astype(f32)).astype(bf16)
+    grad_up_proj = by_rows(grad_up_proj)
     grad_hidden = jnp.sum(grad_up_proj.astype(f32), axis=1)
+    up_sum = GradSum(by_rows(dot_nt(normed_two, grad_up_proj).astype(bf16)), where, "columns")
+    down_sum.move(up_sum.operand)
+    grad_up_proj = after(grad_up_proj, up_sum.operand, down_sum.operand)
     grad_a2 = dot_nn(up_full, grad_up_proj)
     grad_gain_two = jnp.sum(grad_a2 * unit_two, axis=1)
     grad_shift_two = jnp.sum(grad_a2, axis=1)
+    cot_float = cot.astype(f32)
     grad_residual = cot_float + norm_back(grad_a2, unit_two, inverse_two, gain_two)
     grad_branch = grad_residual.astype(bf16)
 
-    grad_out = reduce_weight(dot_nt(mixed, grad_branch).astype(bf16), core, x, z)
+    up_sum.move(grad_branch)
+    out_sum = GradSum(by_rows(dot_nt(mixed, grad_branch).astype(bf16)), where, "plain")
     grad_mixed = dot_nn(out_full, grad_branch).astype(bf16)
-    own_grads, sib_grads = attend_back(
-        info, joined, sibling, start_row, mixed, grad_mixed, log_total
+    out_sum.move(grad_mixed)
+    grad_mixed = after(grad_mixed, up_sum.operand, out_sum.operand, down_sum.operand)
+    back = functools.partial(
+        attend_back, info, joined, sibling, start_row, mixed, grad_mixed, log_total
     )
+    own_grads, sib_one = back(0, 6)
+    own_grads = after(own_grads, sib_one)
+    layer_out = give_back(after(layer_cols, sib_one), bf16, sib_one)
+    own_grads, sib_two = back(6, 12, (own_grads,))
+    sib_one = lax.ppermute(sib_one, "seq", sibling_pairs)
+    up_sum.move(sib_two)
+    out_sum.move()
+    out_sum.move(sib_two)
+    own_grads = after(own_grads, up_sum.operand, out_sum.operand)
+    own_grads, sib_three = back(12, 17, (own_grads,))
+    sib_two = lax.ppermute(sib_two, "seq", sibling_pairs)
+    sib_three = lax.ppermute(sib_three, "seq", sibling_pairs)
     tokens_here = x_in.shape[1]
-    own_grads = own_grads.reshape(3 * D, tokens_here)
-    from_sib = lax.ppermute(sib_grads.reshape(2 * D, tokens_here), "seq", sibling_pairs)
-    grad_joined = jnp.concatenate(
-        [own_grads[:D], (own_grads[D:].astype(f32) + from_sib.astype(f32)).astype(bf16)], axis=0
+    from_sib = jnp.concatenate([sib_one, sib_two, sib_three], axis=1)
+    key_value = (own_grads[1:].astype(f32) + from_sib.astype(f32)).astype(bf16)
+    grad_joined = lax.dynamic_update_slice(own_grads, key_value, (1, 0, 0, 0))
+    grad_joined = by_rows(grad_joined.reshape(3 * D, tokens_here))
+    cut_at = 3 * D // 2
+    first_sum = GradSum(
+        by_rows(dot_nt(normed, grad_joined[:cut_at]).astype(bf16)), where, "hops"
     )
-    grad_qkv = reduce_weight(dot_nt(normed, grad_joined).astype(bf16), core, x, z)
+    grad_joined = after(grad_joined, first_sum.operand)
     joined_sums = jnp.sum(grad_joined.astype(f32), axis=1)
+    first_sum.move(joined_sums)
+    down_sum.move(joined_sums)
+    grad_joined = after(grad_joined, first_sum.operand)
     grad_a1 = dot_nn(qkv_full, grad_joined)
     grad_gain_one = jnp.sum(grad_a1 * unit_one, axis=1)
     grad_shift_one = jnp.sum(grad_a1, axis=1)
-    grad_x = grad_residual + norm_back(grad_a1, unit_one, inverse_one, gain_one)
-    grad_tokens = give_back(grad_x, f32)
-
     small_grads = jnp.stack(
         [
             grad_gain_one,
@@ -640,16 +773,32 @@
         ],
         axis=1,
     )
-    small_own = reduce_small(small_parts, x, z)
+    small_flat = small_parts.reshape(shards, 12 * shard)
+    second_sum = GradSum(
+        by_rows(dot_nt(normed, grad_joined[cut_at:]).astype(bf16)), where, "hops", small_flat
+    )
+    grad_x = grad_residual + norm_back(grad_a1, unit_one, inverse_one, gain_one)
+    first_sum.move(second_sum.operand)
+    second_sum.move(grad_x)
+    up_sum.move(second_sum.operand)
+    first_sum.move(second_sum.operand)
+    second_sum.move(second_sum.operand)
+    grad_tokens = give_back(grad_x, f32, second_sum.operand)
+    layer_out = after(layer_out, second_sum.operand)
+    for total in (first_sum, second_sum, down_sum, up_sum, out_sum):
+        while total.stage < 5:
+            total.move()
+    grad_qkv = jnp.concatenate([first_sum.operand, second_sum.operand], axis=1)
+    small_own = second_sum.extra.reshape(12, shard)
     hidden_own = small_own[8:].reshape(4 * shard)
 
     return (
         layer_out,
         grad_tokens,
         grad_qkv,
-        grad_out,
-        grad_up,
-        grad_down,
+        out_sum.operand,
+        up_sum.operand,
+        down_sum.operand,
         small_own[0:2],
         small_own[2:4],
         small_own[4:8],

time: 986 us -> 738 us (0.75)
  waiting for transfers between devices: 412 us -> 176 us
  starting transfers between devices: 64 us -> 37.6 us
  other arithmetic: 63.7 us -> 85 us
    ppermute x67 -> x50, waiting for transfers between devices: 385 us -> 153 us  [the longest x5 42.7 us: move(): far = arrived(lax.ppermute(self.operand, 'seq', far_pairs))]
    all_gather x2, waiting for transfers between devices: 27 us -> 0.01 us  [from_all(): lax.all_gather(piece.reshape(groups * 8, columns), 'dp', axis=0, tiled=True)]
    ppermute x67 -> x50, starting transfers between devices: 61.6 us -> 35.8 us  [the longest x6 17 us: move(): lax.ppermute(self.operand[hop - 1], 'dp', line_hops[hop])]
    convert_element_type x5, local copies, waits for them, and re-layouts: 20.1 us -> 4.45 us  [the longest x2 2.49 us: move(): lax.dynamic_index_in_dim(chip, x, 1, keepdims=False).astype(bf16)]
    dot_general x4, matrix products: 70.1 us -> 57.2 us  [dot_nn(): lax.dot_general(left, right, (((1,), (0,)), ((), ())), preferred_element_...]
    optimization_barrier x0 -> x3, waiting for transfers between devices: none -> 10.3 us  [after(): return lax.optimization_barrier((value,) + others)[0]]
    ppermute x2, waiting for transfers between devices: 0.01 us -> 10.2 us  [give_back(): got = lax.ppermute(cols[:, block_rows:].astype(bf16), 'seq', mirror_pairs)]
    convert_element_type x9 -> x15, other arithmetic: 15.8 us -> 21.8 us  [the longest x2 8.47 us: move(): self.operand = (self.keep.astype(f32) + came.astype(f32)).astype(bf16)]
  transfers between devices with their start and end apart: 74 -> 60, of which waited for: 28 -> 24; matrix products, arithmetic and copies ran while one was open for 18% -> 39% of each run, Pallas kernels for 19% -> 26%
where the time goes in v2:
time: 738 us; the launch traced here: 726 us
  Pallas kernels  187 us (25%)
  waiting for transfers between devices  176 us (24%)
  matrix products  169 us (23%)
  other arithmetic  85 us (12%)
  local copies, waits for them, and re-layouts  55.8 us (8%)
  starting transfers between devices  37.6 us (5%)
  between operations  15.7 us (2%)
    pallas_call x3, Pallas kernels, attend_back(): pl.pallas_call(kernel, out_shape=(jax.ShapeDtypeStruct((3, H, HD, tokens)...  94.5 us
    pallas_call x2, Pallas kernels, attend(): pl.pallas_call(kernel, out_shape=(jax.ShapeDtypeStruct((D, tokens), bf16)...  65 us
    dot_general x4, matrix products, dot_tn(): lax.dot_general(left, right, (((0,), (0,)), ((), ())), preferred_element_...  64 us
    dot_general x4, matrix products, dot_nn(): lax.dot_general(left, right, (((1,), (0,)), ((), ())), preferred_element_...  57.2 us
    dot_general x5, matrix products, dot_nt(): lax.dot_general(left, right, (((1,), (1,)), ((), ())), preferred_element_...  47.6 us
    ppermute x5, waiting for transfers between devices, move(): far = arrived(lax.ppermute(self.operand, 'seq', far_pairs))  42.7 us
    ppermute x3, waiting for transfers between devices, along_line(): line.append(lax.ppermute(line[-1], 'dp', lines))  29.5 us
    pallas_call x4, Pallas kernels, assemble(): pl.pallas_call(functools.partial(assemble_kernel, groups=groups, half=hal...  27.6 us
  transfers between devices with their start and end apart: 60, of which 24 were waited for; matrix products, arithmetic and copies ran while one was open for 39% of the time, Pallas kernels for 26%

profile of v2, /device:TPU:0, one launch (start us, length us, event | category | flops | bytes accessed | tf_op | source)
XLA Modules:
  0.0 726.3 jit_solution(18145426752085498699)
XLA Ops:
  29.3 12.2 %collective-permute-done.2.refs_2_ = bf16[9,8,3264]{2,1,0:T(8,128)(2,1)} collective-permute-done((bf16[9,8,3264]{2,1,0:T(8,128)(2,1)}, bf16[9,8,3264]{2,1,0:T(8,128)(2,1)}, u32[]{:S(2)}, u32[]{:S(2)}) %collective-permute-start.2) | collective-permute-done | bytes 470048 | tf_op jit(solution)/shard_map/ppermute | solution.py:425
  45.2 9.6 %collective-permute-done.3.refs_3_ = bf16[9,8,3264]{2,1,0:T(8,128)(2,1)} collective-permute-done((bf16[9,8,3264]{2,1,0:T(8,128)(2,1)}, bf16[9,8,3264]{2,1,0:T(8,128)(2,1)}, u32[]{:S(2)}, u32[]{:S(2)}) %collective-permute-start.3) | collective-permute-done | bytes 470048 | tf_op jit(solution)/shard_map/ppermute | solution.py:425
  59.2 12.9 %collective-permute-done.6.refs_6_ = bf16[9,8,3264]{2,1,0:T(8,128)(2,1)} collective-permute-done((bf16[9,8,3264]{2,1,0:T(8,128)(2,1)}, bf16[9,8,3264]{2,1,0:T(8,128)(2,1)}, u32[]{:S(2)}, u32[]{:S(2)}) %collective-permute-start.6) | collective-permute-done | bytes 470048 | tf_op jit(solution)/shard_map/ppermute | solution.py:436
  94.3 12.4 %add_convert_fusion.refs_0_.refs_1_.refs_2_ = bf16[3264,1024]{1,0:T(8,128)(2,1)S(1)} fusion(bf16[136,8,3264]{2,1,0:T(8,128)(2,1)} %get-tuple-element.63, f32[3264]{0:T(1024)S(1)} %reduce.10, f32[1088]{0:T(1024)S(1)} %get-tuple-element.129, f32[1088]{0:T(1024)S(1)} %get-tuple-element.130, f32[1024]{0:T(1024)S(1)} %add_rsqrt_fusion.1, ...), kind=kOutput, calls=%fused_computation.14 | convolution fusion | flops 7289634816 | bytes 16045312 | tf_op jit(solution)/shard_map/dot_general | solution.py:29
  118.6 20.2 %attend.2 = (bf16[1088,1024]{1,0:T(8,128)(2,1)}, f32[17,1,1024]{2,1,0:T(1,128)}) custom-call(s32[8]{0:T(128)} %concatenate.73.info_ref, bf16[3264,1024]{1,0:T(8,128)(2,1)} %copy-done.2, bf16[3264,1024]{1,0:T(8,128)(2,1)} %copy-done.2, bf16[3264,1024]{1,0:T(8,128)(2,1)} %copy-done.2, bf16[2176,1024]{1,0:T(8,128)(2,1)} %collective-permute-done.16.refs_3_.refs_4_, ...), custom_call_target="tpu_custom_call" | custom-call | flops 1000000 | bytes 100000 | tf_op jit(solution)/shard_map/attend/pallas_call | solution.py:222
  144.1 44.9 %attend.3 = (bf16[1088,1024]{1,0:T(8,128)(2,1)}, f32[17,1,1024]{2,1,0:T(1,128)}) custom-call(s32[8]{0:T(128)} %concatenate.73.info_ref, bf16[3264,1024]{1,0:T(8,128)(2,1)} %copy-done.2, bf16[3264,1024]{1,0:T(8,128)(2,1)} %copy-done.2, bf16[3264,1024]{1,0:T(8,128)(2,1)} %copy-done.2, ...), custom_call_target="tpu_custom_call", output_to_operand_aliasing={{0}: (7, {}), {1}: (8, {})} | custom-call | flops 1000000 | bytes 100000 | tf_op jit(solution)/shard_map/attend/pallas_call | solution.py:222
  214.7 8.7 %assemble.6 = (bf16[136,8,4352]{2,1,0:T(8,128)(2,1)}, bf16[8,8,4352]{2,1,0:T(8,128)(2,1)}) custom-call(s32[4]{0:T(128)} %pad_add_fusion.1.info_ref, bf16[8,9,8,2176]{3,2,1,0:T(8,128)(2,1)} %copy-done.18, bf16[8,9,8,2176]{3,2,1,0:T(8,128)(2,1)} %collective-permute-done.21.refs_1_, bf16[8,9,8,2176]{3,2,1,0:T(8,128)(2,1)} %collective-permute-done.17.refs_2_, ...), custom_call_target="tpu_custom_call" | custom-call | bytes 100000 | tf_op jit(solution)/shard_map/assemble/pallas_call | solution.py:382
  223.4 29.6 %fusion.6 = (bf16[4352,1024]{1,0:T(8,128)(2,1)}, bf16[4352,1024]{1,0:T(8,128)(2,1)}) fusion(f32[4352]{0:T(1024)S(1)} %add.349, f32[1088,1024]{1,0:T(8,128)S(1)} %get-tuple-element.173, f32[1088]{0:T(1024)S(1)} %copy-done.50, f32[1088]{0:T(1024)S(1)} %get-tuple-element.127, f32[1024]{0:T(1024)S(1)} %add_rsqrt_fusion, f32[1024]{0:T(1024)S(1)} %broadcast_multiply_fusion.4, ...), kind=kOutput, calls=%fused_computation.10 | convolution fusion | flops 9796386816 | bytes 31786496 | tf_op jit(solution)/shard_map/dot_general | solution.py:29
  253.1 14.8 %convolution_convert_fusion.1 = bf16[4352,1088]{1,0:T(8,128)(2,1)S(1)} fusion(bf16[4352,1024]{1,0:T(8,128)(2,1)} %get-tuple-element.77, bf16[1088,512]{1,0:T(8,128)(2,1)} %collective-permute-done.23, bf16[1088,512]{1,0:T(8,128)(2,1)S(1)} %copy-done.15), kind=kOutput, calls=%fused_computation.3 | convolution fusion | flops 9706422272 | bytes 20611072 | tf_op jit(solution)/shard_map/dot_general | solution.py:37
  273.1 9.3 %collective-permute-done.20.refs_2_ = bf16[8,17,8,1088]{3,2,1,0:T(8,128)(2,1)} collective-permute-done((bf16[8,17,8,1088]{3,2,1,0:T(8,128)(2,1)}, bf16[8,17,8,1088]{3,2,1,0:T(8,128)(2,1)}, u32[]{:S(2)}, u32[]{:S(2)}) %collective-permute-start.20) | collective-permute-done | bytes 2367520 | tf_op jit(solution)/shard_map/ppermute | solution.py:684
  296.2 16.6 %fusion.40 = bf16[1088,1024]{1,0:T(8,128)(2,1)} fusion(f32[1088,1024]{1,0:T(8,128)S(1)} %bitcast.210, bf16[4352,1024]{1,0:T(8,128)(2,1)} %get-tuple-element.77, bf16[544,8,1088]{2,1,0:T(8,128)(2,1)} %get-tuple-element.79, f32[1088]{0:T(1024)S(1)} %copy-done.51), kind=kOutput, calls=%fused_computation.72 | convolution fusion | flops 9700573184 | bytes 25071872 | tf_op jit(solution)/shard_map/dot_general | solution.py:29
  321.8 18.7 %fusion.93 = (bf16[4352]{0:T(1024)(128)(2,1)S(1)}, bf16[4352,1024]{1,0:T(8,128)(2,1)}) fusion(bf16[4352,1024]{1,0:T(8,128)(2,1)} %get-tuple-element.82, bf16[1088,1024]{1,0:T(8,128)(2,1)S(1)} %copy-done.31, bf16[544,8,1088]{2,1,0:T(8,128)(2,1)} %get-tuple-element.79), kind=kOutput, calls=%fused_computation.234 | convolution fusion | flops 9715052544 | bytes 29532672 | tf_op jit(solution)/shard_map/dot_general | solution.py:33
  340.6 17.0 %convolution_convert_fusion = bf16[1088,4352]{1,0:T(8,128)(2,1)} fusion(bf16[4352,1024]{1,0:T(8,128)(2,1)} %get-tuple-element.84, f32[1088,1024]{1,0:T(8,128)} %copy-done.5, f32[1088]{0:T(1024)S(1)} %copy-done.50, f32[1088]{0:T(1024)S(1)} %get-tuple-element.127, f32[1024]{0:T(1024)S(1)} %add_rsqrt_fusion, f32[1024]{0:T(1024)S(1)} %broadcast_multiply_fusion.4), kind=kOutput, calls=%fused_computation.2 | convolution fusion | flops 9707536384 | bytes 22856192 | tf_op jit(solution)/shard_map/dot_general | solution.py:37
  363.1 13.9 %collective-permute-done.26 = bf16[8,17,8,1088]{3,2,1,0:T(8,128)(2,1)} collective-permute-done((bf16[8,17,8,1088]{3,2,1,0:T(8,128)(2,1)S(1)}, bf16[8,17,8,1088]{3,2,1,0:T(8,128)(2,1)}, u32[]{:S(2)}, u32[]{:S(2)}) %collective-permute-start.26) | collective-permute-done | bytes 2367520 | tf_op jit(solution)/shard_map/ppermute | solution.py:532
  380.9 18.1 %multiply_reduce_fusion = (bf16[1088]{0:T(1024)(128)(2,1)S(1)}, f32[1024]{0:T(1024)S(1)}, f32[1024]{0:T(1024)S(1)}, bf16[1088]{0:T(1024)(128)(2,1)S(1)}, f32[1088,1024]{1,0:T(8,128)S(1)}) fusion(f32[1088,1024]{1,0:T(8,128)S(1)} %bitcast.212, f32[1024]{0:T(1024)S(1)} %add_rsqrt_fusion, f32[1024]{0:T(1024)S(1)} %broadcast_multiply_fusion.4, ...), kind=kOutput, calls=%fused_computation.62 | convolution fusion | flops 9707253760 | bytes 27320832 | tf_op jit(solution)/shard_map/dot_general | solution.py:33
  427.2 33.2 %attend_back.3 = (bf16[3,17,64,1024]{3,2,1,0:T(8,128)(2,1)}, bf16[2,6,64,1024]{3,2,1,0:T(8,128)(2,1)}) custom-call(s32[8]{0:T(128)} %concatenate.73.info_ref, bf16[3264,1024]{1,0:T(8,128)(2,1)} %copy-done.2, bf16[3264,1024]{1,0:T(8,128)(2,1)} %copy-done.2, bf16[3264,1024]{1,0:T(8,128)(2,1)} %copy-done.2, ...), custom_call_target="tpu_custom_call" | custom-call | flops 1000000 | bytes 100000 | tf_op jit(solution)/shard_map/attend_back/pallas_call | solution.py:268
  463.8 33.3 %attend_back.4 = (bf16[3,17,64,1024]{3,2,1,0:T(8,128)(2,1)}, bf16[2,6,64,1024]{3,2,1,0:T(8,128)(2,1)}) custom-call(s32[8]{0:T(128)} %concatenate.73.info_ref, bf16[3264,1024]{1,0:T(8,128)(2,1)} %copy-done.2, bf16[3264,1024]{1,0:T(8,128)(2,1)} %copy-done.2, bf16[3264,1024]{1,0:T(8,128)(2,1)} %copy-done.2, ...), custom_call_target="tpu_custom_call", output_to_operand_aliasing={{0}: (10, {})} | custom-call | flops 1000000 | bytes 100000 | tf_op jit(solution)/shard_map/attend_back/pallas_call | solution.py:268
  497.2 10.2 %collective-permute-done.29 = bf16[1088,512]{1,0:T(8,128)(2,1)} collective-permute-done((bf16[1088,512]{1,0:T(8,128)(2,1)}, bf16[1088,512]{1,0:T(8,128)(2,1)}, u32[]{:S(2)}, u32[]{:S(2)}) %collective-permute-start.29) | collective-permute-done | bytes 1114144 | tf_op jit(solution)/shard_map/ppermute | solution.py:642
  512.0 28.0 %attend_back.5 = (bf16[3,17,64,1024]{3,2,1,0:T(8,128)(2,1)}, bf16[2,5,64,1024]{3,2,1,0:T(8,128)(2,1)}) custom-call(s32[8]{0:T(128)} %concatenate.73.info_ref, bf16[3264,1024]{1,0:T(8,128)(2,1)} %copy-done.2, bf16[3264,1024]{1,0:T(8,128)(2,1)} %copy-done.2, bf16[3264,1024]{1,0:T(8,128)(2,1)} %copy-done.2, ...), custom_call_target="tpu_custom_call", output_to_operand_aliasing={{0}: (10, {})} | custom-call | flops 1000000 | bytes 100000 | tf_op jit(solution)/shard_map/attend_back/pallas_call | solution.py:268
  585.1 14.1 %fusion.34 = (f32[1024]{0:T(1024)S(1)}, bf16[1088]{0:T(1024)(128)(2,1)S(1)}, f32[1024]{0:T(1024)S(1)}, bf16[1088]{0:T(1024)(128)(2,1)S(1)}, f32[1088,1024]{1,0:T(8,128)}) fusion(f32[1088]{0:T(1024)S(1)} %copy-done.44, f32[1024]{0:T(1024)S(1)} %copy-done.46, f32[1024]{0:T(1024)S(1)} %copy-done.42, bf16[1088,512]{1,0:T(8,128)(2,1)S(1)} %copy-done.20, ...), kind=kOutput, calls=%fused_computation.55 | convolution fusion | flops 7287402496 | bytes 20496896 | tf_op jit(solution)/shard_map/dot_general | solution.py:33
  626.3 9.6 %collective-permute-done.40 = bf16[9,8,1632]{2,1,0:T(8,128)(2,1)S(1)} collective-permute-done((bf16[9,8,1632]{2,1,0:T(8,128)(2,1)S(1)}, bf16[9,8,1632]{2,1,0:T(8,128)(2,1)S(1)}, u32[]{:S(2)}, u32[]{:S(2)}) %collective-permute-start.40) | collective-permute-done | bytes 235040 | tf_op jit(solution)/shard_map/ppermute | solution.py:538
  642.2 10.3 %reduce-scatter.12.cloned.1.call-done = bf16[72,2176]{1,0:T(8,128)(2,1)} async-done(((bf16[576,2176]{1,0:T(8,128)(2,1)}), bf16[72,2176]{1,0:T(8,128)(2,1)}) %reduce-scatter.12.cloned.1.call-update) | async-done | bytes 313360 | tf_op jit(solution)/shard_map/optimization_barrier | solution.py:41
  653.7 21.7 %collective-permute-done.51 = bf16[72,2176]{1,0:T(8,128)(2,1)S(1)} collective-permute-done((bf16[72,2176]{1,0:T(8,128)(2,1)}, bf16[72,2176]{1,0:T(8,128)(2,1)S(1)}, u32[]{:S(2)}, u32[]{:S(2)}) %collective-permute-start.51) | collective-permute-done | bytes 313376 | tf_op jit(solution)/shard_map/ppermute | solution.py:553
  678.1 10.3 %collective-permute-start.44 = (bf16[9,8,1632]{2,1,0:T(8,128)(2,1)S(1)}, bf16[9,8,1632]{2,1,0:T(8,128)(2,1)S(1)}, u32[]{:S(2)}, u32[]{:S(2)}) collective-permute-start(bf16[9,8,1632]{2,1,0:T(8,128)(2,1)S(1)} %get-tuple-element.153), channel_id=1, source_target_pairs={{0,8},{4,12},{8,16},{12,20},{16,24},{20,28},{24,0},{28,4},{1,9},{5... | collective-permute-start | bytes 705032 | tf_op jit(solution)/shard_map/ppermute | solution.py:538
  (390 shorter events, 281.0 us)
Async XLA Ops:
  7.2 131.6 %all-gather.3.cloned.1.call-start = ((), (), s32[]{:S(2)}) async-start(), calls=%async_computation.3 | async-start | bytes 4313088 | tf_op jit(solution)/shard_map/all_gather | solution.py:431
  16.7 27.6 %collective-permute-start = (bf16[1088,512]{1,0:T(8,128)(2,1)}, bf16[1088,512]{1,0:T(8,128)(2,1)S(1)}, u32[]{:S(2)}, u32[]{:S(2)}) collective-permute-start(bf16[1088,512]{1,0:T(8,128)(2,1)} %get-tuple-element.145), channel_id=1, source_target_pairs={{0,3},{1,2},{2,1},{3,0},{4,7},{5,6},{6,5},{7,4},{8,11},{9,10},{10,... | collective-permute-start | bytes 3342344 | tf_op jit(solution)/shard_map/ppermute | solution.py:638
  17.3 26.4 %collective-permute-start.4 = (bf16[9,8,3264]{2,1,0:T(8,128)(2,1)}, bf16[9,8,3264]{2,1,0:T(8,128)(2,1)}, u32[]{:S(2)}, u32[]{:S(2)}) collective-permute-start(bf16[9,8,3264]{2,1,0:T(8,128)(2,1)} %fusion.58.refs_0_), channel_id=1, source_target_pairs={{0,4},{4,0},{8,12},{12,8},{16,20},{20,16},{24,28},{28,24},{1,5},{5... | collective-permute-start | bytes 1410056 | tf_op jit(solution)/shard_map/ppermute | solution.py:436
  18.8 24.9 %collective-permute-start.8 = (bf16[9,8,3264]{2,1,0:T(8,128)(2,1)}, bf16[9,8,3264]{2,1,0:T(8,128)(2,1)}, u32[]{:S(2)}, u32[]{:S(2)}) collective-permute-start(bf16[9,8,3264]{2,1,0:T(8,128)(2,1)} %fusion.58.refs_0_), channel_id=1, source_target_pairs={{0,1},{1,0},{2,3},{3,2},{4,5},{5,4},{6,7},{7,6},{8,9},{9,8},{10,11... | collective-permute-start | bytes 1410056 | tf_op jit(solution)/shard_map/ppermute | solution.py:440
  42.4 154.9 %all-gather.5.cloned.1.call-start = ((), (), s32[]{:S(2)}) async-start(), calls=%async_computation.4 | async-start | bytes 2820096 | tf_op jit(solution)/shard_map/all_gather | solution.py:431
  44.2 27.9 %collective-permute-start.6 = (bf16[9,8,3264]{2,1,0:T(8,128)(2,1)}, bf16[9,8,3264]{2,1,0:T(8,128)(2,1)}, u32[]{:S(2)}, u32[]{:S(2)}) collective-permute-start(bf16[9,8,3264]{2,1,0:T(8,128)(2,1)} %collective-permute-done.2.refs_2_), channel_id=1, source_target_pairs={{0,4},{4,0},{8,12},{12,8},{16,20},{20,16},{24,28},{28,24},{1,5},{5... | collective-permute-start | bytes 1410056 | tf_op jit(solution)/shard_map/ppermute | solution.py:436
  54.8 24.9 %collective-permute-start.7 = (bf16[9,8,3264]{2,1,0:T(8,128)(2,1)}, bf16[9,8,3264]{2,1,0:T(8,128)(2,1)}, u32[]{:S(2)}, u32[]{:S(2)}) collective-permute-start(bf16[9,8,3264]{2,1,0:T(8,128)(2,1)} %collective-permute-done.3.refs_3_), channel_id=1, source_target_pairs={{0,4},{4,0},{8,12},{12,8},{16,20},{20,16},{24,28},{28,24},{1,5},{5... | collective-permute-start | bytes 1410056 | tf_op jit(solution)/shard_map/ppermute | solution.py:436
  111.9 395.6 %reduce-scatter.10.cloned.1.call-start = ((), (), s32[]{:S(2)}) async-start(), calls=%async_computation.5 | async-start | bytes 1492992
  140.7 56.6 %collective-permute-start.17 = (bf16[8,9,8,2176]{3,2,1,0:T(8,128)(2,1)S(1)}, bf16[8,9,8,2176]{3,2,1,0:T(8,128)(2,1)}, u32[]{:S(2)}, u32[]{:S(2)}) collective-permute-start(bf16[8,9,8,2176]{3,2,1,0:T(8,128)(2,1)S(1)} %slice.155.refs_0_), channel_id=1, source_target_pairs={{0,2},{1,3},{2,0},{3,1},{4,6},{5,7},{6,4},{7,5},{8,10},{9,11},{10,... | collective-permute-start | bytes 7520264 | tf_op jit(solution)/shard_map/ppermute | solution.py:678
  201.5 51.6 %collective-permute-start.23 = (bf16[1088,512]{1,0:T(8,128)(2,1)}, bf16[1088,512]{1,0:T(8,128)(2,1)}, u32[]{:S(2)}, u32[]{:S(2)}) collective-permute-start(bf16[1088,512]{1,0:T(8,128)(2,1)} %get-tuple-element.142), channel_id=1, source_target_pairs={{0,3},{1,2},{2,1},{3,0},{4,7},{5,6},{6,5},{7,4},{8,11},{9,10},{10,... | collective-permute-start | bytes 3342344 | tf_op jit(solution)/shard_map/ppermute | solution.py:638
  202.8 79.5 %collective-permute-start.20 = (bf16[8,17,8,1088]{3,2,1,0:T(8,128)(2,1)}, bf16[8,17,8,1088]{3,2,1,0:T(8,128)(2,1)}, u32[]{:S(2)}, u32[]{:S(2)}) collective-permute-start(bf16[8,17,8,1088]{3,2,1,0:T(8,128)(2,1)} %bitcast.234), channel_id=1, source_target_pairs={{0,2},{1,3},{2,0},{3,1},{4,6},{5,7},{6,4},{7,5},{8,10},{9,11},{10,... | collective-permute-start | bytes 7102472 | tf_op jit(solution)/shard_map/ppermute | solution.py:684
  204.6 81.3 %collective-permute-start.19 = (bf16[8,17,8,1088]{3,2,1,0:T(8,128)(2,1)}, bf16[8,17,8,1088]{3,2,1,0:T(8,128)(2,1)}, u32[]{:S(2)}, u32[]{:S(2)}) collective-permute-start(bf16[8,17,8,1088]{3,2,1,0:T(8,128)(2,1)} %bitcast.235), channel_id=1, source_target_pairs={{0,1},{1,0},{2,3},{3,2},{4,5},{5,4},{6,7},{7,6},{8,9},{9,8},{10,11... | collective-permute-start | bytes 7102472 | tf_op jit(solution)/shard_map/ppermute | solution.py:440
  282.4 30.4 %collective-permute-start.25 = (bf16[8,2,17,8,1088]{4,3,2,1,0:T(8,128)(2,1)}, bf16[8,2,17,8,1088]{4,3,2,1,0:T(8,128)(2,1)}, u32[]{:S(2)}, u32[]{:S(2)}) collective-permute-start(bf16[8,2,17,8,1088]{4,3,2,1,0:T(8,128)(2,1)} %constant_dynamic-slice_fusion.3), channel_id=1, source_target_pairs={{0,1},{1,0},{2,3},{3,2},{4,5},{5,4},{6,7},{7,6},{8,9},{9,8},{10,11... | collective-permute-start | bytes 14204936 | tf_op jit(solution)/shard_map/ppermute | solution.py:515
  320.4 56.6 %collective-permute-start.26 = (bf16[8,17,8,1088]{3,2,1,0:T(8,128)(2,1)S(1)}, bf16[8,17,8,1088]{3,2,1,0:T(8,128)(2,1)}, u32[]{:S(2)}, u32[]{:S(2)}) collective-permute-start(bf16[8,17,8,1088]{3,2,1,0:T(8,128)(2,1)S(1)} %fusion.46), channel_id=1, source_target_pairs={{0,2},{1,3},{2,0},{3,1},{4,6},{5,7},{6,4},{7,5},{8,10},{9,11},{10,... | collective-permute-start | bytes 7102472 | tf_op jit(solution)/shard_map/ppermute | solution.py:532
  363.0 54.8 %collective-permute-start.27 = (bf16[8,9,8,4352]{3,2,1,0:T(8,128)(2,1)}, bf16[8,9,8,4352]{3,2,1,0:T(8,128)(2,1)}, u32[]{:S(2)}, u32[]{:S(2)}) collective-permute-start(bf16[8,9,8,4352]{3,2,1,0:T(8,128)(2,1)} %constant_dynamic-slice_fusion.2), channel_id=1, source_target_pairs={{0,1},{1,0},{2,3},{3,2},{4,5},{5,4},{6,7},{7,6},{8,9},{9,8},{10,11... | collective-permute-start | bytes 15040520 | tf_op jit(solution)/shard_map/ppermute | solution.py:515
  417.8 144.6 %reduce-scatter.14.cloned.1.call-start = ((), (), s32[]{:S(2)}) async-start(), calls=%async_computation.7 | async-start | bytes 2820096
  426.8 80.6 %collective-permute-start.30 = (bf16[8,9,8,2176]{3,2,1,0:T(8,128)(2,1)}, bf16[8,9,8,2176]{3,2,1,0:T(8,128)(2,1)}, u32[]{:S(2)}, u32[]{:S(2)}) collective-permute-start(bf16[8,9,8,2176]{3,2,1,0:T(8,128)(2,1)} %dynamic-slice_convert_fusion.1), channel_id=1, source_target_pairs={{0,2},{1,3},{2,0},{3,1},{4,6},{5,7},{6,4},{7,5},{8,10},{9,11},{10,... | collective-permute-start | bytes 7520264 | tf_op jit(solution)/shard_map/ppermute | solution.py:532
  461.6 45.8 %collective-permute-start.29 = (bf16[1088,512]{1,0:T(8,128)(2,1)}, bf16[1088,512]{1,0:T(8,128)(2,1)}, u32[]{:S(2)}, u32[]{:S(2)}) collective-permute-start(bf16[1088,512]{1,0:T(8,128)(2,1)} %slice.162), channel_id=1, source_target_pairs={{0,3},{1,2},{2,1},{3,0},{4,7},{5,6},{6,5},{7,4},{8,11},{9,10},{10,... | collective-permute-start | bytes 3342344 | tf_op jit(solution)/shard_map/ppermute | solution.py:642
  461.6 190.9 %reduce-scatter.12.cloned.1.call-start = ((), (), s32[]{:S(2)}) async-start(), calls=%async_computation.6 | async-start | bytes 2820096
  463.8 85.5 %collective-permute-start.31 = (bf16[2,6,64,1024]{3,2,1,0:T(8,128)(2,1)}, bf16[2,6,64,1024]{3,2,1,0:T(8,128)(2,1)}, u32[]{:S(2)}, u32[]{:S(2)}) collective-permute-start(bf16[2,6,64,1024]{3,2,1,0:T(8,128)(2,1)} %get-tuple-element.89), channel_id=1, source_target_pairs={{0,1},{1,0},{2,3},{3,2},{4,5},{5,4},{6,7},{7,6},{8,9},{9,8},{10,11... | collective-permute-start | bytes 4718600 | tf_op jit(solution)/shard_map/ppermute | solution.py:731
  497.1 52.2 %collective-permute-start.32 = (bf16[2,6,64,1024]{3,2,1,0:T(8,128)(2,1)}, bf16[2,6,64,1024]{3,2,1,0:T(8,128)(2,1)}, u32[]{:S(2)}, u32[]{:S(2)}) collective-permute-start(bf16[2,6,64,1024]{3,2,1,0:T(8,128)(2,1)} %get-tuple-element.94), channel_id=1, source_target_pairs={{0,1},{1,0},{2,3},{3,2},{4,5},{5,4},{6,7},{7,6},{8,9},{9,8},{10,11... | collective-permute-start | bytes 4718600 | tf_op jit(solution)/shard_map/ppermute | solution.py:737
  584.3 29.4 %collective-permute-start.38 = (bf16[4,9,8,1632]{3,2,1,0:T(8,128)(2,1)}, bf16[4,9,8,1632]{3,2,1,0:T(8,128)(2,1)}, u32[]{:S(2)}, u32[]{:S(2)}) collective-permute-start(bf16[4,9,8,1632]{3,2,1,0:T(8,128)(2,1)} %get-tuple-element.150), channel_id=1, source_target_pairs={{0,4},{4,0},{8,12},{12,8},{16,20},{20,16},{24,28},{28,24},{1,5},{5... | collective-permute-start | bytes 2820104 | tf_op jit(solution)/shard_map/ppermute | solution.py:527
  641.3 49.5 %collective-permute-start.37 = (bf16[1088,512]{1,0:T(8,128)(2,1)}, bf16[1088,512]{1,0:T(8,128)(2,1)}, u32[]{:S(2)}, u32[]{:S(2)}) collective-permute-start(bf16[1088,512]{1,0:T(8,128)(2,1)} %slice.240), channel_id=1, source_target_pairs={{0,3},{1,2},{2,1},{3,0},{4,7},{5,6},{6,5},{7,4},{8,11},{9,10},{10,... | collective-permute-start | bytes 3342344 | tf_op jit(solution)/shard_map/ppermute | solution.py:642
  641.4 35.4 %collective-permute-start.36 = (bf16[4,9,8,1632]{3,2,1,0:T(8,128)(2,1)}, bf16[4,9,8,1632]{3,2,1,0:T(8,128)(2,1)}, u32[]{:S(2)}, u32[]{:S(2)}) collective-permute-start(bf16[4,9,8,1632]{3,2,1,0:T(8,128)(2,1)} %get-tuple-element.155), channel_id=1, source_target_pairs={{0,4},{4,0},{8,12},{12,8},{16,20},{20,16},{24,28},{28,24},{1,5},{5... | collective-permute-start | bytes 2820104 | tf_op jit(solution)/shard_map/ppermute | solution.py:527
  (102 other events, 1364.9 us)
Sparse Core Ops, SparseCore 0:
  42.5 73.1 all-gather.2
  118.4 52.0 all-gather.4
  417.9 61.9 reduce-scatter.9
  483.4 68.8 reduce-scatter.13
  577.2 75.2 reduce-scatter.11

commit v3 on v2

--- a/solution.py
+++ b/solution.py
@@ -64,8 +64,7 @@
         store(which // 2, which % 2, info_ref[which])
 
 
-def allowed_mask(key_first, query_first, start_row):
-    shape = (TK, TQ)
+def allowed_mask(shape, key_first, query_first, start_row):
     key_pos = key_first + lax.broadcasted_iota(jnp.int32, shape, 0)
     query_pos = query_first + lax.broadcasted_iota(jnp.int32, shape, 1)
     return (key_pos <= query_pos) & (key_pos >= start_row)
@@ -93,16 +92,20 @@
         first = info_ref[4 + part]
         clear = info_ref[6 + part]
 
-        def step(block, state, masked, query=query, start_row=start_row, own_block=own_block):
+        def step(
+            block, state, masked, keys=TK, queries=slice(0, TQ), query=query,
+            start_row=start_row, own_block=own_block,
+        ):
             peak, total = state
-            scores = dot_nn(key_s[block], query)
+            scores = dot_nn(key_s[block, :keys], query[:, queries])
             if masked:
-                scores = jnp.where(
-                    allowed_mask(block * TK, own_block * TQ, start_row), scores, masked_score
+                allowed = allowed_mask(
+                    scores.shape, block * TK, own_block * TQ + queries.start, start_row[:, queries]
                 )
+                scores = jnp.where(allowed, scores, masked_score)
             new_peak = jnp.maximum(peak, jnp.max(scores, axis=0, keepdims=True))
             weights = jnp.exp(scores - new_peak).astype(bf16)
-            total = total * jnp.exp(peak - new_peak) + dot_nn(value_s[block], weights)
+            total = total * jnp.exp(peak - new_peak) + dot_nn(value_s[block, :, :keys], weights)
             return new_peak, total
 
         state = (
@@ -111,10 +114,14 @@
         )
         state = lax.fori_loop(first, clear, functools.partial(step, masked=True), state)
         state = lax.fori_loop(clear, own_block, functools.partial(step, masked=False), state)
-        peak, total = step(own_block, state, masked=True)
-        row_sum = total[HD : HD + 1]
-        mixed_ref[:, lanes] = (total[:HD] / row_sum).astype(bf16)
-        log_ref[0, :, lanes] = peak + jnp.log(row_sum)
+        for queries, keys in ((slice(0, TQ // 2), TK // 2), (slice(TQ // 2, TQ), TK)):
+            peak, total = step(
+                own_block, tuple(part[:, queries] for part in state), True, keys, queries
+            )
+            row_sum = total[HD : HD + 1]
+            place = slice(lanes.start + queries.start, lanes.start + queries.stop)
+            mixed_ref[:, place] = (total[:HD] / row_sum).astype(bf16)
+            log_ref[0, :, place] = peak + jnp.log(row_sum)
 
 
 def split_three(row):
@@ -172,26 +179,31 @@
         clear = info_ref[6 + part]
 
         def step(
-            block, grad_query, masked, query_rows=query_rows, grad_rows=grad_rows,
-            query_n=query_n, grad_n=grad_n, start_row=start_row, own_block=own_block,
+            block, grad_query, masked, keys=TK, queries=slice(0, TQ), query_rows=query_rows,
+            grad_rows=grad_rows, query_n=query_n, grad_n=grad_n, start_row=start_row,
+            own_block=own_block,
         ):
-            weights = jnp.exp(dot_nn(key_s[block], query_rows))
+            weights = jnp.exp(dot_nn(key_s[block, :keys], query_rows[:, queries]))
             if masked:
-                weights = jnp.where(
-                    allowed_mask(block * TK, own_block * TQ, start_row), weights, 0.0
+                allowed = allowed_mask(
+                    weights.shape, block * TK, own_block * TQ + queries.start, start_row[:, queries]
                 )
-            grad_score = (weights * dot_nn(value_s[block], grad_rows)).astype(bf16)
-            grad_value_s[block] += dot_nn(weights.astype(bf16), grad_n)
-            grad_key_s[block] += dot_nn(grad_score, query_n)
-            return grad_query + dot_nn(key_t[block], grad_score)
+                weights = jnp.where(allowed, weights, 0.0)
+            grad_prob = dot_nn(value_s[block, :keys], grad_rows[:, queries])
+            grad_score = (weights * grad_prob).astype(bf16)
+            grad_value_s[block, :keys] += dot_nn(weights.astype(bf16), grad_n[queries])
+            grad_key_s[block, :keys] += dot_nn(grad_score, query_n[queries])
+            return grad_query + dot_nn(key_t[block, :, :keys], grad_score)
 
         grad_query = jnp.zeros((HD, half), f32)
         grad_query = lax.fori_loop(first, clear, functools.partial(step, masked=True), grad_query)
         grad_query = lax.fori_loop(
             clear, own_block, functools.partial(step, masked=False), grad_query
         )
-        grad_query = step(own_block, grad_query, masked=True)
-        own_ref[0, 0, :, lanes] = (grad_query * score_scale).astype(bf16)
+        for queries, keys in ((slice(0, TQ // 2), TK // 2), (slice(TQ // 2, TQ), TK)):
+            total = step(own_block, grad_query[:, queries], True, keys, queries)
+            place = slice(lanes.start + queries.start, lanes.start + queries.stop)
+            own_ref[0, 0, :, place] = (total * score_scale).astype(bf16)
 
     def give(sibling, part, block):
         lanes = slice(part * half, (part + 1) * half)
@@ -452,7 +464,7 @@
 
 
 class GradSum:
-    def __init__(self, grad, place, kind, extra=None):
+    def __init__(self, grad, place, kind):
         self.z, self.x, self.core, self.plane = place
         self.shards = lax.axis_size("dp")
         self.rows = grad.shape[0] // self.shards
@@ -460,7 +472,6 @@
         self.kind = kind
         grad = grad.astype(bf16)
         self.stage = 0
-        self.extra = extra
         self.operand = grad
         if self.shards == 8:
             groups = self.rows // 8
@@ -472,10 +483,6 @@
                 self.half = half_groups(groups)
                 self.even = groups - self.half
             if kind == "hops":
-                if extra is not None:
-                    below = jnp.pad(extra.astype(bf16)[:, None, None, :], ((0, 0), (0, 0), (0, 7), (0, 0)))
-                    parts = jnp.concatenate([parts, below], axis=1)
-                    self.even = self.half
                 parts = parts.reshape((4, 2) + parts.shape[1:])
             self.parts = parts
             self.operand = self.core_part(1 - self.core)
@@ -501,9 +508,6 @@
             if self.stage == 5:
                 part = lax.psum_scatter(self.operand, "dp", scatter_dimension=0, tiled=True)
                 self.operand = lax.psum(part, "seq").astype(f32)
-                if self.extra is not None:
-                    self.extra = lax.psum_scatter(self.extra, "dp", scatter_dimension=0)
-                    self.extra = lax.psum(self.extra, "seq")
             return
         core, x, z, plane = self.core, self.x, self.z, self.plane
         hops = self.kind == "hops"
@@ -573,9 +577,7 @@
                 second = jnp.where(core == 0, sib, own)
                 cut = (self.half - self.even) * 8
                 both = jnp.concatenate([first, second[cut:]], axis=0).astype(f32)
-                self.operand = both[: self.rows]
-                if self.extra is not None:
-                    self.extra = both[self.rows]
+                self.operand = both
 
 
 def body(
@@ -637,10 +639,11 @@
         give = lax.dynamic_index_in_dim(cols, 1 - kept, 0, keepdims=False)
         return jnp.concatenate([keep, lax.ppermute(give, "seq", mirror_pairs)], axis=1)
 
-    def give_back(cols, dtype, beside=()):
+    def mirrored(cols):
+        return lax.ppermute(cols[:, block_rows:].astype(bf16), "seq", mirror_pairs)
+
+    def give_back(cols, got, dtype):
         keep = cols[:, :block_rows]
-        got = lax.ppermute(cols[:, block_rows:].astype(bf16), "seq", mirror_pairs)
-        got = after(got, beside)
         keep, got = keep.astype(dtype), got.astype(dtype)
         first = jnp.where(kept == 0, keep, got)
         second = jnp.where(kept == 0, got, keep)
@@ -717,25 +720,30 @@
     grad_branch = grad_residual.astype(bf16)
 
     up_sum.move(grad_branch)
-    out_sum = GradSum(by_rows(dot_nt(mixed, grad_branch).astype(bf16)), where, "plain")
+    out_sum = GradSum(by_rows(dot_nt(mixed, grad_branch).astype(bf16)), where, "hops")
     grad_mixed = dot_nn(out_full, grad_branch).astype(bf16)
     out_sum.move(grad_mixed)
-    grad_mixed = after(grad_mixed, up_sum.operand, out_sum.operand, down_sum.operand)
+    grad_mixed = after(grad_mixed, out_sum.operand, up_sum.operand)
     back = functools.partial(
         attend_back, info, joined, sibling, start_row, mixed, grad_mixed, log_total
     )
-    own_grads, sib_one = back(0, 6)
-    own_grads = after(own_grads, sib_one)
-    layer_out = give_back(after(layer_cols, sib_one), bf16, sib_one)
-    own_grads, sib_two = back(6, 12, (own_grads,))
+    own_grads, sib_one = back(0, 8)
+    up_sum.move(sib_one)
+    out_sum.move(sib_one)
+    own_grads = after(own_grads, sib_one, up_sum.operand, out_sum.operand)
+    own_grads, sib_two = back(8, 13, (own_grads,))
     sib_one = lax.ppermute(sib_one, "seq", sibling_pairs)
-    up_sum.move(sib_two)
-    out_sum.move()
+    got = after(mirrored(after(layer_cols, up_sum.operand)), sib_two)
+    layer_out = give_back(layer_cols, got, bf16)
+    down_sum.move(sib_two)
     out_sum.move(sib_two)
-    own_grads = after(own_grads, up_sum.operand, out_sum.operand)
-    own_grads, sib_three = back(12, 17, (own_grads,))
+    own_grads = after(own_grads, sib_two, down_sum.operand, layer_out, out_sum.operand)
+    own_grads, sib_three = back(13, 17, (own_grads,))
     sib_two = lax.ppermute(sib_two, "seq", sibling_pairs)
     sib_three = lax.ppermute(sib_three, "seq", sibling_pairs)
+    up_sum.move(sib_three)
+    down_sum.move(sib_three)
+    out_sum.move(sib_three)
     tokens_here = x_in.shape[1]
     from_sib = jnp.concatenate([sib_one, sib_two, sib_three], axis=1)
     key_value = (own_grads[1:].astype(f32) + from_sib.astype(f32)).astype(bf16)
@@ -746,13 +754,17 @@
         by_rows(dot_nt(normed, grad_joined[:cut_at]).astype(bf16)), where, "hops"
     )
     grad_joined = after(grad_joined, first_sum.operand)
-    joined_sums = jnp.sum(grad_joined.astype(f32), axis=1)
-    first_sum.move(joined_sums)
-    down_sum.move(joined_sums)
-    grad_joined = after(grad_joined, first_sum.operand)
+    second_sum = GradSum(
+        by_rows(dot_nt(normed, grad_joined[cut_at:]).astype(bf16)), where, "hops"
+    )
+    first_sum.move(second_sum.operand)
+    joined_sums = jnp.sum(after(grad_joined, first_sum.operand).astype(f32), axis=1)
+    second_sum.move(joined_sums)
+    grad_joined = after(grad_joined, second_sum.operand, joined_sums)
     grad_a1 = dot_nn(qkv_full, grad_joined)
     grad_gain_one = jnp.sum(grad_a1 * unit_one, axis=1)
     grad_shift_one = jnp.sum(grad_a1, axis=1)
+
     small_grads = jnp.stack(
         [
             grad_gain_one,
@@ -773,23 +785,25 @@
         ],
         axis=1,
     )
-    small_flat = small_parts.reshape(shards, 12 * shard)
-    second_sum = GradSum(
-        by_rows(dot_nt(normed, grad_joined[cut_at:]).astype(bf16)), where, "hops", small_flat
-    )
+    small_flat = jnp.pad(small_parts.reshape(shards, 1, 12 * shard), ((0, 0), (0, 7), (0, 0)))
+    small_sum = GradSum(small_flat.reshape(shards * 8, 12 * shard), where, "hops")
     grad_x = grad_residual + norm_back(grad_a1, unit_one, inverse_one, gain_one)
+    first_sum.move(grad_x)
+    first_operand = first_sum.operand
+    got = mirrored(grad_x)
+    small_sum.move(first_operand)
+    second_sum.move(first_operand)
+    small_sum.operand = after(small_sum.operand, second_sum.operand)
+    up_sum.operand = after(up_sum.operand, second_sum.operand)
     first_sum.move(second_sum.operand)
-    second_sum.move(grad_x)
+    second_sum.move()
     up_sum.move(second_sum.operand)
-    first_sum.move(second_sum.operand)
-    second_sum.move(second_sum.operand)
-    grad_tokens = give_back(grad_x, f32, second_sum.operand)
-    layer_out = after(layer_out, second_sum.operand)
-    for total in (first_sum, second_sum, down_sum, up_sum, out_sum):
+    grad_tokens = give_back(grad_x, after(got, second_sum.operand), f32)
+    for total in (first_sum, second_sum, small_sum, up_sum, down_sum, out_sum):
         while total.stage < 5:
             total.move()
     grad_qkv = jnp.concatenate([first_sum.operand, second_sum.operand], axis=1)
-    small_own = second_sum.extra.reshape(12, shard)
+    small_own = small_sum.operand[0].reshape(12, shard)
     hidden_own = small_own[8:].reshape(4 * shard)
 
     return (

time: 738 us -> 720 us (0.976)
  waiting for transfers between devices: 176 us -> 135 us
  starting transfers between devices: 37.6 us -> 66.2 us
    ppermute x5 -> x6, waiting for transfers between devices: 42.7 us -> 4.25 us  [move(): far = arrived(lax.ppermute(self.operand, 'seq', far_pairs))]
    ppermute x2 -> x4, waiting for transfers between devices: 1.05 us -> 28.1 us  [move(): self.came = arrived(lax.ppermute(self.operand, 'dp', across))]
    ppermute x6 -> x12, starting transfers between devices: 17 us -> 37.9 us  [move(): lax.ppermute(self.operand[hop - 1], 'dp', line_hops[hop])]
    ppermute x6 -> x12, waiting for transfers between devices: 23 us -> 9.01 us  [move(): lax.ppermute(self.operand[hop - 1], 'dp', line_hops[hop])]
    optimization_barrier x3 -> x2, waiting for transfers between devices: 10.3 us -> 0.02 us  [after(): return lax.optimization_barrier((value,) + others)[0]]
    ppermute x2, waiting for transfers between devices: 10.2 us -> 0.01 us  [mirrored(): return lax.ppermute(cols[:, block_rows:].astype(bf16), 'seq', mirror_pairs)]
  transfers between devices with their start and end apart: 60 -> 70, of which waited for: 24 -> 23; matrix products, arithmetic and copies ran while one was open for 39% -> 40% of each run, Pallas kernels for 26% -> 26%
where the time goes in v3:
time: 720 us; the launch traced here: 711 us
  Pallas kernels  183 us (25%)
  matrix products  170 us (24%)
  waiting for transfers between devices  135 us (19%)
  other arithmetic  86.7 us (12%)
  starting transfers between devices  66.2 us (9%)
  local copies, waits for them, and re-layouts  54.3 us (8%)
  between operations  15.6 us (2%)
    pallas_call x3, Pallas kernels, attend_back(): pl.pallas_call(kernel, out_shape=(jax.ShapeDtypeStruct((3, H, HD, tokens)...  93.4 us
    dot_general x4, matrix products, dot_tn(): lax.dot_general(left, right, (((0,), (0,)), ((), ())), preferred_element_...  63.9 us
    pallas_call x2, Pallas kernels, attend(): pl.pallas_call(kernel, out_shape=(jax.ShapeDtypeStruct((D, tokens), bf16)...  62.3 us
    dot_general x4, matrix products, dot_nn(): lax.dot_general(left, right, (((1,), (0,)), ((), ())), preferred_element_...  58.5 us
    dot_general x5, matrix products, dot_nt(): lax.dot_general(left, right, (((1,), (1,)), ((), ())), preferred_element_...  47.5 us
    ppermute x12, starting transfers between devices, move(): lax.ppermute(self.operand[hop - 1], 'dp', line_hops[hop])  37.9 us
    ppermute x3, waiting for transfers between devices, along_line(): line.append(lax.ppermute(line[-1], 'dp', lines))  29.5 us
    ppermute x4, waiting for transfers between devices, move(): self.came = arrived(lax.ppermute(self.operand, 'dp', across))  28.1 us
  transfers between devices with their start and end apart: 70, of which 23 were waited for; matrix products, arithmetic and copies ran while one was open for 40% of the time, Pallas kernels for 26%

profile of v3, /device:TPU:0, one launch (start us, length us, event | category | flops | bytes accessed | tf_op | source)
XLA Modules:
  0.0 710.7 jit_solution(15298931141918807101)
XLA Ops:
  29.3 12.2 %collective-permute-done.2.refs_2_ = bf16[9,8,3264]{2,1,0:T(8,128)(2,1)} collective-permute-done((bf16[9,8,3264]{2,1,0:T(8,128)(2,1)}, bf16[9,8,3264]{2,1,0:T(8,128)(2,1)}, u32[]{:S(2)}, u32[]{:S(2)}) %collective-permute-start.2) | collective-permute-done | bytes 470048 | tf_op jit(solution)/shard_map/ppermute | solution.py:437
  45.2 9.6 %collective-permute-done.3.refs_3_ = bf16[9,8,3264]{2,1,0:T(8,128)(2,1)} collective-permute-done((bf16[9,8,3264]{2,1,0:T(8,128)(2,1)}, bf16[9,8,3264]{2,1,0:T(8,128)(2,1)}, u32[]{:S(2)}, u32[]{:S(2)}) %collective-permute-start.3) | collective-permute-done | bytes 470048 | tf_op jit(solution)/shard_map/ppermute | solution.py:437
  59.2 12.9 %collective-permute-done.6.refs_6_ = bf16[9,8,3264]{2,1,0:T(8,128)(2,1)} collective-permute-done((bf16[9,8,3264]{2,1,0:T(8,128)(2,1)}, bf16[9,8,3264]{2,1,0:T(8,128)(2,1)}, u32[]{:S(2)}, u32[]{:S(2)}) %collective-permute-start.6) | collective-permute-done | bytes 470048 | tf_op jit(solution)/shard_map/ppermute | solution.py:448
  94.3 12.3 %add_convert_fusion.refs_0_.refs_1_.refs_2_ = bf16[3264,1024]{1,0:T(8,128)(2,1)S(1)} fusion(bf16[136,8,3264]{2,1,0:T(8,128)(2,1)} %get-tuple-element.72, f32[3264]{0:T(1024)S(1)} %reduce.10, f32[1088]{0:T(1024)S(1)} %get-tuple-element.148, f32[1088]{0:T(1024)S(1)} %get-tuple-element.149, f32[1024]{0:T(1024)S(1)} %add_rsqrt_fusion.1, ...), kind=kOutput, calls=%fused_computation.14 | convolution fusion | flops 7289634816 | bytes 16045312 | tf_op jit(solution)/shard_map/dot_general | solution.py:29
  118.6 19.3 %attend.2 = (bf16[1088,1024]{1,0:T(8,128)(2,1)}, f32[17,1,1024]{2,1,0:T(1,128)}) custom-call(s32[8]{0:T(128)} %concatenate.68.info_ref, bf16[3264,1024]{1,0:T(8,128)(2,1)} %copy-done.2, bf16[3264,1024]{1,0:T(8,128)(2,1)} %copy-done.2, bf16[3264,1024]{1,0:T(8,128)(2,1)} %copy-done.2, bf16[2176,1024]{1,0:T(8,128)(2,1)} %collective-permute-done.16.refs_3_.refs_4_, ...), custom_call_target="tpu_custom_call" | custom-call | flops 1000000 | bytes 100000 | tf_op jit(solution)/shard_map/attend/pallas_call | solution.py:234
  143.2 43.0 %attend.3 = (bf16[1088,1024]{1,0:T(8,128)(2,1)}, f32[17,1,1024]{2,1,0:T(1,128)}) custom-call(s32[8]{0:T(128)} %concatenate.68.info_ref, bf16[3264,1024]{1,0:T(8,128)(2,1)} %copy-done.2, bf16[3264,1024]{1,0:T(8,128)(2,1)} %copy-done.2, bf16[3264,1024]{1,0:T(8,128)(2,1)} %copy-done.2, ...), custom_call_target="tpu_custom_call", output_to_operand_aliasing={{0}: (7, {}), {1}: (8, {})} | custom-call | flops 1000000 | bytes 100000 | tf_op jit(solution)/shard_map/attend/pallas_call | solution.py:234
  186.3 10.1 %collective-permute-done.17.refs_2_ = bf16[8,9,8,2176]{3,2,1,0:T(8,128)(2,1)} collective-permute-done((bf16[8,9,8,2176]{3,2,1,0:T(8,128)(2,1)S(1)}, bf16[8,9,8,2176]{3,2,1,0:T(8,128)(2,1)}, u32[]{:S(2)}, u32[]{:S(2)}) %collective-permute-start.17) | collective-permute-done | bytes 2506784 | tf_op jit(solution)/shard_map/ppermute | solution.py:681
  213.8 8.7 %assemble.6 = (bf16[136,8,4352]{2,1,0:T(8,128)(2,1)}, bf16[8,8,4352]{2,1,0:T(8,128)(2,1)}) custom-call(s32[4]{0:T(128)} %pad_add_fusion.1.info_ref, bf16[8,9,8,2176]{3,2,1,0:T(8,128)(2,1)} %copy-done.15, bf16[8,9,8,2176]{3,2,1,0:T(8,128)(2,1)} %collective-permute-done.21.refs_1_, bf16[8,9,8,2176]{3,2,1,0:T(8,128)(2,1)} %collective-permute-done.17.refs_2_, ...), custom_call_target="tpu_custom_call" | custom-call | bytes 100000 | tf_op jit(solution)/shard_map/assemble/pallas_call | solution.py:394
  222.5 29.5 %fusion.6 = (bf16[4352,1024]{1,0:T(8,128)(2,1)}, bf16[4352,1024]{1,0:T(8,128)(2,1)}) fusion(f32[4352]{0:T(1024)S(1)} %add.467, f32[1088,1024]{1,0:T(8,128)S(1)} %get-tuple-element.199, f32[1088]{0:T(1024)S(1)} %copy-done.48, f32[1088]{0:T(1024)S(1)} %get-tuple-element.146, f32[1024]{0:T(1024)S(1)} %add_rsqrt_fusion, f32[1024]{0:T(1024)S(1)} %broadcast_multiply_fusion.4, ...), kind=kOutput, calls=%fused_computation.10 | convolution fusion | flops 9796386816 | bytes 31786496 | tf_op jit(solution)/shard_map/dot_general | solution.py:29
  252.1 15.0 %convolution_convert_fusion.1 = bf16[4352,1088]{1,0:T(8,128)(2,1)S(1)} fusion(bf16[4352,1024]{1,0:T(8,128)(2,1)} %get-tuple-element.86, bf16[1088,512]{1,0:T(8,128)(2,1)} %collective-permute-done.23, bf16[1088,512]{1,0:T(8,128)(2,1)S(1)} %copy-done.13), kind=kOutput, calls=%fused_computation.3 | convolution fusion | flops 9706422272 | bytes 20611072 | tf_op jit(solution)/shard_map/dot_general | solution.py:37
  272.3 9.1 %collective-permute-done.20.refs_2_ = bf16[8,17,8,1088]{3,2,1,0:T(8,128)(2,1)} collective-permute-done((bf16[8,17,8,1088]{3,2,1,0:T(8,128)(2,1)}, bf16[8,17,8,1088]{3,2,1,0:T(8,128)(2,1)}, u32[]{:S(2)}, u32[]{:S(2)}) %collective-permute-start.20) | collective-permute-done | bytes 2367520 | tf_op jit(solution)/shard_map/ppermute | solution.py:687
  286.6 8.6 %assemble.7 = (bf16[544,8,1088]{2,1,0:T(8,128)(2,1)}, bf16[8,8,1088]{2,1,0:T(8,128)(2,1)}) custom-call(s32[4]{0:T(128)} %pad_add_fusion.1.info_ref, bf16[8,17,8,1088]{3,2,1,0:T(8,128)(2,1)} %bitcast.304, bf16[8,17,8,1088]{3,2,1,0:T(8,128)(2,1)} %collective-permute-done.19.refs_1_, bf16[8,17,8,1088]{3,2,1,0:T(8,128)(2,1)} %collective-permute-done.20.refs_2_, ...), custom_call_target="tpu_custom_call" | custom-call | bytes 100000 | tf_op jit(solution)/shard_map/assemble/pallas_call | solution.py:394
  295.3 16.6 %fusion.40 = bf16[1088,1024]{1,0:T(8,128)(2,1)} fusion(f32[1088,1024]{1,0:T(8,128)S(1)} %bitcast.285, bf16[4352,1024]{1,0:T(8,128)(2,1)} %get-tuple-element.86, bf16[544,8,1088]{2,1,0:T(8,128)(2,1)} %get-tuple-element.88, f32[1088]{0:T(1024)S(1)} %copy-done.49), kind=kOutput, calls=%fused_computation.70 | convolution fusion | flops 9700573184 | bytes 25071872 | tf_op jit(solution)/shard_map/dot_general | solution.py:29
  321.8 18.7 %fusion.117 = (bf16[4352]{0:T(1024)(128)(2,1)S(1)}, bf16[4352,1024]{1,0:T(8,128)(2,1)}) fusion(bf16[4352,1024]{1,0:T(8,128)(2,1)} %get-tuple-element.91, bf16[1088,1024]{1,0:T(8,128)(2,1)S(1)} %copy-done.24, bf16[544,8,1088]{2,1,0:T(8,128)(2,1)} %get-tuple-element.88), kind=kOutput, calls=%fused_computation.268 | convolution fusion | flops 9715052544 | bytes 29532672 | tf_op jit(solution)/shard_map/dot_general | solution.py:33
  340.5 17.0 %convolution_convert_fusion = bf16[1088,4352]{1,0:T(8,128)(2,1)} fusion(bf16[4352,1024]{1,0:T(8,128)(2,1)} %get-tuple-element.93, f32[1088,1024]{1,0:T(8,128)} %copy-done.4, f32[1088]{0:T(1024)S(1)} %copy-done.48, f32[1088]{0:T(1024)S(1)} %get-tuple-element.146, f32[1024]{0:T(1024)S(1)} %add_rsqrt_fusion, f32[1024]{0:T(1024)S(1)} %broadcast_multiply_fusion.4), kind=kOutput, calls=%fused_computation.2 | convolution fusion | flops 9707536384 | bytes 22856192 | tf_op jit(solution)/shard_map/dot_general | solution.py:37
  362.6 15.2 %collective-permute-done.27 = bf16[8,17,8,1088]{3,2,1,0:T(8,128)(2,1)} collective-permute-done((bf16[8,17,8,1088]{3,2,1,0:T(8,128)(2,1)}, bf16[8,17,8,1088]{3,2,1,0:T(8,128)(2,1)}, u32[]{:S(2)}, u32[]{:S(2)}) %collective-permute-start.27) | collective-permute-done | bytes 2367520 | tf_op jit(solution)/shard_map/ppermute | solution.py:536
  382.4 18.5 %multiply_reduce_fusion = (bf16[1088]{0:T(1024)(128)(2,1)S(1)}, f32[1024]{0:T(1024)S(1)}, f32[1024]{0:T(1024)S(1)}, bf16[1088]{0:T(1024)(128)(2,1)S(1)}, f32[1088,1024]{1,0:T(8,128)S(1)}) fusion(f32[1088,1024]{1,0:T(8,128)} %copy-done.4, f32[1024]{0:T(1024)S(1)} %add_rsqrt_fusion, f32[1024]{0:T(1024)S(1)} %broadcast_multiply_fusion.4, ...), kind=kOutput, calls=%fused_computation.60 | convolution fusion | flops 9707253760 | bytes 27320832 | tf_op jit(solution)/shard_map/dot_general | solution.py:33
  432.7 42.9 %attend_back.3 = (bf16[3,17,64,1024]{3,2,1,0:T(8,128)(2,1)}, bf16[2,8,64,1024]{3,2,1,0:T(8,128)(2,1)}) custom-call(s32[8]{0:T(128)} %concatenate.68.info_ref, bf16[3264,1024]{1,0:T(8,128)(2,1)} %copy-done.2, bf16[3264,1024]{1,0:T(8,128)(2,1)} %copy-done.2, bf16[3264,1024]{1,0:T(8,128)(2,1)} %copy-done.2, ...), custom_call_target="tpu_custom_call" | custom-call | flops 1000000 | bytes 100000 | tf_op jit(solution)/shard_map/attend_back/pallas_call | solution.py:280
  485.8 27.7 %attend_back.4 = (bf16[3,17,64,1024]{3,2,1,0:T(8,128)(2,1)}, bf16[2,5,64,1024]{3,2,1,0:T(8,128)(2,1)}) custom-call(s32[8]{0:T(128)} %concatenate.68.info_ref, bf16[3264,1024]{1,0:T(8,128)(2,1)} %copy-done.2, bf16[3264,1024]{1,0:T(8,128)(2,1)} %copy-done.2, bf16[3264,1024]{1,0:T(8,128)(2,1)} %copy-done.2, ...), custom_call_target="tpu_custom_call", output_to_operand_aliasing={{0}: (10, {})} | custom-call | flops 1000000 | bytes 100000 | tf_op jit(solution)/shard_map/attend_back/pallas_call | solution.py:280
  517.1 22.7 %attend_back.5 = (bf16[3,17,64,1024]{3,2,1,0:T(8,128)(2,1)}, bf16[2,4,64,1024]{3,2,1,0:T(8,128)(2,1)}) custom-call(s32[8]{0:T(128)} %concatenate.68.info_ref, bf16[3264,1024]{1,0:T(8,128)(2,1)} %copy-done.2, bf16[3264,1024]{1,0:T(8,128)(2,1)} %copy-done.2, bf16[3264,1024]{1,0:T(8,128)(2,1)} %copy-done.2, ...), custom_call_target="tpu_custom_call", output_to_operand_aliasing={{0}: (10, {})} | custom-call | flops 1000000 | bytes 100000 | tf_op jit(solution)/shard_map/attend_back/pallas_call | solution.py:280
  575.4 14.4 %fusion.37 = (bf16[1088]{0:T(1024)(128)(2,1)S(1)}, f32[1024]{0:T(1024)S(1)}, f32[1024]{0:T(1024)S(1)}, bf16[1088]{0:T(1024)(128)(2,1)S(1)}, f32[1088,1024]{1,0:T(8,128)}) fusion(f32[1024]{0:T(1024)S(1)} %copy-done.44, f32[1024]{0:T(1024)S(1)} %copy-done.40, bf16[1088,512]{1,0:T(8,128)(2,1)S(1)} %copy-done.17, bf16[1088,512]{1,0:T(8,128)(2,1)S(1)} %copy-done.11, ...), kind=kOutput, calls=%fused_computation.56 | convolution fusion | flops 7287402496 | bytes 20496896 | tf_op jit(solution)/shard_map/dot_general | solution.py:33
  603.8 21.0 %collective-permute-done.41 = bf16[4,9,8,1632]{3,2,1,0:T(8,128)(2,1)} collective-permute-done((bf16[4,9,8,1632]{3,2,1,0:T(8,128)(2,1)}, bf16[4,9,8,1632]{3,2,1,0:T(8,128)(2,1)}, u32[]{:S(2)}, u32[]{:S(2)}) %collective-permute-start.41) | collective-permute-done | bytes 940064 | tf_op jit(solution)/shard_map/ppermute | solution.py:531
  662.0 13.0 %collective-permute-start.44 = (bf16[9,8,1632]{2,1,0:T(8,128)(2,1)S(1)}, bf16[9,8,1632]{2,1,0:T(8,128)(2,1)S(1)}, u32[]{:S(2)}, u32[]{:S(2)}) collective-permute-start(bf16[9,8,1632]{2,1,0:T(8,128)(2,1)S(1)} %copy-done.36), channel_id=1, source_target_pairs={{0,16},{4,20},{8,24},{12,28},{16,0},{20,4},{24,8},{28,12},{1,17},{... | collective-permute-start | bytes 705032 | tf_op jit(solution)/shard_map/ppermute | solution.py:542
  675.0 8.6 %collective-permute-start.45 = (bf16[9,8,1632]{2,1,0:T(8,128)(2,1)S(1)}, bf16[9,8,1632]{2,1,0:T(8,128)(2,1)S(1)}, u32[]{:S(2)}, u32[]{:S(2)}) collective-permute-start(bf16[9,8,1632]{2,1,0:T(8,128)(2,1)S(1)} %get-tuple-element.166), channel_id=1, source_target_pairs={{0,24},{4,28},{8,0},{12,4},{16,8},{20,12},{24,16},{28,20},{1,25},{... | collective-permute-start | bytes 705032 | tf_op jit(solution)/shard_map/ppermute | solution.py:542
  (393 shorter events, 268.4 us)
Async XLA Ops:
  7.2 130.7 %all-gather.3.cloned.1.call-start = ((), (), s32[]{:S(2)}) async-start(), calls=%async_computation.2 | async-start | bytes 4313088 | tf_op jit(solution)/shard_map/all_gather | solution.py:443
  42.4 154.0 %all-gather.5.cloned.1.call-start = ((), (), s32[]{:S(2)}) async-start(), calls=%async_computation.3 | async-start | bytes 2820096 | tf_op jit(solution)/shard_map/all_gather | solution.py:443
  111.8 401.9 %reduce-scatter.7.cloned.1.call-start = ((), (), s32[]{:S(2)}) async-start(), calls=%async_computation.4 | async-start | bytes 2820096
  139.8 56.6 %collective-permute-start.17 = (bf16[8,9,8,2176]{3,2,1,0:T(8,128)(2,1)S(1)}, bf16[8,9,8,2176]{3,2,1,0:T(8,128)(2,1)}, u32[]{:S(2)}, u32[]{:S(2)}) collective-permute-start(bf16[8,9,8,2176]{3,2,1,0:T(8,128)(2,1)S(1)} %slice.161.refs_0_), channel_id=1, source_target_pairs={{0,2},{1,3},{2,0},{3,1},{4,6},{5,7},{6,4},{7,5},{8,10},{9,11},{10,... | collective-permute-start | bytes 7520264 | tf_op jit(solution)/shard_map/ppermute | solution.py:681
  200.6 51.5 %collective-permute-start.23 = (bf16[1088,512]{1,0:T(8,128)(2,1)}, bf16[1088,512]{1,0:T(8,128)(2,1)}, u32[]{:S(2)}, u32[]{:S(2)}) collective-permute-start(bf16[1088,512]{1,0:T(8,128)(2,1)} %get-tuple-element.161), channel_id=1, source_target_pairs={{0,3},{1,2},{2,1},{3,0},{4,7},{5,6},{6,5},{7,4},{8,11},{9,10},{10,... | collective-permute-start | bytes 3342344 | tf_op jit(solution)/shard_map/ppermute | solution.py:640
  201.9 79.5 %collective-permute-start.20 = (bf16[8,17,8,1088]{3,2,1,0:T(8,128)(2,1)}, bf16[8,17,8,1088]{3,2,1,0:T(8,128)(2,1)}, u32[]{:S(2)}, u32[]{:S(2)}) collective-permute-start(bf16[8,17,8,1088]{3,2,1,0:T(8,128)(2,1)} %bitcast.302), channel_id=1, source_target_pairs={{0,2},{1,3},{2,0},{3,1},{4,6},{5,7},{6,4},{7,5},{8,10},{9,11},{10,... | collective-permute-start | bytes 7102472 | tf_op jit(solution)/shard_map/ppermute | solution.py:687
  203.8 81.3 %collective-permute-start.19 = (bf16[8,17,8,1088]{3,2,1,0:T(8,128)(2,1)}, bf16[8,17,8,1088]{3,2,1,0:T(8,128)(2,1)}, u32[]{:S(2)}, u32[]{:S(2)}) collective-permute-start(bf16[8,17,8,1088]{3,2,1,0:T(8,128)(2,1)} %bitcast.303), channel_id=1, source_target_pairs={{0,1},{1,0},{2,3},{3,2},{4,5},{5,4},{6,7},{7,6},{8,9},{9,8},{10,11... | collective-permute-start | bytes 7102472 | tf_op jit(solution)/shard_map/ppermute | solution.py:452
  281.5 30.3 %collective-permute-start.25 = (bf16[8,2,17,8,1088]{4,3,2,1,0:T(8,128)(2,1)}, bf16[8,2,17,8,1088]{4,3,2,1,0:T(8,128)(2,1)}, u32[]{:S(2)}, u32[]{:S(2)}) collective-permute-start(bf16[8,2,17,8,1088]{4,3,2,1,0:T(8,128)(2,1)} %constant_dynamic-slice_fusion.4), channel_id=1, source_target_pairs={{0,1},{1,0},{2,3},{3,2},{4,5},{5,4},{6,7},{7,6},{8,9},{9,8},{10,11... | collective-permute-start | bytes 14204936 | tf_op jit(solution)/shard_map/ppermute | solution.py:519
  321.0 56.8 %collective-permute-start.27 = (bf16[8,17,8,1088]{3,2,1,0:T(8,128)(2,1)}, bf16[8,17,8,1088]{3,2,1,0:T(8,128)(2,1)}, u32[]{:S(2)}, u32[]{:S(2)}) collective-permute-start(bf16[8,17,8,1088]{3,2,1,0:T(8,128)(2,1)} %fusion.46), channel_id=1, source_target_pairs={{0,2},{1,3},{2,0},{3,1},{4,6},{5,7},{6,4},{7,5},{8,10},{9,11},{10,... | collective-permute-start | bytes 7102472 | tf_op jit(solution)/shard_map/ppermute | solution.py:536
  362.4 44.4 %collective-permute-start.26 = (bf16[8,9,8,4352]{3,2,1,0:T(8,128)(2,1)}, bf16[8,9,8,4352]{3,2,1,0:T(8,128)(2,1)}, u32[]{:S(2)}, u32[]{:S(2)}) collective-permute-start(bf16[8,9,8,4352]{3,2,1,0:T(8,128)(2,1)} %constant_dynamic-slice_fusion.3), channel_id=1, source_target_pairs={{0,1},{1,0},{2,3},{3,2},{4,5},{5,4},{6,7},{7,6},{8,9},{9,8},{10,11... | collective-permute-start | bytes 15040520 | tf_op jit(solution)/shard_map/ppermute | solution.py:519
  382.3 267.9 %reduce-scatter.9.cloned.1.call-start = ((), (), s32[]{:S(2)}) async-start(), calls=%async_computation.5 | async-start | bytes 2820096
  414.5 61.1 %collective-permute-start.28 = (bf16[8,9,8,2176]{3,2,1,0:T(8,128)(2,1)}, bf16[8,9,8,2176]{3,2,1,0:T(8,128)(2,1)}, u32[]{:S(2)}, u32[]{:S(2)}) collective-permute-start(bf16[8,9,8,2176]{3,2,1,0:T(8,128)(2,1)} %dynamic-slice_convert_fusion), channel_id=1, source_target_pairs={{0,2},{1,3},{2,0},{3,1},{4,6},{5,7},{6,4},{7,5},{8,10},{9,11},{10,... | collective-permute-start | bytes 7520264 | tf_op jit(solution)/shard_map/ppermute | solution.py:536
  431.7 49.1 %collective-permute-start.31 = (bf16[4,9,8,1088]{3,2,1,0:T(8,128)(2,1)}, bf16[4,9,8,1088]{3,2,1,0:T(8,128)(2,1)S(1)}, u32[]{:S(2)}, u32[]{:S(2)}) collective-permute-start(bf16[4,9,8,1088]{3,2,1,0:T(8,128)(2,1)} %get-tuple-element.179), channel_id=1, source_target_pairs={{0,4},{4,0},{8,12},{12,8},{16,20},{20,16},{24,28},{28,24},{1,5},{5... | collective-permute-start | bytes 1880072 | tf_op jit(solution)/shard_map/ppermute | solution.py:531
  480.8 33.0 %collective-permute-start.30 = (bf16[1088,512]{1,0:T(8,128)(2,1)}, bf16[1088,512]{1,0:T(8,128)(2,1)}, u32[]{:S(2)}, u32[]{:S(2)}) collective-permute-start(bf16[1088,512]{1,0:T(8,128)(2,1)} %slice.168), channel_id=1, source_target_pairs={{0,3},{1,2},{2,1},{3,0},{4,7},{5,6},{6,5},{7,4},{8,11},{9,10},{10,... | collective-permute-start | bytes 3342344 | tf_op jit(solution)/shard_map/ppermute | solution.py:643
  481.6 31.9 %collective-permute-start.32 = (bf16[9,8,1088]{2,1,0:T(8,128)(2,1)}, bf16[9,8,1088]{2,1,0:T(8,128)(2,1)S(1)}, u32[]{:S(2)}, u32[]{:S(2)}) collective-permute-start(bf16[9,8,1088]{2,1,0:T(8,128)(2,1)} %get-tuple-element.177), channel_id=1, source_target_pairs={{0,8},{4,12},{8,16},{12,20},{16,24},{20,28},{24,0},{28,4},{1,9},{5... | collective-permute-start | bytes 470024 | tf_op jit(solution)/shard_map/ppermute | solution.py:542
  481.6 32.0 %collective-permute-start.33 = (bf16[9,8,1088]{2,1,0:T(8,128)(2,1)S(1)}, bf16[9,8,1088]{2,1,0:T(8,128)(2,1)S(1)}, u32[]{:S(2)}, u32[]{:S(2)}) collective-permute-start(bf16[9,8,1088]{2,1,0:T(8,128)(2,1)S(1)} %get-tuple-element.176), channel_id=1, source_target_pairs={{0,16},{4,20},{8,24},{12,28},{16,0},{20,4},{24,8},{28,12},{1,17},{... | collective-permute-start | bytes 470024 | tf_op jit(solution)/shard_map/ppermute | solution.py:542
  485.8 58.3 %collective-permute-start.35 = (bf16[2,8,64,1024]{3,2,1,0:T(8,128)(2,1)}, bf16[2,8,64,1024]{3,2,1,0:T(8,128)(2,1)}, u32[]{:S(2)}, u32[]{:S(2)}) collective-permute-start(bf16[2,8,64,1024]{3,2,1,0:T(8,128)(2,1)} %get-tuple-element.98), channel_id=1, source_target_pairs={{0,1},{1,0},{2,3},{3,2},{4,5},{5,4},{6,7},{7,6},{8,9},{9,8},{10,11... | collective-permute-start | bytes 6291464 | tf_op jit(solution)/shard_map/ppermute | solution.py:735
  513.5 30.6 %collective-permute-start.36 = (bf16[2,5,64,1024]{3,2,1,0:T(8,128)(2,1)}, bf16[2,5,64,1024]{3,2,1,0:T(8,128)(2,1)}, u32[]{:S(2)}, u32[]{:S(2)}) collective-permute-start(bf16[2,5,64,1024]{3,2,1,0:T(8,128)(2,1)} %get-tuple-element.104), channel_id=1, source_target_pairs={{0,1},{1,0},{2,3},{3,2},{4,5},{5,4},{6,7},{7,6},{8,9},{9,8},{10,11... | collective-permute-start | bytes 3932168 | tf_op jit(solution)/shard_map/ppermute | solution.py:742
  567.5 69.6 %collective-permute-start.58 = (bf16[2,136,1088]{2,1,0:T(8,128)(2,1)}, bf16[2,136,1088]{2,1,0:T(8,128)(2,1)}, u32[]{:S(2)}, u32[]{:S(2)}) collective-permute-start(bf16[2,136,1088]{2,1,0:T(8,128)(2,1)} %pad_maximum_fusion.4), channel_id=1, source_target_pairs={{0,1},{1,0},{2,3},{3,2},{4,5},{5,4},{6,7},{7,6},{8,9},{9,8},{10,11... | collective-permute-start | bytes 1775624 | tf_op jit(solution)/shard_map/ppermute | solution.py:567
  570.4 31.1 %collective-permute-start.42 = (bf16[4,9,8,1632]{3,2,1,0:T(8,128)(2,1)}, bf16[4,9,8,1632]{3,2,1,0:T(8,128)(2,1)}, u32[]{:S(2)}, u32[]{:S(2)}) collective-permute-start(bf16[4,9,8,1632]{3,2,1,0:T(8,128)(2,1)} %get-tuple-element.174), channel_id=1, source_target_pairs={{0,4},{4,0},{8,12},{12,8},{16,20},{20,16},{24,28},{28,24},{1,5},{5... | collective-permute-start | bytes 2820104 | tf_op jit(solution)/shard_map/ppermute | solution.py:531
  573.9 50.9 %collective-permute-start.41 = (bf16[4,9,8,1632]{3,2,1,0:T(8,128)(2,1)}, bf16[4,9,8,1632]{3,2,1,0:T(8,128)(2,1)}, u32[]{:S(2)}, u32[]{:S(2)}) collective-permute-start(bf16[4,9,8,1632]{3,2,1,0:T(8,128)(2,1)} %get-tuple-element.169), channel_id=1, source_target_pairs={{0,4},{4,0},{8,12},{12,8},{16,20},{20,16},{24,28},{28,24},{1,5},{5... | collective-permute-start | bytes 2820104 | tf_op jit(solution)/shard_map/ppermute | solution.py:531
  645.0 46.7 %collective-permute-start.40 = (bf16[1088,512]{1,0:T(8,128)(2,1)S(1)}, bf16[1088,512]{1,0:T(8,128)(2,1)S(1)}, u32[]{:S(2)}, u32[]{:S(2)}) collective-permute-start(bf16[1088,512]{1,0:T(8,128)(2,1)S(1)} %slice.264), channel_id=1, source_target_pairs={{0,3},{1,2},{2,1},{3,0},{4,7},{5,6},{6,5},{7,4},{8,11},{9,10},{10,... | collective-permute-start | bytes 3342344 | tf_op jit(solution)/shard_map/ppermute | solution.py:643
  645.9 40.2 %collective-permute-start.43 = (bf16[9,8,1632]{2,1,0:T(8,128)(2,1)}, bf16[9,8,1632]{2,1,0:T(8,128)(2,1)S(1)}, u32[]{:S(2)}, u32[]{:S(2)}) collective-permute-start(bf16[9,8,1632]{2,1,0:T(8,128)(2,1)} %get-tuple-element.165), channel_id=1, source_target_pairs={{0,8},{4,12},{8,16},{12,20},{16,24},{20,28},{24,0},{28,4},{1,9},{5... | collective-permute-start | bytes 705032 | tf_op jit(solution)/shard_map/ppermute | solution.py:542
  650.3 33.3 %collective-permute-start.48 = (bf16[9,8,1632]{2,1,0:T(8,128)(2,1)S(1)}, bf16[9,8,1632]{2,1,0:T(8,128)(2,1)}, u32[]{:S(2)}, u32[]{:S(2)}) collective-permute-start(bf16[9,8,1632]{2,1,0:T(8,128)(2,1)S(1)} %copy-done.37), channel_id=1, source_target_pairs={{0,24},{4,28},{8,0},{12,4},{16,8},{20,12},{24,16},{28,20},{1,25},{... | collective-permute-start | bytes 705032 | tf_op jit(solution)/shard_map/ppermute | solution.py:542
  (102 other events, 1526.0 us)
Sparse Core Ops, SparseCore 0:
  42.5 73.1 all-gather.2
  118.4 52.0 all-gather.4
  382.5 72.8 reduce-scatter.6
  544.2 77.3 reduce-scatter.8
